TPU v7x, 32 devices: a whole 2x2x4 slice. The times are simulated.
32 devices in a mesh: rep: 2 (over y), lat: 4 (over z), ch: 2 (over x), sub: 2 (over core).
Axes of the slice: x: 2, y: 2, z: 4, core: 2. Of those that a mesh axis runs over, the one named last changes fastest.
Arguments:
- field: float32 [224, 128, 1440], P(('rep', 'lat'), 'ch'), parts along dimension 0, may hold values from -6 to 6
- legendre: bfloat16 [192, 112, 384], P('sub', 'lat'), as said below
- ownership: int32 [192], replicated, may hold values from 0 to 191, as said below
- w_real: bfloat16 [128, 128], P('ch'), may hold values from -0.375 to 0.375
- w_imag: bfloat16 [128, 128], P('ch'), may hold values from -0.375 to 0.375
Outputs:
- mixed: bfloat16 [4, 192, 128, 384], P('rep', ('lat', 'sub'), 'ch'), parts along dimension 0
There are 2 independent parts, one for each index of `rep`. A program takes and returns all parts, laid end to end along the dimension named above; an argument that names none is the same for every part. Nothing has to cross between parts.
Inputs may be any that keep to these rules, and one draw needn't show every extreme that they name: `ownership`: A permutation of 0 to 191. With S the number of devices of sub, the positions p with (p // 24) % S = s hold the wavenumbers s * 192 / S to (s + 1) * 192 / S - 1, and entries 2i and 2i + 1 are some m of that range and the wavenumber as far from the range's other end. `legendre`: zero wherever the degree l is below the wavenumber m.
All inputs are finite; a program needn't handle non-finite values.
Results may differ from a plain program's by a relative error of at most 0.014.
Values may be sent and summed in bfloat16 or wider, within the bound.
No kernel may reach another device: no remote copies, remote signals or barrier semaphores. Data moves between devices by JAX's collectives and lax.ppermute only.
A program may use at most 128 MiB of HBM per device.

v0:
```python
import math

import jax
import jax.numpy as jnp
from jax import lax
from jax.sharding import PartitionSpec as P


def fourier_rows(flat_field, modes, lat_rows, chans, nlon):
    longitude = jnp.arange(nlon, dtype=jnp.int32)
    phase = longitude[:, None] * modes[None, :] % nlon
    angle = phase.astype(jnp.float32) * (2.0 * math.pi / nlon)
    scale = 1.0 / math.sqrt(nlon)
    real_part = (
        jnp.dot(
            flat_field,
            jnp.cos(angle),
            precision=lax.Precision.HIGHEST,
            preferred_element_type=jnp.float32,
        )
        * scale
    )
    imag_part = (
        -jnp.dot(
            flat_field,
            jnp.sin(angle),
            precision=lax.Precision.HIGHEST,
            preferred_element_type=jnp.float32,
        )
        * scale
    )
    both = jnp.stack([real_part, imag_part]).reshape(2, lat_rows, chans, modes.shape[0])
    both = jnp.transpose(both, (3, 1, 0, 2)).reshape(modes.shape[0], lat_rows, 2 * chans)
    return both.astype(jnp.bfloat16)


def per_device(field, legendre, ownership, w_real, w_imag):
    lat_rows, chans, nlon = field.shape
    degrees = legendre.shape[2]
    slab_modes = legendre.shape[0]
    blocks = lax.axis_size("lat")
    halves = lax.axis_size("sub")
    per_block = ownership.shape[0] // (blocks * halves)
    my_modes = lax.dynamic_index_in_dim(
        ownership.reshape(blocks, halves, per_block), lax.axis_index("sub"), 1, keepdims=False
    ).reshape(blocks * per_block)
    slab_index = my_modes - lax.axis_index("sub") * slab_modes
    flat_field = field.reshape(lat_rows * chans, nlon)
    spectra_rows = fourier_rows(flat_field, my_modes, lat_rows, chans, nlon)
    table_rows = jnp.take(legendre, slab_index, axis=0)
    spectra_all, tables_all = (
        lax.all_to_all(spectra_rows, "lat", split_axis=0, concat_axis=1, tiled=True),
        lax.all_to_all(table_rows, "lat", split_axis=0, concat_axis=1, tiled=True),
    )
    spectra_all = spectra_all.reshape(per_block, blocks, lat_rows, 2 * chans)
    tables_all = tables_all.reshape(per_block, blocks, lat_rows, degrees)
    block_part = jnp.einsum(
        "kbtc,kbtl->kbcl", spectra_all, tables_all, preferred_element_type=jnp.float32
    )
    block_part = lax.optimization_barrier(block_part.astype(jnp.bfloat16)).astype(jnp.float32)
    total = jnp.sum(block_part, axis=1)
    coeff = total.astype(jnp.bfloat16).reshape(per_block, 2, chans, degrees)
    piece = lax.all_gather(coeff, "ch", axis=2, tiled=True)
    real_in = piece[:, 0]
    imag_in = piece[:, 1]
    real_out = jnp.einsum(
        "oc,kcl->kol", w_real, real_in, preferred_element_type=jnp.float32
    ) - jnp.einsum("oc,kcl->kol", w_imag, imag_in, preferred_element_type=jnp.float32)
    imag_out = jnp.einsum(
        "oc,kcl->kol", w_real, imag_in, preferred_element_type=jnp.float32
    ) + jnp.einsum("oc,kcl->kol", w_imag, real_in, preferred_element_type=jnp.float32)
    mixed = jnp.stack([real_out, imag_out])
    return mixed.astype(jnp.bfloat16)


def solution(mesh):
    in_specs = (
        P(("rep", "lat"), "ch", None),
        P("sub", "lat", None),
        P(),
        P("ch", None),
        P("ch", None),
    )
    out_specs = P("rep", ("lat", "sub"), "ch", None)
    return jax.shard_map(
        per_device, mesh=mesh, in_specs=in_specs, out_specs=out_specs, check_vma=False
    )
```

profile of v0, /device:TPU:0, one launch (start us, length us, event | category | flops | bytes accessed | tf_op | source)
XLA Modules:
  0.0 213.7 jit_solution(16990924426114101295)
XLA Ops:
  6.5 0.0 copy-start
  6.5 0.9 reshape.53
  7.5 0.1 mul.37
  7.6 0.0 copy-start.1
  7.6 15.8 %fusion.6 = bf16[1792,96]{0,1:T(8,128)(2,1)S(1)} fusion(f32[1792,1440]{1,0:T(8,128)} %bitcast.57, s32[96]{0:T(128)S(1)} %mul.37), kind=kOutput, calls=%fused_computation.15 | convolution fusion | flops 2974473216 | bytes 10666368 | tf_op jit(solution)/shard_map/dot_general | solution.py:24
  23.4 0.0 copy-done.1
  23.4 13.2 %fusion.5 = bf16[1792,96]{0,1:T(8,128)(2,1)S(1)} fusion(f32[1792,1440]{1,0:T(8,128)S(1)} %bitcast.58, s32[96]{0:T(128)S(1)} %mul.37), kind=kOutput, calls=%fused_computation.14 | convolution fusion | flops 2974301184 | bytes 10666368 | tf_op jit(solution)/shard_map/dot_general | solution.py:15
  36.6 0.5 copy.14
  37.1 0.3 copy.13
  37.4 0.2 maximum_bitcast_fusion
  37.6 0.1 copy.15
  37.6 1.6 copy.16
  39.3 6.3 %all-to-all-start = ((bf16[96,28,128]{2,1,0:T(8,128)(2,1)}), bf16[96,28,128]{2,1,0:T(8,128)(2,1)S(1)}, u32[]{:S(2)}, u32[]{:S(2)}) async-start(bf16[96,28,128]{2,1,0:T(8,128)(2,1)} %copy.16), calls=%async_computation | async-start | bytes 1572864 | tf_op jit(solution)/shard_map/all_to_all | solution.py:52
  45.6 0.0 all-gather.2.cloned.1.call-start
  45.6 0.1 sub.32
  45.7 0.0 copy-done
  45.7 9.9 %gather_fusion = bf16[96,28,384]{2,0,1:T(8,128)(2,1)} fusion(bf16[96,28,384]{2,0,1:T(8,128)(2,1)S(1)} %copy-done, s32[1024]{0:T(1024)S(1)} %pad_clamp_fusion), kind=kCustom, calls=%fused_computation | custom fusion | bytes 4129152 | tf_op jit(solution)/shard_map/jit(_take)/gather | solution.py:50
  55.6 1.9 broadcast_select_fusion
  57.5 2.2 %copy.19 = bf16[96,28,384]{2,1,0:T(8,128)(2,1)} copy(bf16[96,28,384]{2,0,1:T(8,128)(2,1)S(1)} %broadcast_select_fusion) | data formatting | bytes 4128768 | tf_op jit(solution)/shard_map/jit(_take)/select_n | solution.py:50
  59.7 6.0 %all-to-all-done = bf16[96,28,128]{2,1,0:T(8,128)(2,1)S(1)} async-done(((bf16[96,28,128]{2,1,0:T(8,128)(2,1)}), bf16[96,28,128]{2,1,0:T(8,128)(2,1)S(1)}, u32[]{:S(2)}, u32[]{:S(2)}) %all-to-all-start) | async-done | bytes 688160 | tf_op jit(solution)/shard_map/all_to_all | solution.py:52
  65.7 56.9 %all_to_all.30 = bf16[96,28,384]{2,1,0:T(8,128)(2,1)S(1)} all-to-all(bf16[96,28,384]{2,1,0:T(8,128)(2,1)} %copy.19), channel_id=1, replica_groups=mesh['rep'=2,'lat'=4,'ch'=2,'sub'=2] {'lat'}, dimensions={0} | all-to-all | bytes 4128768 | tf_op jit(solution)/shard_map/all_to_all | solution.py:53
  122.6 5.1 %convolution_convert_fusion = bf16[24,4,128,384]{3,2,1,0:T(8,128)(2,1)} fusion(bf16[4,24,28,384]{3,2,1,0:T(8,128)(2,1)S(1)} %bitcast.59, bf16[4,24,28,128]{3,2,1,0:T(8,128)(2,1)S(1)} %bitcast.62), kind=kOutput, calls=%fused_computation.1 | convolution fusion | flops 268959744 | bytes 12189696 | tf_op jit(solution)/shard_map/kbtc,kbtl->kbcl/dot_general | solution.py:57
  127.8 7.6 %reduce_sum.12 = bf16[24,128,384]{2,1,0:T(8,128)(2,1)} reduce(bf16[24,4,128,384]{3,2,1,0:T(8,128)(2,1)} %convolution_convert_fusion, bf16[]{:T(256)} %constant.43.clone.1), dimensions={1}, to_apply=%region_0.1 | reduce | flops 3538944 | bytes 11796482 | tf_op jit(solution)/shard_map/reduce_sum | solution.py:61
  135.4 3.4 %copy.22 = bf16[24,2,64,384]{3,2,0,1:T(8,128)(2,1)} copy(bf16[24,2,64,384]{3,2,1,0:T(8,128)(2,1)} %bitcast.60) | data formatting | bytes 4718592 | tf_op jit(solution)/shard_map/reshape | solution.py:62
  138.7 0.0 copy-start.4
  138.7 0.0 all-gather.2.cloned.1.call-update
  138.8 0.0 copy-start.3
  138.8 61.9 %all-gather.2.cloned.1.call-done = bf16[24,2,128,384]{3,2,0,1:T(8,128)(2,1)} async-done(((bf16[24,2,64,384]{3,2,0,1:T(8,128)(2,1)}), bf16[24,2,128,384]{3,2,0,1:T(8,128)(2,1)}) %all-gather.2.cloned.1.call-update) | async-done | bytes 4718608 | tf_op jit(solution)/shard_map/all_gather | solution.py:63
  200.7 0.0 copy-done.4
  200.7 0.0 copy-start.2
  200.7 2.3 %fusion.7 = f32[24,384,64]{1,2,0:T(8,128)S(1)} fusion(bf16[24,2,128,384]{3,2,0,1:T(8,128)(2,1)} %all-gather.2.cloned.1.call-done, bf16[64,128]{1,0:T(8,128)(2,1)S(1)} %copy-done.4), kind=kOutput, calls=%fused_computation.16 | convolution fusion | flops 150994944 | bytes 4734976 | tf_op jit(solution)/shard_map/oc,kcl->kol/dot_general | solution.py:66
  203.0 0.0 copy-done.3
  203.0 0.8 copy-done.2
  203.7 0.5 fusion.8
  204.2 0.5 fusion.11
  204.7 0.5 fusion.12
  205.2 1.7 pad_maximum_fusion
  (4 shorter events, 0.0 us)
Async XLA Ops:
  6.5 39.2 %copy-start = (bf16[96,28,384]{2,0,1:T(8,128)(2,1)S(1)}, bf16[96,28,384]{2,0,1:T(8,128)(2,1)}, u32[]{:S(2)}) copy-start(bf16[96,28,384]{2,0,1:T(8,128)(2,1)} %param.6) | copy-start | bytes 6193156
  7.6 15.8 %copy-start.1 = (f32[28,64,1440]{2,1,0:T(8,128)S(1)}, f32[28,64,1440]{2,1,0:T(8,128)}, u32[]{:S(2)}) copy-start(f32[28,64,1440]{2,1,0:T(8,128)} %param.5) | copy-start | bytes 30965764
  39.3 26.4 %all-to-all-start = ((bf16[96,28,128]{2,1,0:T(8,128)(2,1)}), bf16[96,28,128]{2,1,0:T(8,128)(2,1)S(1)}, u32[]{:S(2)}, u32[]{:S(2)}) async-start(bf16[96,28,128]{2,1,0:T(8,128)(2,1)} %copy.16), calls=%async_computation | async-start | bytes 1572864 | tf_op jit(solution)/shard_map/all_to_all | solution.py:52
  45.6 155.1 %all-gather.2.cloned.1.call-start = ((), (), s32[]{:S(2)}) async-start(), calls=%async_computation.2 | async-start | bytes 7077888 | tf_op jit(solution)/shard_map/all_gather | solution.py:63
  138.7 62.0 %copy-start.4 = (bf16[64,128]{1,0:T(8,128)(2,1)S(1)}, bf16[64,128]{1,0:T(8,128)(2,1)}, u32[]{:S(2)}) copy-start(bf16[64,128]{1,0:T(8,128)(2,1)} %param.8) | copy-start | bytes 49156
  138.8 64.2 %copy-start.3 = (bf16[64,128]{1,0:T(8,128)(2,1)S(1)}, bf16[64,128]{1,0:T(8,128)(2,1)}, u32[]{:S(2)}) copy-start(bf16[64,128]{1,0:T(8,128)(2,1)} %param.9) | copy-start | bytes 49156
  200.7 3.0 %copy-start.2 = (bf16[24,2,128,384]{3,2,0,1:T(8,128)(2,1)S(1)}, bf16[24,2,128,384]{3,2,0,1:T(8,128)(2,1)}, u32[]{:S(2)}) copy-start(bf16[24,2,128,384]{3,2,0,1:T(8,128)(2,1)} %all-gather.2.cloned.1.call-done) | copy-start | bytes 14155780
Sparse Core Ops, SparseCore 0:
  138.9 61.7 all-gather.1
where the time goes:
time: 214 us
  waiting for transfers between devices  67.9 us (32%)
  blocking collectives  56.9 us (27%)
  matrix products  37.9 us (18%)
  local copies, waits for them, and re-layouts  19.8 us (9%)
  between operations  13.5 us (6%)
  other arithmetic  11.4 us (5%)
  starting transfers between devices  6.32 us (3%)
    all_gather x1, waiting for transfers between devices, per_device(): piece = lax.all_gather(coeff, 'ch', axis=2, tiled=True)  61.9 us
    all_to_all x1, blocking collectives, per_device(): lax.all_to_all(table_rows, 'lat', split_axis=0, concat_axis=1, tiled=True)  56.9 us
    dot_general x1, matrix products, fourier_rows(): jnp.dot(flat_field, jnp.sin(angle), precision=lax.Precision.HIGHEST, pref...  15.8 us
    dot_general x1, matrix products, fourier_rows(): jnp.dot(flat_field, jnp.cos(angle), precision=lax.Precision.HIGHEST, pref...  13.2 us
    gather x1, local copies, waits for them, and re-layouts, per_device(): table_rows = jnp.take(legendre, slab_index, axis=0)  9.87 us
    reduce_sum x1, other arithmetic, per_device(): total = jnp.sum(block_part, axis=1)  7.59 us
    all_to_all x1, starting transfers between devices, per_device(): lax.all_to_all(spectra_rows, 'lat', split_axis=0, concat_axis=1, tiled=True)  6.31 us
    all_to_all x1, waiting for transfers between devices, per_device(): lax.all_to_all(spectra_rows, 'lat', split_axis=0, concat_axis=1, tiled=True)  6.01 us
  transfers between devices with their start and end apart: 2, of which 2 were waited for; matrix products, arithmetic and copies ran while one was open for 7% of the time, Pallas kernels for 0%

commit v1 on v0

--- a/solution.py
+++ b/solution.py
@@ -1,9 +1,224 @@
+import functools
 import math
 
 import jax
 import jax.numpy as jnp
+import numpy as np
 from jax import lax
+from jax.experimental import pallas as pl
+from jax.experimental.pallas import tpu as pltpu
 from jax.sharding import PartitionSpec as P
+
+F32 = jnp.float32
+BF16 = jnp.bfloat16
+
+
+def twiddles(nlon, modes):
+    phase = np.arange(nlon)[:, None] * np.arange(modes)[None, :] % nlon
+    angle = phase * (2.0 * math.pi / nlon)
+    scale = 1.0 / math.sqrt(nlon)
+    return np.stack([np.cos(angle) * scale, -np.sin(angle) * scale]).astype(BF16)
+
+
+def position(shift, k, sizes):
+    owner = lax.rem(lax.axis_index("lat") + shift, sizes["lat"])
+    return (owner * sizes["sub"] + lax.axis_index("sub")) * sizes["per"] + k
+
+
+def owned_row(owner_ref, sizes, shifts):
+    lane = lax.broadcasted_iota(jnp.int32, (1, 128), 1)
+    row = jnp.full((1, 128), -1, jnp.int32)
+    j = 0
+    for shift in shifts:
+        base = position(shift, 0, sizes)
+        for k in range(sizes["per"]):
+            row = jnp.where(lane == j, owner_ref[base + k], row)
+            j += 1
+    return row
+
+
+def dft_kernel(sizes, owner_ref, table_ref, field_ref, *refs):
+    outs, chosen = refs[:-1], refs[-1]
+    per = sizes["per"]
+
+    @pl.when(pl.program_id(0) == 0)
+    def _():
+        row = owned_row(owner_ref, sizes, range(sizes["lat"]))
+        modes = table_ref.shape[2]
+        pick = (lax.broadcasted_iota(jnp.int32, (modes, 128), 0) == row).astype(F32).astype(BF16)
+        for r in range(2):
+            chosen[:, r * 128 : (r + 1) * 128] = jnp.dot(
+                table_ref[r], pick, preferred_element_type=F32
+            ).astype(BF16)
+
+    rows, chans, nlon = field_ref.shape
+    grid_values = field_ref[...].reshape(rows * chans, nlon).astype(BF16)
+    spectrum = jnp.dot(grid_values, chosen[...], preferred_element_type=F32)
+    for t in range(rows):
+        part = spectrum[t * chans : (t + 1) * chans]
+        both = jnp.concatenate([part[:, :128], part[:, 128:]], axis=0)
+        turned = both.T
+        for shift in range(sizes["lat"]):
+            outs[shift][t] = turned[shift * per : (shift + 1) * per].astype(BF16)
+
+
+def dft(field, ownership, sizes):
+    lat_rows, chans, nlon = field.shape
+    modes = ownership.shape[0]
+    step = 4
+    per = sizes["per"]
+    table = jnp.asarray(twiddles(nlon, modes))
+    return pl.pallas_call(
+        functools.partial(dft_kernel, sizes),
+        grid=(lat_rows // step,),
+        in_specs=[
+            pl.BlockSpec(memory_space=pltpu.SMEM),
+            pl.BlockSpec((2, nlon, modes), lambda i: (0, 0, 0)),
+            pl.BlockSpec((step, chans, nlon), lambda i: (i, 0, 0)),
+        ],
+        out_specs=[pl.BlockSpec((step, per, 128), lambda i: (i, 0, 0))] * sizes["lat"],
+        out_shape=[jax.ShapeDtypeStruct((lat_rows, per, 128), BF16)] * sizes["lat"],
+        scratch_shapes=[pltpu.VMEM((nlon, 256), BF16)],
+        compiler_params=pltpu.CompilerParams(vmem_limit_bytes=40 << 20),
+        cost_estimate=pl.CostEstimate(
+            flops=2 * lat_rows * chans * nlon * 256, bytes_accessed=field.size * 4, transcendentals=0
+        ),
+        name="dft",
+    )(ownership, table, field)
+
+
+def pick_kernel(sizes, shifts, owner_ref, legendre_ref, *outs):
+    per = sizes["per"]
+    row = owned_row(owner_ref, sizes, shifts) - lax.axis_index("sub") * legendre_ref.shape[1]
+    pick = (lax.broadcasted_iota(jnp.int32, (legendre_ref.shape[1], 128), 0) == row).astype(F32)
+    pick = pick.T[: len(shifts) * per].astype(BF16)
+    for t in range(legendre_ref.shape[0]):
+        rows = jnp.dot(pick, legendre_ref[t], preferred_element_type=F32)
+        for i in range(len(shifts)):
+            outs[i][t] = rows[i * per : (i + 1) * per].astype(BF16)
+
+
+def pick_rows(table, ownership, sizes, shifts, rows, mine):
+    _, slab, degrees = table.shape
+    per = sizes["per"]
+    share = lambda: lax.axis_index("rep") * sizes["ch"] + lax.axis_index("ch") if mine else 0
+    return pl.pallas_call(
+        functools.partial(pick_kernel, sizes, shifts),
+        grid=(1,),
+        in_specs=[
+            pl.BlockSpec(memory_space=pltpu.SMEM),
+            pl.BlockSpec((rows, slab, degrees), lambda i: (share(), 0, 0)),
+        ],
+        out_specs=[pl.BlockSpec((rows, per, degrees), lambda i: (0, 0, 0))] * len(shifts),
+        out_shape=[jax.ShapeDtypeStruct((rows, per, degrees), BF16)] * len(shifts),
+        compiler_params=pltpu.CompilerParams(vmem_limit_bytes=40 << 20),
+        cost_estimate=pl.CostEstimate(
+            flops=2 * rows * slab * degrees * per * len(shifts),
+            bytes_accessed=rows * slab * degrees * 2,
+            transcendentals=0,
+        ),
+        name="pick_rows",
+    )(ownership, table)
+
+
+def contract_kernel(sizes, group, *refs):
+    lats, plane, per = sizes["lat"], sizes["rep"] * sizes["ch"], sizes["per"]
+    near, refs = refs[:lats], refs[lats:]
+    far, refs = refs[:lats], refs[lats:]
+    own_table, refs = refs[0], refs[1:]
+    tables, refs = refs[: plane * (lats - 1)], refs[plane * (lats - 1) :]
+    w_near, w_far, out_ref, spectra, table = refs
+    lat_rows = near[0].shape[0]
+    share = lat_rows // plane
+    depth = lats * lat_rows
+    block = share * per
+
+    @pl.when(pl.program_id(0) == 0)
+    def _():
+        q = lax.axis_index("rep") * sizes["ch"] + lax.axis_index("ch")
+        nt = (((1,), (1,)), ((), ()))
+        for s in range(lats):
+            for d in range(plane):
+                first = d * share if s == 0 else jnp.bitwise_xor(q, d) * share
+                a = near[s][pl.ds(first, share)].reshape(block, 128)
+                b = far[s][pl.ds(first, share)].reshape(block, 128)
+                mixed = lax.dot_general(a, w_near[...], nt, preferred_element_type=F32)
+                mixed += lax.dot_general(b, w_far[...], nt, preferred_element_type=F32)
+                at = (s * plane + d) * block
+                spectra[at : at + block, :] = mixed
+                if s == 0:
+                    values = own_table[d * share : (d + 1) * share]
+                else:
+                    values = tables[d * (lats - 1) + s - 1][...]
+                values = values.astype(F32).reshape(block, values.shape[-1])
+                for tile in range(table.shape[0]):
+                    table[tile, at : at + block, :] = values[:, tile * 128 : (tile + 1) * 128]
+
+    first = pl.program_id(0) * group
+    half = out_ref.shape[2]
+    for k in range(group):
+        a = spectra[pl.ds(first + k, depth, stride=per), :].astype(BF16)
+        b = jnp.concatenate(
+            [table[i, pl.ds(first + k, depth, stride=per), :] for i in range(table.shape[0])], axis=1
+        ).astype(BF16)
+        c = lax.dot_general(a, b, (((0,), (0,)), ((), ())), preferred_element_type=F32)
+        out_ref[0, k] = c[:half].astype(BF16)
+        out_ref[1, k] = c[half:].astype(BF16)
+
+
+def contract(near, far, own_table, tables, w_near, w_far, sizes):
+    lat_rows, per, _ = near[0].shape
+    degrees = own_table.shape[2]
+    half = w_near.shape[0] // 2
+    group = 8
+    depth = sizes["lat"] * lat_rows
+    operands = [*near, *far, own_table, *tables, w_near, w_far]
+    whole = lambda x: pl.BlockSpec(x.shape, lambda i: (0,) * x.ndim)
+    return pl.pallas_call(
+        functools.partial(contract_kernel, sizes, group),
+        grid=(per // group,),
+        in_specs=[whole(x) for x in operands],
+        out_specs=pl.BlockSpec((2, group, half, degrees), lambda i: (0, i, 0, 0)),
+        out_shape=jax.ShapeDtypeStruct((2, per, half, degrees), BF16),
+        scratch_shapes=[pltpu.VMEM((depth * per, 128), F32), pltpu.VMEM((degrees // 128, depth * per, 128), F32)],
+        compiler_params=pltpu.CompilerParams(vmem_limit_bytes=48 << 20),
+        name="contract",
+    )(*operands)
+
+
+def mixing_weights(w_real, w_imag):
+    half = w_real.shape[0]
+    x = lax.axis_index("ch")
+    out = []
+    for side in (x, 1 - x):
+        wr = lax.dynamic_slice_in_dim(w_real, side * half, half, 1)
+        wi = lax.dynamic_slice_in_dim(w_imag, side * half, half, 1)
+        out.append(
+            jnp.concatenate(
+                [jnp.concatenate([wr, -wi], axis=1), jnp.concatenate([wi, wr], axis=1)], axis=0
+            )
+        )
+    return out
+
+
+def fast(field, legendre, ownership, w_real, w_imag, sizes):
+    lats, plane = sizes["lat"], sizes["rep"] * sizes["ch"]
+    lat_rows = field.shape[0]
+    by_latitude = jnp.transpose(legendre, (1, 0, 2))
+    turn = lambda s: [(i, (i + s) % lats) for i in range(lats)]
+    flip = lambda d: [(i, i ^ d) for i in range(plane)]
+    others = tuple(range(1, lats))
+    sent = pick_rows(by_latitude, ownership, sizes, others, lat_rows // plane, True)
+    landed = [lax.ppermute(sent[s - 1], "lat", turn(s)) for s in others]
+    spectra = dft(field, ownership, sizes)
+    near = [spectra[0]] + [lax.ppermute(spectra[s], "lat", turn(s)) for s in others]
+    far = [lax.ppermute(v, "ch", [(0, 1), (1, 0)]) for v in near]
+    tables = list(landed)
+    for d in range(1, plane):
+        tables += [lax.ppermute(v, ("rep", "ch"), flip(d)) for v in landed]
+    (own_table,) = pick_rows(by_latitude, ownership, sizes, (0,), lat_rows, False)
+    w_near, w_far = mixing_weights(w_real, w_imag)
+    return contract(near, far, own_table, tables, w_near, w_far, sizes)
 
 
 def fourier_rows(flat_field, modes, lat_rows, chans, nlon):
@@ -34,7 +249,7 @@
     return both.astype(jnp.bfloat16)
 
 
-def per_device(field, legendre, ownership, w_real, w_imag):
+def general(field, legendre, ownership, w_real, w_imag):
     lat_rows, chans, nlon = field.shape
     degrees = legendre.shape[2]
     slab_modes = legendre.shape[0]
@@ -57,7 +272,6 @@
     block_part = jnp.einsum(
         "kbtc,kbtl->kbcl", spectra_all, tables_all, preferred_element_type=jnp.float32
     )
-    block_part = lax.optimization_barrier(block_part.astype(jnp.bfloat16)).astype(jnp.float32)
     total = jnp.sum(block_part, axis=1)
     coeff = total.astype(jnp.bfloat16).reshape(per_block, 2, chans, degrees)
     piece = lax.all_gather(coeff, "ch", axis=2, tiled=True)
@@ -73,6 +287,25 @@
     return mixed.astype(jnp.bfloat16)
 
 
+def per_device(sizes, field, legendre, ownership, w_real, w_imag):
+    lat_rows, chans, nlon = field.shape
+    sizes = dict(sizes, per=ownership.shape[0] // (sizes["lat"] * sizes["sub"]))
+    plane = sizes["rep"] * sizes["ch"]
+    fits = (
+        sizes["ch"] == 2
+        and 2 * chans == 128
+        and plane & (plane - 1) == 0
+        and lat_rows % plane == 0
+        and lat_rows % 4 == 0
+        and sizes["per"] % 8 == 0
+        and sizes["lat"] * sizes["per"] <= 128
+        and legendre.shape[2] % 128 == 0
+    )
+    if fits:
+        return fast(field, legendre, ownership, w_real, w_imag, sizes)
+    return general(field, legendre, ownership, w_real, w_imag)
+
+
 def solution(mesh):
     in_specs = (
         P(("rep", "lat"), "ch", None),
@@ -83,5 +316,9 @@
     )
     out_specs = P("rep", ("lat", "sub"), "ch", None)
     return jax.shard_map(
-        per_device, mesh=mesh, in_specs=in_specs, out_specs=out_specs, check_vma=False
-    )
+        functools.partial(per_device, dict(mesh.shape)),
+        mesh=mesh,
+        in_specs=in_specs,
+        out_specs=out_specs,
+        check_vma=False,
+    )

time: 214 us -> 65.5 us (0.31)
  blocking collectives: 56.9 us -> 0 us
  waiting for transfers between devices: 67.9 us -> 19.2 us
  matrix products: 37.9 us -> 0 us
  starting transfers between devices: 6.32 us -> 27.2 us
  between operations: 13.5 us -> 0.11 us
  local copies, waits for them, and re-layouts: 19.8 us -> 7.06 us
  Pallas kernels: 0 us -> 11.4 us
  other arithmetic: 11.4 us -> 0.26 us
    all_gather x1 -> x0, waiting for transfers between devices: 61.9 us -> none  [per_device(): piece = lax.all_gather(coeff, 'ch', axis=2, tiled=True)]
    all_to_all x1 -> x0, blocking collectives: 56.9 us -> none  [per_device(): lax.all_to_all(table_rows, 'lat', split_axis=0, concat_axis=1, tiled=True)]
    dot_general x7 -> x0, matrix products: 37.9 us -> none  [the longest x1 15.8 us: fourier_rows(): jnp.dot(flat_field, jnp.sin(angle), precision=lax.Precision.HIGHEST, pref...]
    ppermute x0 -> x19, starting transfers between devices: none -> 27.2 us  [the longest x9 11.8 us: fast(): tables += [lax.ppermute(v, ('rep', 'ch'), flip(d)) for v in landed]]
    ppermute x0 -> x19, waiting for transfers between devices: none -> 19.2 us  [the longest x4 6.96 us: fast(): far = [lax.ppermute(v, 'ch', [(0, 1), (1, 0)]) for v in near]]
    pallas_call x0 -> x4, Pallas kernels: none -> 11.4 us  [the longest x1 4.85 us: contract(): pl.pallas_call(functools.partial(contract_kernel, sizes, group), grid=(pe...]
    gather x1 -> x0, local copies, waits for them, and re-layouts: 9.87 us -> none  [per_device(): table_rows = jnp.take(legendre, slab_index, axis=0)]
    reduce_sum x1 -> x0, other arithmetic: 7.59 us -> none  [per_device(): total = jnp.sum(block_part, axis=1)]
  transfers between devices with their start and end apart: 2 -> 19, of which waited for: 2 -> 7; matrix products, arithmetic and copies ran while one was open for 7% -> 0% of each run, Pallas kernels for 0% -> 9%
where the time goes in v1:
time: 65.5 us; the launch traced here: 65.2 us
  starting transfers between devices  27.2 us (42%)
  waiting for transfers between devices  19.2 us (29%)
  Pallas kernels  11.4 us (17%)
  local copies, waits for them, and re-layouts  7.06 us (11%)
    ppermute x9, starting transfers between devices, fast(): tables += [lax.ppermute(v, ('rep', 'ch'), flip(d)) for v in landed]  11.8 us
    ppermute x3, starting transfers between devices, fast(): landed = [lax.ppermute(sent[s - 1], 'lat', turn(s)) for s in others]  9.41 us
    unnamed x20, local copies, waits for them, and re-layouts  7.06 us
    ppermute x4, waiting for transfers between devices, fast(): far = [lax.ppermute(v, 'ch', [(0, 1), (1, 0)]) for v in near]  6.96 us
    ppermute x4, starting transfers between devices, fast(): far = [lax.ppermute(v, 'ch', [(0, 1), (1, 0)]) for v in near]  5.23 us
    pallas_call x1, Pallas kernels, contract(): pl.pallas_call(functools.partial(contract_kernel, sizes, group), grid=(pe...  4.85 us
    ppermute x3, waiting for transfers between devices, fast(): landed = [lax.ppermute(sent[s - 1], 'lat', turn(s)) for s in others]  4.84 us
    pallas_call x1, Pallas kernels, dft(): pl.pallas_call(functools.partial(dft_kernel, sizes), grid=(lat_rows // st...  4.48 us
  transfers between devices with their start and end apart: 19, of which 7 were waited for; matrix products, arithmetic and copies ran while one was open for 0% of the time, Pallas kernels for 9%

profile of v1, /device:TPU:0, one launch (start us, length us, event | category | flops | bytes accessed | tf_op | source)
XLA Modules:
  0.0 65.2 jit_solution(9360581145793942203)
XLA Ops:
  0.0 0.0 copy-start.1
  0.0 1.6 %copy-done.1 = bf16[96,28,384]{2,0,1:T(8,128)(2,1)S(1)} copy-done((bf16[96,28,384]{2,0,1:T(8,128)(2,1)S(1)}, bf16[96,28,384]{2,0,1:T(8,128)(2,1)}, u32[]{:S(2)}) %copy-start.1) | copy-done | bytes 2064408
  1.6 0.0 copy-start.6
  1.6 0.7 %copy-done.6 = s32[192]{0:T(256)S(1)} copy-done((s32[192]{0:T(256)S(1)}, s32[192]{0:T(256)}, u32[]{:S(2)}) %copy-start.6) | copy-done | bytes 792
  2.3 0.0 copy-start.3
  2.3 1.0 %pick_rows.3 = (bf16[7,24,384]{2,1,0:T(8,128)(2,1)S(1)}, bf16[7,24,384]{2,1,0:T(8,128)(2,1)S(1)}, bf16[7,24,384]{2,1,0:T(8,128)(2,1)S(1)}) custom-call(s32[192]{0:T(256)S(1)} %copy-done.6, bf16[28,96,384]{2,1,0:T(8,128)(2,1)S(1)} %bitcast.1), custom_call_target="tpu_custom_call" | custom-call | flops 37158912 | bytes 516096 | tf_op jit(solution)/shard_map/pick_rows/pallas_call | solution.py:105
  3.2 3.1 %collective-permute-start.7 = (bf16[7,24,384]{2,1,0:T(8,128)(2,1)S(1)}, bf16[7,24,384]{2,1,0:T(8,128)(2,1)S(1)}, u32[]{:S(2)}, u32[]{:S(2)}) collective-permute-start(bf16[7,24,384]{2,1,0:T(8,128)(2,1)S(1)} %get-tuple-element.16), channel_id=1, source_target_pairs={{0,4},{4,8},{8,12},{12,0},{1,5},{5,9},{9,13},{13,1},{2,6},{6,10},{... | collective-permute-start | bytes 387080 | tf_op jit(solution)/shard_map/ppermute | solution.py:212
  6.3 2.6 %collective-permute-start.8 = (bf16[7,24,384]{2,1,0:T(8,128)(2,1)S(1)}, bf16[7,24,384]{2,1,0:T(8,128)(2,1)S(1)}, u32[]{:S(2)}, u32[]{:S(2)}) collective-permute-start(bf16[7,24,384]{2,1,0:T(8,128)(2,1)S(1)} %get-tuple-element.17), channel_id=1, source_target_pairs={{0,8},{4,12},{8,0},{12,4},{1,9},{5,13},{9,1},{13,5},{2,10},{6,14},... | collective-permute-start | bytes 387080 | tf_op jit(solution)/shard_map/ppermute | solution.py:212
  8.9 0.0 copy-done.3
  8.9 4.1 %copy-done = f32[28,64,1440]{2,1,0:T(8,128)S(1)} copy-done((f32[28,64,1440]{2,1,0:T(8,128)S(1)}, f32[28,64,1440]{2,1,0:T(8,128)}, u32[]{:S(2)}) %copy-start) | copy-done | bytes 10321944
  13.0 0.0 copy-start.8
  13.0 0.0 copy-start.9
  13.0 0.0 copy-start.2
  13.0 0.0 copy-start.7
  13.0 4.5 %dft.1 = (bf16[28,24,128]{2,1,0:T(8,128)(2,1)S(1)}, bf16[28,24,128]{2,1,0:T(8,128)(2,1)S(1)}, bf16[28,24,128]{2,1,0:T(8,128)(2,1)S(1)}, bf16[28,24,128]{2,1,0:T(8,128)(2,1)S(1)}) custom-call(s32[192]{0:T(256)S(1)} %copy-done.6, bf16[2,1440,192]{2,1,0:T(8,128)(2,1)S(1)} %copy-done.3, f32[28,64,1440]{2,1,0:T(8,128)S(1)} %copy-done), custom_call_target="tpu_custom_call" | custom-call | flops 1321205760 | bytes 10321920 | tf_op jit(solution)/shard_map/dft/pallas_call | solution.py:71
  17.5 0.1 collective-permute-start
  17.6 3.7 %collective-permute-start.9 = (bf16[7,24,384]{2,1,0:T(8,128)(2,1)S(1)}, bf16[7,24,384]{2,1,0:T(8,128)(2,1)S(1)}, u32[]{:S(2)}, u32[]{:S(2)}) collective-permute-start(bf16[7,24,384]{2,1,0:T(8,128)(2,1)S(1)} %get-tuple-element.18), channel_id=1, source_target_pairs={{0,12},{4,0},{8,4},{12,8},{1,13},{5,1},{9,5},{13,9},{2,14},{6,2},{... | collective-permute-start | bytes 387080 | tf_op jit(solution)/shard_map/ppermute | solution.py:212
  21.4 0.0 collective-permute-start.1
  21.4 0.0 collective-permute-done.7.refs_9_
  21.4 0.6 collective-permute-start.2
  22.0 0.0 collective-permute-done.8.refs_10_
  22.0 1.6 %collective-permute-start.3 = (bf16[28,24,128]{2,1,0:T(8,128)(2,1)S(1)}, bf16[28,24,128]{2,1,0:T(8,128)(2,1)S(1)}, u32[]{:S(2)}, u32[]{:S(2)}) collective-permute-start(bf16[28,24,128]{2,1,0:T(8,128)(2,1)S(1)} %get-tuple-element.12.refs_0_), channel_id=1, source_target_pairs={{0,2},{2,0},{1,3},{3,1},{4,6},{6,4},{5,7},{7,5},{8,10},{10,8},{9,1... | collective-permute-start | bytes 516104 | tf_op jit(solution)/shard_map/ppermute | solution.py:215
  23.7 4.8 %collective-permute-done.9.refs_11_ = bf16[7,24,384]{2,1,0:T(8,128)(2,1)S(1)} collective-permute-done((bf16[7,24,384]{2,1,0:T(8,128)(2,1)S(1)}, bf16[7,24,384]{2,1,0:T(8,128)(2,1)S(1)}, u32[]{:S(2)}, u32[]{:S(2)}) %collective-permute-start.9) | collective-permute-done | bytes 129056 | tf_op jit(solution)/shard_map/ppermute | solution.py:212
  28.5 2.6 %collective-permute-start.16 = (bf16[7,24,384]{2,1,0:T(8,128)(2,1)S(1)}, bf16[7,24,384]{2,1,0:T(8,128)(2,1)S(1)}, u32[]{:S(2)}, u32[]{:S(2)}) collective-permute-start(bf16[7,24,384]{2,1,0:T(8,128)(2,1)S(1)} %collective-permute-done.7.refs_9_), channel_id=1, source_target_pairs={{0,18},{2,16},{16,2},{18,0},{1,19},{3,17},{17,3},{19,1},{4,22},{6,... | collective-permute-start | bytes 387080 | tf_op jit(solution)/shard_map/ppermute | solution.py:218
  31.1 0.0 collective-permute-done.refs_1_
  31.1 0.5 collective-permute-start.13
  31.6 3.2 %collective-permute-done.1.refs_2_ = bf16[28,24,128]{2,1,0:T(8,128)(2,1)S(1)} collective-permute-done((bf16[28,24,128]{2,1,0:T(8,128)(2,1)S(1)}, bf16[28,24,128]{2,1,0:T(8,128)(2,1)S(1)}, u32[]{:S(2)}, u32[]{:S(2)}) %collective-permute-start.1) | collective-permute-done | bytes 172064 | tf_op jit(solution)/shard_map/ppermute | solution.py:214
  34.8 1.5 %collective-permute-start.10 = (bf16[7,24,384]{2,1,0:T(8,128)(2,1)S(1)}, bf16[7,24,384]{2,1,0:T(8,128)(2,1)}, u32[]{:S(2)}, u32[]{:S(2)}) collective-permute-start(bf16[7,24,384]{2,1,0:T(8,128)(2,1)S(1)} %collective-permute-done.7.refs_9_), channel_id=1, source_target_pairs={{0,2},{2,0},{16,18},{18,16},{1,3},{3,1},{17,19},{19,17},{4,6},{6,4... | collective-permute-start | bytes 387080 | tf_op jit(solution)/shard_map/ppermute | solution.py:218
  36.3 0.0 collective-permute-done.2.refs_3_
  36.3 1.5 %collective-permute-start.17 = (bf16[7,24,384]{2,1,0:T(8,128)(2,1)S(1)}, bf16[7,24,384]{2,1,0:T(8,128)(2,1)}, u32[]{:S(2)}, u32[]{:S(2)}) collective-permute-start(bf16[7,24,384]{2,1,0:T(8,128)(2,1)S(1)} %collective-permute-done.8.refs_10_), channel_id=1, source_target_pairs={{0,18},{2,16},{16,2},{18,0},{1,19},{3,17},{17,3},{19,1},{4,22},{6,... | collective-permute-start | bytes 387080 | tf_op jit(solution)/shard_map/ppermute | solution.py:218
  37.8 0.0 collective-permute-done.3.refs_4_
  37.8 0.5 collective-permute-start.14
  38.3 0.0 collective-permute-done.16.refs_18_
  38.3 1.5 %collective-permute-start.11 = (bf16[7,24,384]{2,1,0:T(8,128)(2,1)S(1)}, bf16[7,24,384]{2,1,0:T(8,128)(2,1)}, u32[]{:S(2)}, u32[]{:S(2)}) collective-permute-start(bf16[7,24,384]{2,1,0:T(8,128)(2,1)S(1)} %collective-permute-done.8.refs_10_), channel_id=1, source_target_pairs={{0,2},{2,0},{16,18},{18,16},{1,3},{3,1},{17,19},{19,17},{4,6},{6,4... | collective-permute-start | bytes 387080 | tf_op jit(solution)/shard_map/ppermute | solution.py:218
  39.8 0.0 collective-permute-done.13.refs_15_
  39.8 0.0 copy-start.4
  39.9 0.6 copy-done.4
  40.5 1.5 %collective-permute-start.18 = (bf16[7,24,384]{2,1,0:T(8,128)(2,1)S(1)}, bf16[7,24,384]{2,1,0:T(8,128)(2,1)}, u32[]{:S(2)}, u32[]{:S(2)}) collective-permute-start(bf16[7,24,384]{2,1,0:T(8,128)(2,1)S(1)} %collective-permute-done.9.refs_11_), channel_id=1, source_target_pairs={{0,18},{2,16},{16,2},{18,0},{1,19},{3,17},{17,3},{19,1},{4,22},{6,... | collective-permute-start | bytes 387080 | tf_op jit(solution)/shard_map/ppermute | solution.py:218
  42.0 0.0 copy-done.8
  42.0 0.0 copy-done.9
  42.0 0.0 copy-start.5
  42.0 0.1 constant_dynamic-slice_fusion.1
  42.1 0.0 collective-permute-done.10.refs_12_
  42.1 0.7 %collective-permute-start.15 = (bf16[7,24,384]{2,1,0:T(8,128)(2,1)S(1)}, bf16[7,24,384]{2,1,0:T(8,128)(2,1)S(1)}, u32[]{:S(2)}, u32[]{:S(2)}) collective-permute-start(bf16[7,24,384]{2,1,0:T(8,128)(2,1)S(1)} %collective-permute-done.9.refs_11_), channel_id=1, source_target_pairs={{0,16},{2,18},{16,0},{18,2},{1,17},{3,19},{17,1},{19,3},{4,20},{6,... | collective-permute-start | bytes 387080 | tf_op jit(solution)/shard_map/ppermute | solution.py:218
  42.8 2.2 %collective-permute-done.17.refs_19_ = bf16[7,24,384]{2,1,0:T(8,128)(2,1)} collective-permute-done((bf16[7,24,384]{2,1,0:T(8,128)(2,1)S(1)}, bf16[7,24,384]{2,1,0:T(8,128)(2,1)}, u32[]{:S(2)}, u32[]{:S(2)}) %collective-permute-start.17) | collective-permute-done | bytes 129056 | tf_op jit(solution)/shard_map/ppermute | solution.py:218
  45.0 1.6 %collective-permute-start.12 = (bf16[7,24,384]{2,1,0:T(8,128)(2,1)S(1)}, bf16[7,24,384]{2,1,0:T(8,128)(2,1)S(1)}, u32[]{:S(2)}, u32[]{:S(2)}) collective-permute-start(bf16[7,24,384]{2,1,0:T(8,128)(2,1)S(1)} %collective-permute-done.9.refs_11_), channel_id=1, source_target_pairs={{0,2},{2,0},{16,18},{18,16},{1,3},{3,1},{17,19},{19,17},{4,6},{6,4... | collective-permute-start | bytes 387080 | tf_op jit(solution)/shard_map/ppermute | solution.py:218
  46.6 0.0 collective-permute-done.14.refs_16_
  46.6 0.8 %collective-permute-start.4 = (bf16[28,24,128]{2,1,0:T(8,128)(2,1)S(1)}, bf16[28,24,128]{2,1,0:T(8,128)(2,1)S(1)}, u32[]{:S(2)}, u32[]{:S(2)}) collective-permute-start(bf16[28,24,128]{2,1,0:T(8,128)(2,1)S(1)} %collective-permute-done.refs_1_), channel_id=1, source_target_pairs={{0,2},{2,0},{1,3},{3,1},{4,6},{6,4},{5,7},{7,5},{8,10},{10,8},{9,1... | collective-permute-start | bytes 516104 | tf_op jit(solution)/shard_map/ppermute | solution.py:215
  47.4 0.0 collective-permute-done.11.refs_13_
  47.4 1.2 %collective-permute-start.5 = (bf16[28,24,128]{2,1,0:T(8,128)(2,1)S(1)}, bf16[28,24,128]{2,1,0:T(8,128)(2,1)S(1)}, u32[]{:S(2)}, u32[]{:S(2)}) collective-permute-start(bf16[28,24,128]{2,1,0:T(8,128)(2,1)S(1)} %collective-permute-done.1.refs_2_), channel_id=1, source_target_pairs={{0,2},{2,0},{1,3},{3,1},{4,6},{6,4},{5,7},{7,5},{8,10},{10,8},{9,1... | collective-permute-start | bytes 516104 | tf_op jit(solution)/shard_map/ppermute | solution.py:215
  48.6 1.9 %collective-permute-done.18.refs_20_ = bf16[7,24,384]{2,1,0:T(8,128)(2,1)} collective-permute-done((bf16[7,24,384]{2,1,0:T(8,128)(2,1)S(1)}, bf16[7,24,384]{2,1,0:T(8,128)(2,1)}, u32[]{:S(2)}, u32[]{:S(2)}) %collective-permute-start.18) | collective-permute-done | bytes 129056 | tf_op jit(solution)/shard_map/ppermute | solution.py:218
  50.5 1.6 %collective-permute-start.6 = (bf16[28,24,128]{2,1,0:T(8,128)(2,1)S(1)}, bf16[28,24,128]{2,1,0:T(8,128)(2,1)S(1)}, u32[]{:S(2)}, u32[]{:S(2)}) collective-permute-start(bf16[28,24,128]{2,1,0:T(8,128)(2,1)S(1)} %collective-permute-done.2.refs_3_), channel_id=1, source_target_pairs={{0,2},{2,0},{1,3},{3,1},{4,6},{6,4},{5,7},{7,5},{8,10},{10,8},{9,1... | collective-permute-start | bytes 516104 | tf_op jit(solution)/shard_map/ppermute | solution.py:215
  52.1 0.1 maximum_maximum_fusion.1.refs_22_
  52.2 0.0 copy-done.2
  52.2 0.0 copy-done.7
  52.2 1.1 %pick_rows.2.refs_8_ = bf16[28,24,384]{2,1,0:T(8,128)(2,1)S(1)} custom-call(s32[192]{0:T(256)S(1)} %copy-done.7, bf16[28,96,384]{2,1,0:T(8,128)(2,1)S(1)} %bitcast.2), custom_call_target="tpu_custom_call" | custom-call | flops 49545216 | bytes 2064384 | tf_op jit(solution)/shard_map/pick_rows/pallas_call | solution.py:105
  53.3 0.1 maximum_maximum_fusion.refs_21_
  53.4 0.0 collective-permute-done.15.refs_17_
  53.4 0.0 collective-permute-done.12.refs_14_
  53.4 2.6 %collective-permute-done.4.refs_5_ = bf16[28,24,128]{2,1,0:T(8,128)(2,1)S(1)} collective-permute-done((bf16[28,24,128]{2,1,0:T(8,128)(2,1)S(1)}, bf16[28,24,128]{2,1,0:T(8,128)(2,1)S(1)}, u32[]{:S(2)}, u32[]{:S(2)}) %collective-permute-start.4) | collective-permute-done | bytes 172064 | tf_op jit(solution)/shard_map/ppermute | solution.py:215
  56.0 2.5 %collective-permute-done.5.refs_6_ = bf16[28,24,128]{2,1,0:T(8,128)(2,1)S(1)} collective-permute-done((bf16[28,24,128]{2,1,0:T(8,128)(2,1)S(1)}, bf16[28,24,128]{2,1,0:T(8,128)(2,1)S(1)}, u32[]{:S(2)}, u32[]{:S(2)}) %collective-permute-start.5) | collective-permute-done | bytes 172064 | tf_op jit(solution)/shard_map/ppermute | solution.py:215
  58.5 1.8 %collective-permute-done.6.refs_7_ = bf16[28,24,128]{2,1,0:T(8,128)(2,1)S(1)} collective-permute-done((bf16[28,24,128]{2,1,0:T(8,128)(2,1)S(1)}, bf16[28,24,128]{2,1,0:T(8,128)(2,1)S(1)}, u32[]{:S(2)}, u32[]{:S(2)}) %collective-permute-start.6) | collective-permute-done | bytes 172064 | tf_op jit(solution)/shard_map/ppermute | solution.py:215
  60.4 0.0 copy-done.5
  60.4 4.8 %contract.1 = bf16[2,24,64,384]{3,2,1,0:T(8,128)(2,1)} custom-call(bf16[28,24,128]{2,1,0:T(8,128)(2,1)S(1)} %get-tuple-element.12.refs_0_, bf16[28,24,128]{2,1,0:T(8,128)(2,1)S(1)} %collective-permute-done.refs_1_, bf16[28,24,128]{2,1,0:T(8,128)(2,1)S(1)} %collective-permute-done.1.refs_2_, bf16[28,24,128]{2,1,0:T(8,128)(2,1)S(1)} %collective-permute-done.2.refs_3_, ...), custom_call_target="tpu_custom_call" | custom-call | tf_op jit(solution)/shard_map/contract/pallas_call | solution.py:177
  (1 shorter events, 0.0 us)
Async XLA Ops:
  0.0 1.6 %copy-start.1 = (bf16[96,28,384]{2,0,1:T(8,128)(2,1)S(1)}, bf16[96,28,384]{2,0,1:T(8,128)(2,1)}, u32[]{:S(2)}) copy-start(bf16[96,28,384]{2,0,1:T(8,128)(2,1)} %param.7) | copy-start | bytes 6193156
  1.6 0.7 %copy-start.6 = (s32[192]{0:T(256)S(1)}, s32[192]{0:T(256)}, u32[]{:S(2)}) copy-start(s32[192]{0:T(256)} %owner_ref.5) | copy-start | bytes 2308
  2.3 6.6 %copy-start.3 = (bf16[2,1440,192]{2,1,0:T(8,128)(2,1)S(1)}, bf16[2,1440,192]{2,1,0:T(8,128)(2,1)}, u32[]{:S(2)}) copy-start(bf16[2,1440,192]{2,1,0:T(8,128)(2,1)} %constant.14.clone.table_ref) | copy-start | bytes 3317764
  3.2 18.2 %collective-permute-start.7 = (bf16[7,24,384]{2,1,0:T(8,128)(2,1)S(1)}, bf16[7,24,384]{2,1,0:T(8,128)(2,1)S(1)}, u32[]{:S(2)}, u32[]{:S(2)}) collective-permute-start(bf16[7,24,384]{2,1,0:T(8,128)(2,1)S(1)} %get-tuple-element.16), channel_id=1, source_target_pairs={{0,4},{4,8},{8,12},{12,0},{1,5},{5,9},{9,13},{13,1},{2,6},{6,10},{... | collective-permute-start | bytes 387080 | tf_op jit(solution)/shard_map/ppermute | solution.py:212
  6.3 15.7 %collective-permute-start.8 = (bf16[7,24,384]{2,1,0:T(8,128)(2,1)S(1)}, bf16[7,24,384]{2,1,0:T(8,128)(2,1)S(1)}, u32[]{:S(2)}, u32[]{:S(2)}) collective-permute-start(bf16[7,24,384]{2,1,0:T(8,128)(2,1)S(1)} %get-tuple-element.17), channel_id=1, source_target_pairs={{0,8},{4,12},{8,0},{12,4},{1,9},{5,13},{9,1},{13,5},{2,10},{6,14},... | collective-permute-start | bytes 387080 | tf_op jit(solution)/shard_map/ppermute | solution.py:212
  8.9 4.1 %copy-start = (f32[28,64,1440]{2,1,0:T(8,128)S(1)}, f32[28,64,1440]{2,1,0:T(8,128)}, u32[]{:S(2)}) copy-start(f32[28,64,1440]{2,1,0:T(8,128)} %field_ref.1) | copy-start | bytes 30965764
  13.0 29.0 %copy-start.8 = (bf16[64,128]{1,0:T(8,128)(2,1)S(1)}, bf16[64,128]{1,0:T(8,128)(2,1)}, u32[]{:S(2)}) copy-start(bf16[64,128]{1,0:T(8,128)(2,1)} %param.9) | copy-start | bytes 49156
  13.0 29.0 %copy-start.9 = (bf16[64,128]{1,0:T(8,128)(2,1)S(1)}, bf16[64,128]{1,0:T(8,128)(2,1)}, u32[]{:S(2)}) copy-start(bf16[64,128]{1,0:T(8,128)(2,1)} %param.10) | copy-start | bytes 49156
  13.0 39.2 %copy-start.2 = (bf16[96,28,384]{2,0,1:T(8,128)(2,1)S(1)}, bf16[96,28,384]{2,0,1:T(8,128)(2,1)}, u32[]{:S(2)}) copy-start(bf16[96,28,384]{2,0,1:T(8,128)(2,1)} %param.7) | copy-start | bytes 6193156
  13.0 39.2 %copy-start.7 = (s32[192]{0:T(256)S(1)}, s32[192]{0:T(256)}, u32[]{:S(2)}) copy-start(s32[192]{0:T(256)} %owner_ref.5) | copy-start | bytes 2308
  17.5 13.6 %collective-permute-start = (bf16[28,24,128]{2,1,0:T(8,128)(2,1)S(1)}, bf16[28,24,128]{2,1,0:T(8,128)(2,1)S(1)}, u32[]{:S(2)}, u32[]{:S(2)}) collective-permute-start(bf16[28,24,128]{2,1,0:T(8,128)(2,1)S(1)} %get-tuple-element.13), channel_id=1, source_target_pairs={{0,4},{4,8},{8,12},{12,0},{1,5},{5,9},{9,13},{13,1},{2,6},{6,10},{... | collective-permute-start | bytes 516104 | tf_op jit(solution)/shard_map/ppermute | solution.py:214
  17.6 10.9 %collective-permute-start.9 = (bf16[7,24,384]{2,1,0:T(8,128)(2,1)S(1)}, bf16[7,24,384]{2,1,0:T(8,128)(2,1)S(1)}, u32[]{:S(2)}, u32[]{:S(2)}) collective-permute-start(bf16[7,24,384]{2,1,0:T(8,128)(2,1)S(1)} %get-tuple-element.18), channel_id=1, source_target_pairs={{0,12},{4,0},{8,4},{12,8},{1,13},{5,1},{9,5},{13,9},{2,14},{6,2},{... | collective-permute-start | bytes 387080 | tf_op jit(solution)/shard_map/ppermute | solution.py:212
  21.4 13.4 %collective-permute-start.1 = (bf16[28,24,128]{2,1,0:T(8,128)(2,1)S(1)}, bf16[28,24,128]{2,1,0:T(8,128)(2,1)S(1)}, u32[]{:S(2)}, u32[]{:S(2)}) collective-permute-start(bf16[28,24,128]{2,1,0:T(8,128)(2,1)S(1)} %get-tuple-element.14), channel_id=1, source_target_pairs={{0,8},{4,12},{8,0},{12,4},{1,9},{5,13},{9,1},{13,5},{2,10},{6,14},... | collective-permute-start | bytes 516104 | tf_op jit(solution)/shard_map/ppermute | solution.py:214
  21.4 14.9 %collective-permute-start.2 = (bf16[28,24,128]{2,1,0:T(8,128)(2,1)S(1)}, bf16[28,24,128]{2,1,0:T(8,128)(2,1)S(1)}, u32[]{:S(2)}, u32[]{:S(2)}) collective-permute-start(bf16[28,24,128]{2,1,0:T(8,128)(2,1)S(1)} %get-tuple-element.15), channel_id=1, source_target_pairs={{0,12},{4,0},{8,4},{12,8},{1,13},{5,1},{9,5},{13,9},{2,14},{6,2},{... | collective-permute-start | bytes 516104 | tf_op jit(solution)/shard_map/ppermute | solution.py:214
  22.0 15.8 %collective-permute-start.3 = (bf16[28,24,128]{2,1,0:T(8,128)(2,1)S(1)}, bf16[28,24,128]{2,1,0:T(8,128)(2,1)S(1)}, u32[]{:S(2)}, u32[]{:S(2)}) collective-permute-start(bf16[28,24,128]{2,1,0:T(8,128)(2,1)S(1)} %get-tuple-element.12.refs_0_), channel_id=1, source_target_pairs={{0,2},{2,0},{1,3},{3,1},{4,6},{6,4},{5,7},{7,5},{8,10},{10,8},{9,1... | collective-permute-start | bytes 516104 | tf_op jit(solution)/shard_map/ppermute | solution.py:215
  28.5 9.8 %collective-permute-start.16 = (bf16[7,24,384]{2,1,0:T(8,128)(2,1)S(1)}, bf16[7,24,384]{2,1,0:T(8,128)(2,1)S(1)}, u32[]{:S(2)}, u32[]{:S(2)}) collective-permute-start(bf16[7,24,384]{2,1,0:T(8,128)(2,1)S(1)} %collective-permute-done.7.refs_9_), channel_id=1, source_target_pairs={{0,18},{2,16},{16,2},{18,0},{1,19},{3,17},{17,3},{19,1},{4,22},{6,... | collective-permute-start | bytes 387080 | tf_op jit(solution)/shard_map/ppermute | solution.py:218
  31.1 8.7 %collective-permute-start.13 = (bf16[7,24,384]{2,1,0:T(8,128)(2,1)S(1)}, bf16[7,24,384]{2,1,0:T(8,128)(2,1)S(1)}, u32[]{:S(2)}, u32[]{:S(2)}) collective-permute-start(bf16[7,24,384]{2,1,0:T(8,128)(2,1)S(1)} %collective-permute-done.7.refs_9_), channel_id=1, source_target_pairs={{0,16},{2,18},{16,0},{18,2},{1,17},{3,19},{17,1},{19,3},{4,20},{6,... | collective-permute-start | bytes 387080 | tf_op jit(solution)/shard_map/ppermute | solution.py:218
  34.8 7.2 %collective-permute-start.10 = (bf16[7,24,384]{2,1,0:T(8,128)(2,1)S(1)}, bf16[7,24,384]{2,1,0:T(8,128)(2,1)}, u32[]{:S(2)}, u32[]{:S(2)}) collective-permute-start(bf16[7,24,384]{2,1,0:T(8,128)(2,1)S(1)} %collective-permute-done.7.refs_9_), channel_id=1, source_target_pairs={{0,2},{2,0},{16,18},{18,16},{1,3},{3,1},{17,19},{19,17},{4,6},{6,4... | collective-permute-start | bytes 387080 | tf_op jit(solution)/shard_map/ppermute | solution.py:218
  36.3 8.7 %collective-permute-start.17 = (bf16[7,24,384]{2,1,0:T(8,128)(2,1)S(1)}, bf16[7,24,384]{2,1,0:T(8,128)(2,1)}, u32[]{:S(2)}, u32[]{:S(2)}) collective-permute-start(bf16[7,24,384]{2,1,0:T(8,128)(2,1)S(1)} %collective-permute-done.8.refs_10_), channel_id=1, source_target_pairs={{0,18},{2,16},{16,2},{18,0},{1,19},{3,17},{17,3},{19,1},{4,22},{6,... | collective-permute-start | bytes 387080 | tf_op jit(solution)/shard_map/ppermute | solution.py:218
  37.8 8.7 %collective-permute-start.14 = (bf16[7,24,384]{2,1,0:T(8,128)(2,1)S(1)}, bf16[7,24,384]{2,1,0:T(8,128)(2,1)}, u32[]{:S(2)}, u32[]{:S(2)}) collective-permute-start(bf16[7,24,384]{2,1,0:T(8,128)(2,1)S(1)} %collective-permute-done.8.refs_10_), channel_id=1, source_target_pairs={{0,16},{2,18},{16,0},{18,2},{1,17},{3,19},{17,1},{19,3},{4,20},{6,... | collective-permute-start | bytes 387080 | tf_op jit(solution)/shard_map/ppermute | solution.py:218
  38.3 9.1 %collective-permute-start.11 = (bf16[7,24,384]{2,1,0:T(8,128)(2,1)S(1)}, bf16[7,24,384]{2,1,0:T(8,128)(2,1)}, u32[]{:S(2)}, u32[]{:S(2)}) collective-permute-start(bf16[7,24,384]{2,1,0:T(8,128)(2,1)S(1)} %collective-permute-done.8.refs_10_), channel_id=1, source_target_pairs={{0,2},{2,0},{16,18},{18,16},{1,3},{3,1},{17,19},{19,17},{4,6},{6,4... | collective-permute-start | bytes 387080 | tf_op jit(solution)/shard_map/ppermute | solution.py:218
  39.8 0.7 copy-start.4
  40.5 10.0 %collective-permute-start.18 = (bf16[7,24,384]{2,1,0:T(8,128)(2,1)S(1)}, bf16[7,24,384]{2,1,0:T(8,128)(2,1)}, u32[]{:S(2)}, u32[]{:S(2)}) collective-permute-start(bf16[7,24,384]{2,1,0:T(8,128)(2,1)S(1)} %collective-permute-done.9.refs_11_), channel_id=1, source_target_pairs={{0,18},{2,16},{16,2},{18,0},{1,19},{3,17},{17,3},{19,1},{4,22},{6,... | collective-permute-start | bytes 387080 | tf_op jit(solution)/shard_map/ppermute | solution.py:218
  42.0 18.4 %copy-start.5 = (bf16[7,24,384]{2,1,0:T(8,128)(2,1)S(1)}, bf16[7,24,384]{2,1,0:T(8,128)(2,1)}, u32[]{:S(2)}) copy-start(bf16[7,24,384]{2,1,0:T(8,128)(2,1)} %copy-done.4) | copy-start | bytes 387076
  42.1 11.3 %collective-permute-start.15 = (bf16[7,24,384]{2,1,0:T(8,128)(2,1)S(1)}, bf16[7,24,384]{2,1,0:T(8,128)(2,1)S(1)}, u32[]{:S(2)}, u32[]{:S(2)}) collective-permute-start(bf16[7,24,384]{2,1,0:T(8,128)(2,1)S(1)} %collective-permute-done.9.refs_11_), channel_id=1, source_target_pairs={{0,16},{2,18},{16,0},{18,2},{1,17},{3,19},{17,1},{19,3},{4,20},{6,... | collective-permute-start | bytes 387080 | tf_op jit(solution)/shard_map/ppermute | solution.py:218
  45.0 8.4 %collective-permute-start.12 = (bf16[7,24,384]{2,1,0:T(8,128)(2,1)S(1)}, bf16[7,24,384]{2,1,0:T(8,128)(2,1)S(1)}, u32[]{:S(2)}, u32[]{:S(2)}) collective-permute-start(bf16[7,24,384]{2,1,0:T(8,128)(2,1)S(1)} %collective-permute-done.9.refs_11_), channel_id=1, source_target_pairs={{0,2},{2,0},{16,18},{18,16},{1,3},{3,1},{17,19},{19,17},{4,6},{6,4... | collective-permute-start | bytes 387080 | tf_op jit(solution)/shard_map/ppermute | solution.py:218
  46.6 9.5 %collective-permute-start.4 = (bf16[28,24,128]{2,1,0:T(8,128)(2,1)S(1)}, bf16[28,24,128]{2,1,0:T(8,128)(2,1)S(1)}, u32[]{:S(2)}, u32[]{:S(2)}) collective-permute-start(bf16[28,24,128]{2,1,0:T(8,128)(2,1)S(1)} %collective-permute-done.refs_1_), channel_id=1, source_target_pairs={{0,2},{2,0},{1,3},{3,1},{4,6},{6,4},{5,7},{7,5},{8,10},{10,8},{9,1... | collective-permute-start | bytes 516104 | tf_op jit(solution)/shard_map/ppermute | solution.py:215
  47.4 11.1 %collective-permute-start.5 = (bf16[28,24,128]{2,1,0:T(8,128)(2,1)S(1)}, bf16[28,24,128]{2,1,0:T(8,128)(2,1)S(1)}, u32[]{:S(2)}, u32[]{:S(2)}) collective-permute-start(bf16[28,24,128]{2,1,0:T(8,128)(2,1)S(1)} %collective-permute-done.1.refs_2_), channel_id=1, source_target_pairs={{0,2},{2,0},{1,3},{3,1},{4,6},{6,4},{5,7},{7,5},{8,10},{10,8},{9,1... | collective-permute-start | bytes 516104 | tf_op jit(solution)/shard_map/ppermute | solution.py:215
  50.5 9.9 %collective-permute-start.6 = (bf16[28,24,128]{2,1,0:T(8,128)(2,1)S(1)}, bf16[28,24,128]{2,1,0:T(8,128)(2,1)S(1)}, u32[]{:S(2)}, u32[]{:S(2)}) collective-permute-start(bf16[28,24,128]{2,1,0:T(8,128)(2,1)S(1)} %collective-permute-done.2.refs_3_), channel_id=1, source_target_pairs={{0,2},{2,0},{1,3},{3,1},{4,6},{6,4},{5,7},{7,5},{8,10},{10,8},{9,1... | collective-permute-start | bytes 516104 | tf_op jit(solution)/shard_map/ppermute | solution.py:215

commit v2 on v1

v2 whole, which is shorter than its diff:
```python
import functools
import math

import jax
import jax.numpy as jnp
import numpy as np
from jax import lax
from jax.experimental import pallas as pl
from jax.experimental.pallas import tpu as pltpu
from jax.sharding import PartitionSpec as P

F32 = jnp.float32
BF16 = jnp.bfloat16


def twiddles(nlon, modes):
    phase = np.arange(nlon)[:, None] * np.arange(modes)[None, :] % nlon
    angle = phase * (2.0 * math.pi / nlon)
    scale = 1.0 / math.sqrt(nlon)
    return np.stack([np.cos(angle) * scale, -np.sin(angle) * scale]).astype(BF16)


def position(shift, k, sizes):
    owner = lax.rem(lax.axis_index("lat") + shift, sizes["lat"])
    return (owner * sizes["sub"] + lax.axis_index("sub")) * sizes["per"] + k


def owned_row(owner_ref, sizes, shifts):
    lane = lax.broadcasted_iota(jnp.int32, (1, 128), 1)
    row = jnp.full((1, 128), -1, jnp.int32)
    j = 0
    for shift in shifts:
        base = position(shift, 0, sizes)
        for k in range(sizes["per"]):
            row = jnp.where(lane == j, owner_ref[base + k], row)
            j += 1
    return row


def dft_kernel(sizes, step, owner_ref, table_ref, field_ref, *refs):
    *outs, grid_values, chosen, arrived = refs
    per = sizes["per"]
    rows, chans, nlon = grid_values.shape

    def part_copy(i):
        part = pl.ds(i * step, step)
        return pltpu.make_async_copy(field_ref.at[part], grid_values.at[part], arrived.at[i])

    for i in range(rows // step):
        part_copy(i).start()

    row = owned_row(owner_ref, sizes, range(sizes["lat"]))
    modes = table_ref.shape[2]
    pick = (lax.broadcasted_iota(jnp.int32, (modes, 128), 0) == row).astype(F32).astype(BF16)
    for r in range(2):
        chosen[:, r * 128 : (r + 1) * 128] = jnp.dot(
            table_ref[r], pick, preferred_element_type=F32
        ).astype(BF16)

    @pl.loop(0, rows // step)
    def _(i):
        part_copy(i).wait()
        values = grid_values[pl.ds(i * step, step)].reshape(step * chans, nlon).astype(BF16)
        spectrum = jnp.dot(values, chosen[...], preferred_element_type=F32)
        for t in range(step):
            part = spectrum[t * chans : (t + 1) * chans]
            turned = jnp.concatenate([part[:, :128], part[:, 128:]], axis=0).T
            for shift in range(sizes["lat"]):
                outs[shift][i * step + t] = turned[shift * per : (shift + 1) * per].astype(BF16)


def dft(field, ownership, sizes):
    lat_rows, chans, nlon = field.shape
    modes = ownership.shape[0]
    step = 4
    per = sizes["per"]
    table = jnp.asarray(twiddles(nlon, modes))
    vmem = pl.BlockSpec(memory_space=pltpu.VMEM)
    return pl.pallas_call(
        functools.partial(dft_kernel, sizes, step),
        in_specs=[
            pl.BlockSpec(memory_space=pltpu.SMEM),
            vmem,
            pl.BlockSpec(memory_space=pl.ANY),
        ],
        out_specs=[vmem] * sizes["lat"],
        out_shape=[jax.ShapeDtypeStruct((lat_rows, per, 128), BF16)] * sizes["lat"],
        scratch_shapes=[
            pltpu.VMEM(field.shape, F32),
            pltpu.VMEM((nlon, 256), BF16),
            pltpu.SemaphoreType.DMA((lat_rows // step,)),
        ],
        compiler_params=pltpu.CompilerParams(vmem_limit_bytes=52 << 20),
        cost_estimate=pl.CostEstimate(
            flops=2 * lat_rows * chans * nlon * 256, bytes_accessed=field.size * 4, transcendentals=0
        ),
        name="dft",
    )(ownership, table, field)


def pick_kernel(sizes, shifts, owner_ref, legendre_ref, *outs):
    per = sizes["per"]
    row = owned_row(owner_ref, sizes, shifts) - lax.axis_index("sub") * legendre_ref.shape[1]
    pick = (lax.broadcasted_iota(jnp.int32, (legendre_ref.shape[1], 128), 0) == row).astype(F32)
    pick = pick.T[: len(shifts) * per].astype(BF16)
    for t in range(legendre_ref.shape[0]):
        rows = jnp.dot(pick, legendre_ref[t], preferred_element_type=F32)
        for i in range(len(shifts)):
            outs[i][t] = rows[i * per : (i + 1) * per].astype(BF16)


def pick_rows(table, ownership, sizes, shifts, rows):
    _, slab, degrees = table.shape
    per = sizes["per"]
    return pl.pallas_call(
        functools.partial(pick_kernel, sizes, shifts),
        grid=(1,),
        in_specs=[
            pl.BlockSpec(memory_space=pltpu.SMEM),
            pl.BlockSpec(
                (rows, slab, degrees),
                lambda i: (lax.axis_index("rep") * sizes["ch"] + lax.axis_index("ch"), 0, 0),
            ),
        ],
        out_specs=[pl.BlockSpec((rows, per, degrees), lambda i: (0, 0, 0))] * len(shifts),
        out_shape=[jax.ShapeDtypeStruct((rows, per, degrees), BF16)] * len(shifts),
        compiler_params=pltpu.CompilerParams(vmem_limit_bytes=60 << 20),
        cost_estimate=pl.CostEstimate(
            flops=2 * rows * slab * degrees * per * len(shifts),
            bytes_accessed=rows * slab * degrees * 2,
            transcendentals=0,
        ),
        name="pick_rows",
    )(ownership, table)


def pack_kernel(*refs):
    *parts, out_ref = refs
    share = parts[0].shape[0]
    for i, part in enumerate(parts):
        out_ref[i * share : (i + 1) * share] = part[...]


def pack(parts):
    share, per, degrees = parts[0].shape
    return pl.pallas_call(
        pack_kernel,
        out_shape=jax.ShapeDtypeStruct((len(parts) * share, per, degrees), BF16),
        compiler_params=pltpu.CompilerParams(vmem_limit_bytes=16 << 20),
        name="pack",
    )(*parts)


def turn_kernel(sizes, owner_ref, legendre_ref, *refs):
    *shares, out_ref, table = refs
    per, lats, plane = sizes["per"], sizes["lat"], sizes["rep"] * sizes["ch"]
    lat_rows, slab, degrees = legendre_ref.shape
    deep = out_ref.shape[1] // lats
    share = lat_rows // plane
    tiles = degrees // 128
    for s in range(lats):
        end = (s * deep + lat_rows) * per
        table[:, end : (s + 1) * deep * per, :] = jnp.zeros((tiles, (deep - lat_rows) * per, 128), F32)
    row = owned_row(owner_ref, sizes, (0,)) - lax.axis_index("sub") * slab
    pick = (lax.broadcasted_iota(jnp.int32, (slab, 128), 0) == row).astype(F32)
    pick = pick.T[:per].astype(BF16)
    for t in range(lat_rows):
        rows = jnp.dot(pick, legendre_ref[t], preferred_element_type=F32)
        for i in range(tiles):
            table[i, t * per : (t + 1) * per, :] = rows[:, i * 128 : (i + 1) * 128]
    block = share * per
    q = lax.axis_index("rep") * sizes["ch"] + lax.axis_index("ch")
    for s in range(1, lats):
        for d in range(plane):
            values = shares[d][(s - 1) * share : s * share].astype(F32).reshape(block, degrees)
            at = pl.multiple_of((s * deep + jnp.bitwise_xor(q, d) * share) * per, 8)
            for i in range(tiles):
                table[i, pl.ds(at, block), :] = values[:, i * 128 : (i + 1) * 128]
    for k in range(per):
        for i in range(tiles):
            out_ref[k, :, i * 128 : (i + 1) * 128] = table[
                i, pl.ds(k, lats * deep, stride=per), :
            ].astype(BF16)


def turn(by_latitude, ownership, shares, deep, sizes):
    lat_rows, _, degrees = by_latitude.shape
    per, depth = sizes["per"], sizes["lat"] * deep
    vmem = pl.BlockSpec(memory_space=pltpu.VMEM)
    return pl.pallas_call(
        functools.partial(turn_kernel, sizes),
        in_specs=[pl.BlockSpec(memory_space=pltpu.SMEM)] + [vmem] * (1 + len(shares)),
        out_specs=vmem,
        out_shape=jax.ShapeDtypeStruct((per, depth, degrees), BF16),
        scratch_shapes=[pltpu.VMEM((degrees // 128, depth * per, 128), F32)],
        compiler_params=pltpu.CompilerParams(vmem_limit_bytes=32 << 20),
        name="turn",
    )(ownership, by_latitude, *shares)


def mix_kernel(near_ref, far_ref, w_near, w_far, out_ref, spectra):
    lat_rows, per, width = near_ref.shape
    deep = out_ref.shape[1]
    nt = (((1,), (1,)), ((), ()))
    a = near_ref[...].reshape(lat_rows * per, width)
    b = far_ref[...].reshape(lat_rows * per, width)
    mixed = lax.dot_general(a, w_near[...], nt, preferred_element_type=F32)
    mixed += lax.dot_general(b, w_far[...], nt, preferred_element_type=F32)
    spectra[: lat_rows * per, :] = mixed
    spectra[lat_rows * per :, :] = jnp.zeros(((deep - lat_rows) * per, width), F32)
    for k in range(per):
        out_ref[k] = spectra[pl.ds(k, deep, stride=per), :].astype(BF16)


def mix(near, far, w_near, w_far, deep):
    lat_rows, per, width = near.shape
    return pl.pallas_call(
        mix_kernel,
        out_shape=jax.ShapeDtypeStruct((per, deep, width), BF16),
        scratch_shapes=[pltpu.VMEM((deep * per, width), F32)],
        compiler_params=pltpu.CompilerParams(vmem_limit_bytes=16 << 20),
        cost_estimate=pl.CostEstimate(
            flops=100 * 2 * near.size * width, bytes_accessed=near.size * 4, transcendentals=0
        ),
        name="mix",
    )(near, far, w_near, w_far)


def contract_kernel(group, *refs):
    *spectra, table, out_ref = refs
    half = out_ref.shape[2]
    for k in range(group):
        a = jnp.concatenate([part[k] for part in spectra], axis=0)
        c = lax.dot_general(a, table[k], (((0,), (0,)), ((), ())), preferred_element_type=F32)
        out_ref[0, k] = c[:half].astype(BF16)
        out_ref[1, k] = c[half:].astype(BF16)


def contract(spectra, table):
    per, deep, width = spectra[0].shape
    _, depth, degrees = table.shape
    group = 8
    block = lambda x: pl.BlockSpec((group, *x.shape[1:]), lambda i: (i, 0, 0))
    return pl.pallas_call(
        functools.partial(contract_kernel, group),
        grid=(per // group,),
        in_specs=[block(x) for x in (*spectra, table)],
        out_specs=pl.BlockSpec((2, group, width // 2, degrees), lambda i: (0, i, 0, 0)),
        out_shape=jax.ShapeDtypeStruct((2, per, width // 2, degrees), BF16),
        compiler_params=pltpu.CompilerParams(vmem_limit_bytes=40 << 20),
        name="contract",
    )(*spectra, table)


def mixing_weights(w_real, w_imag):
    half = w_real.shape[0]
    x = lax.axis_index("ch")
    out = []
    for side in (x, 1 - x):
        wr = lax.dynamic_slice_in_dim(w_real, side * half, half, 1)
        wi = lax.dynamic_slice_in_dim(w_imag, side * half, half, 1)
        out.append(
            jnp.concatenate(
                [jnp.concatenate([wr, -wi], axis=1), jnp.concatenate([wi, wr], axis=1)], axis=0
            )
        )
    return out


def fast(field, legendre, ownership, w_real, w_imag, sizes):
    lats, plane = sizes["lat"], sizes["rep"] * sizes["ch"]
    lat_rows = field.shape[0]
    by_latitude = jnp.transpose(legendre, (1, 0, 2))
    along = lambda s: [(i, (i + s) % lats) for i in range(lats)]
    swap = [(0, 1), (1, 0)]
    others = tuple(range(1, lats))
    sent = pick_rows(by_latitude, ownership, sizes, others, lat_rows // plane)
    landed = [lax.ppermute(sent[s - 1], "lat", along(s)) for s in others]
    after_sent, _ = lax.optimization_barrier((ownership, sent[0]))
    spectra = dft(field, after_sent, sizes)
    landed, starts = lax.optimization_barrier((landed, spectra[1:]))
    near = [spectra[0]] + [lax.ppermute(v, "lat", along(s)) for s, v in zip(others, starts)]
    far = [lax.ppermute(v, "ch", swap) for v in near]
    mine = pack(landed)
    beside = lax.ppermute(mine, "ch", swap)
    shares = [mine, beside, lax.ppermute(mine, "rep", swap), lax.ppermute(beside, "rep", swap)]
    deep = (lat_rows + 15) // 16 * 16
    table = turn(by_latitude, ownership, shares, deep, sizes)
    w_near, w_far = mixing_weights(w_real, w_imag)
    mixed = [mix(n, f, w_near, w_far, deep) for n, f in zip(near, far)]
    return contract(mixed, table)


def fourier_rows(flat_field, modes, lat_rows, chans, nlon):
    longitude = jnp.arange(nlon, dtype=jnp.int32)
    phase = longitude[:, None] * modes[None, :] % nlon
    angle = phase.astype(jnp.float32) * (2.0 * math.pi / nlon)
    scale = 1.0 / math.sqrt(nlon)
    real_part = (
        jnp.dot(
            flat_field,
            jnp.cos(angle),
            precision=lax.Precision.HIGHEST,
            preferred_element_type=jnp.float32,
        )
        * scale
    )
    imag_part = (
        -jnp.dot(
            flat_field,
            jnp.sin(angle),
            precision=lax.Precision.HIGHEST,
            preferred_element_type=jnp.float32,
        )
        * scale
    )
    both = jnp.stack([real_part, imag_part]).reshape(2, lat_rows, chans, modes.shape[0])
    both = jnp.transpose(both, (3, 1, 0, 2)).reshape(modes.shape[0], lat_rows, 2 * chans)
    return both.astype(jnp.bfloat16)


def general(field, legendre, ownership, w_real, w_imag):
    lat_rows, chans, nlon = field.shape
    degrees = legendre.shape[2]
    slab_modes = legendre.shape[0]
    blocks = lax.axis_size("lat")
    halves = lax.axis_size("sub")
    per_block = ownership.shape[0] // (blocks * halves)
    my_modes = lax.dynamic_index_in_dim(
        ownership.reshape(blocks, halves, per_block), lax.axis_index("sub"), 1, keepdims=False
    ).reshape(blocks * per_block)
    slab_index = my_modes - lax.axis_index("sub") * slab_modes
    flat_field = field.reshape(lat_rows * chans, nlon)
    spectra_rows = fourier_rows(flat_field, my_modes, lat_rows, chans, nlon)
    table_rows = jnp.take(legendre, slab_index, axis=0)
    spectra_all, tables_all = (
        lax.all_to_all(spectra_rows, "lat", split_axis=0, concat_axis=1, tiled=True),
        lax.all_to_all(table_rows, "lat", split_axis=0, concat_axis=1, tiled=True),
    )
    spectra_all = spectra_all.reshape(per_block, blocks, lat_rows, 2 * chans)
    tables_all = tables_all.reshape(per_block, blocks, lat_rows, degrees)
    block_part = jnp.einsum(
        "kbtc,kbtl->kbcl", spectra_all, tables_all, preferred_element_type=jnp.float32
    )
    total = jnp.sum(block_part, axis=1)
    coeff = total.astype(jnp.bfloat16).reshape(per_block, 2, chans, degrees)
    piece = lax.all_gather(coeff, "ch", axis=2, tiled=True)
    real_in = piece[:, 0]
    imag_in = piece[:, 1]
    real_out = jnp.einsum(
        "oc,kcl->kol", w_real, real_in, preferred_element_type=jnp.float32
    ) - jnp.einsum("oc,kcl->kol", w_imag, imag_in, preferred_element_type=jnp.float32)
    imag_out = jnp.einsum(
        "oc,kcl->kol", w_real, imag_in, preferred_element_type=jnp.float32
    ) + jnp.einsum("oc,kcl->kol", w_imag, real_in, preferred_element_type=jnp.float32)
    mixed = jnp.stack([real_out, imag_out])
    return mixed.astype(jnp.bfloat16)


def per_device(sizes, field, legendre, ownership, w_real, w_imag):
    lat_rows, chans, nlon = field.shape
    sizes = dict(sizes, per=ownership.shape[0] // (sizes["lat"] * sizes["sub"]))
    plane = sizes["rep"] * sizes["ch"]
    fits = (
        sizes["ch"] == 2
        and sizes["rep"] == 2
        and 2 * chans == 128
        and lat_rows % plane == 0
        and lat_rows % 4 == 0
        and sizes["per"] % 8 == 0
        and sizes["lat"] * sizes["per"] <= 128
        and legendre.shape[2] % 128 == 0
    )
    if fits:
        return fast(field, legendre, ownership, w_real, w_imag, sizes)
    return general(field, legendre, ownership, w_real, w_imag)


def solution(mesh):
    in_specs = (
        P(("rep", "lat"), "ch", None),
        P("sub", "lat", None),
        P(),
        P("ch", None),
        P("ch", None),
    )
    out_specs = P("rep", ("lat", "sub"), "ch", None)
    return jax.shard_map(
        functools.partial(per_device, dict(mesh.shape)),
        mesh=mesh,
        in_specs=in_specs,
        out_specs=out_specs,
        check_vma=False,
    )
```

time: 65.5 us -> 51.1 us (0.78)
  the two profiles are of different devices: /device:TPU:0 before, /device:TPU:26 now
where the time goes in v2:
time: 51.1 us; the launch traced here: 51 us
  waiting for transfers between devices  19.6 us (38%)
  starting transfers between devices  15.8 us (31%)
  Pallas kernels  14.5 us (28%)
  local copies, waits for them, and re-layouts  0.7 us (1%)
    ppermute x3, waiting for transfers between devices, fast(): lax.ppermute(v, 'lat', along(s))  11.9 us
    pallas_call x1, Pallas kernels, dft(): pl.pallas_call(functools.partial(dft_kernel, sizes, step), in_specs=[pl.B...  6.18 us
    ppermute x4, waiting for transfers between devices, fast(): far = [lax.ppermute(v, 'ch', swap) for v in near]  4.92 us
    ppermute x3, starting transfers between devices, fast(): lax.ppermute(v, 'lat', along(s))  4.23 us
    ppermute x3, starting transfers between devices, fast(): landed = [lax.ppermute(sent[s - 1], 'lat', along(s)) for s in others]  4.17 us
    ppermute x4, starting transfers between devices, fast(): far = [lax.ppermute(v, 'ch', swap) for v in near]  3.43 us
    pallas_call x1, Pallas kernels, contract(): pl.pallas_call(functools.partial(contract_kernel, group), grid=(per // gr...  2.59 us
    ppermute x1, waiting for transfers between devices, fast(): lax.ppermute(beside, 'rep', swap)  2.46 us
  transfers between devices with their start and end apart: 13, of which 7 were waited for; matrix products, arithmetic and copies ran while one was open for 1% of the time, Pallas kernels for 14%

profile of v2, /device:TPU:26, one launch (start us, length us, event | category | flops | bytes accessed | tf_op | source)
XLA Modules:
  0.0 51.0 jit_solution(8183611984225732184)
XLA Ops:
  0.0 2.2 %pick_rows.1 = (bf16[7,24,384]{2,1,0:T(8,128)(2,1)}, bf16[7,24,384]{2,1,0:T(8,128)(2,1)}, bf16[7,24,384]{2,1,0:T(8,128)(2,1)}) custom-call(s32[192]{0:T(256)} %owner_ref.4, bf16[28,96,384]{2,1,0:T(8,128)(2,1)} %bitcast.1), custom_call_target="tpu_custom_call" | custom-call | flops 37158912 | bytes 516096 | tf_op jit(solution)/shard_map/pick_rows/pallas_call | solution.py:115
  2.2 0.3 collective-permute-start.2
  2.5 0.4 collective-permute-start.3
  3.0 3.4 %collective-permute-start.1 = (bf16[7,24,384]{2,1,0:T(8,128)(2,1)}, bf16[7,24,384]{2,1,0:T(8,128)(2,1)S(1)}, u32[]{:S(2)}, u32[]{:S(2)}) collective-permute-start(bf16[7,24,384]{2,1,0:T(8,128)(2,1)} %get-tuple-element.19), channel_id=1, source_target_pairs={{0,4},{4,8},{8,12},{12,0},{1,5},{5,9},{9,13},{13,1},{2,6},{6,10},{... | collective-permute-start | bytes 387080 | tf_op jit(solution)/shard_map/ppermute | solution.py:278
  6.4 0.0 copy-start.1
  6.4 0.7 %copy-done.1 = s32[192]{0:T(256)S(1)} copy-done((s32[192]{0:T(256)S(1)}, s32[192]{0:T(256)}, u32[]{:S(2)}) %copy-start.1) | copy-done | bytes 792
  7.0 0.0 copy-start.3
  7.0 0.0 copy-start.4
  7.0 6.2 %dft.1 = (bf16[28,24,128]{2,1,0:T(8,128)(2,1)S(1)}, bf16[28,24,128]{2,1,0:T(8,128)(2,1)S(1)}, bf16[28,24,128]{2,1,0:T(8,128)(2,1)S(1)}, bf16[28,24,128]{2,1,0:T(8,128)(2,1)S(1)}) custom-call(s32[192]{0:T(256)S(1)} %copy-done.1, bf16[2,1440,192]{2,1,0:T(8,128)(2,1)} %constant.14.clone.table_ref, f32[28,64,1440]{2,1,0:T(8,128)} %field_ref.1), custom_call_target="tpu_custom_call" | custom-call | flops 1321205760 | bytes 10321920 | tf_op jit(solution)/shard_map/dft/pallas_call | solution.py:79
  13.2 0.6 %collective-permute-start = (bf16[28,24,128]{2,1,0:T(8,128)(2,1)S(1)}, bf16[28,24,128]{2,1,0:T(8,128)(2,1)S(1)}, u32[]{:S(2)}, u32[]{:S(2)}) collective-permute-start(bf16[28,24,128]{2,1,0:T(8,128)(2,1)S(1)} %get-tuple-element.21.near_ref), channel_id=1, source_target_pairs={{0,2},{2,0},{1,3},{3,1},{4,6},{6,4},{5,7},{7,5},{8,10},{10,8},{9,1... | collective-permute-start | bytes 516104 | tf_op jit(solution)/shard_map/ppermute | solution.py:283
  13.8 0.0 copy-done.3
  13.8 0.0 copy-done.4
  13.8 0.1 constant_dynamic-slice_fusion.1
  13.9 0.1 collective-permute-done.2.refs_1_
  14.1 0.0 collective-permute-done.3.refs_2_
  14.1 0.2 collective-permute-done.1.refs_0_
  14.3 1.1 %collective-permute-start.4 = (bf16[28,24,128]{2,1,0:T(8,128)(2,1)S(1)}, bf16[28,24,128]{2,1,0:T(8,128)(2,1)S(1)}, u32[]{:S(2)}, u32[]{:S(2)}) collective-permute-start(bf16[28,24,128]{2,1,0:T(8,128)(2,1)S(1)} %get-tuple-element.27), channel_id=1, source_target_pairs={{0,4},{4,8},{8,12},{12,0},{1,5},{5,9},{9,13},{13,1},{2,6},{6,10},{... | collective-permute-start | bytes 516104 | tf_op jit(solution)/shard_map/ppermute | solution.py:282
  15.4 0.1 maximum_maximum_fusion.1.w_far
  15.5 0.1 maximum_maximum_fusion.w_near
  15.6 1.6 %collective-permute-start.11 = (bf16[21,24,384]{2,1,0:T(8,128)(2,1)S(1)}, bf16[21,24,384]{2,1,0:T(8,128)(2,1)S(1)}, u32[]{:S(2)}, u32[]{:S(2)}) collective-permute-start(bf16[21,24,384]{2,1,0:T(8,128)(2,1)S(1)} %pack.1.refs_0_), channel_id=1, source_target_pairs={{0,16},{16,0},{1,17},{17,1},{2,18},{18,2},{3,19},{19,3},{4,20},{20... | collective-permute-start | bytes 1161224 | tf_op jit(solution)/shard_map/ppermute | solution.py:286
  17.2 0.8 %collective-permute-start.10 = (bf16[21,24,384]{2,1,0:T(8,128)(2,1)S(1)}, bf16[21,24,384]{2,1,0:T(8,128)(2,1)S(1)}, u32[]{:S(2)}, u32[]{:S(2)}) collective-permute-start(bf16[21,24,384]{2,1,0:T(8,128)(2,1)S(1)} %pack.1.refs_0_), channel_id=1, source_target_pairs={{0,2},{2,0},{1,3},{3,1},{4,6},{6,4},{5,7},{7,5},{8,10},{10,8},{9,1... | collective-permute-start | bytes 1161224 | tf_op jit(solution)/shard_map/ppermute | solution.py:285
  18.0 3.1 %collective-permute-start.6 = (bf16[28,24,128]{2,1,0:T(8,128)(2,1)S(1)}, bf16[28,24,128]{2,1,0:T(8,128)(2,1)S(1)}, u32[]{:S(2)}, u32[]{:S(2)}) collective-permute-start(bf16[28,24,128]{2,1,0:T(8,128)(2,1)S(1)} %get-tuple-element.28), channel_id=1, source_target_pairs={{0,8},{4,12},{8,0},{12,4},{1,9},{5,13},{9,1},{13,5},{2,10},{6,14},... | collective-permute-start | bytes 516104 | tf_op jit(solution)/shard_map/ppermute | solution.py:282
  21.1 0.0 collective-permute-done.far_ref
  21.1 0.0 collective-permute-start.8
  21.1 0.7 %collective-permute-done.4.near_ref = bf16[28,24,128]{2,1,0:T(8,128)(2,1)S(1)} collective-permute-done((bf16[28,24,128]{2,1,0:T(8,128)(2,1)S(1)}, bf16[28,24,128]{2,1,0:T(8,128)(2,1)S(1)}, u32[]{:S(2)}, u32[]{:S(2)}) %collective-permute-start.4) | collective-permute-done | bytes 172064 | tf_op jit(solution)/shard_map/ppermute | solution.py:282
  21.8 0.8 %collective-permute-start.5 = (bf16[28,24,128]{2,1,0:T(8,128)(2,1)S(1)}, bf16[28,24,128]{2,1,0:T(8,128)(2,1)S(1)}, u32[]{:S(2)}, u32[]{:S(2)}) collective-permute-start(bf16[28,24,128]{2,1,0:T(8,128)(2,1)S(1)} %collective-permute-done.4.near_ref), channel_id=1, source_target_pairs={{0,2},{2,0},{1,3},{3,1},{4,6},{6,4},{5,7},{7,5},{8,10},{10,8},{9,1... | collective-permute-start | bytes 516104 | tf_op jit(solution)/shard_map/ppermute | solution.py:283
  22.7 0.3 mix.4.refs_0_
  22.9 11.1 %collective-permute-done.6.near_ref = bf16[28,24,128]{2,1,0:T(8,128)(2,1)S(1)} collective-permute-done((bf16[28,24,128]{2,1,0:T(8,128)(2,1)S(1)}, bf16[28,24,128]{2,1,0:T(8,128)(2,1)S(1)}, u32[]{:S(2)}, u32[]{:S(2)}) %collective-permute-start.6) | collective-permute-done | bytes 172064 | tf_op jit(solution)/shard_map/ppermute | solution.py:282
  34.1 0.6 %collective-permute-start.7 = (bf16[28,24,128]{2,1,0:T(8,128)(2,1)S(1)}, bf16[28,24,128]{2,1,0:T(8,128)(2,1)S(1)}, u32[]{:S(2)}, u32[]{:S(2)}) collective-permute-start(bf16[28,24,128]{2,1,0:T(8,128)(2,1)S(1)} %collective-permute-done.6.near_ref), channel_id=1, source_target_pairs={{0,2},{2,0},{1,3},{3,1},{4,6},{6,4},{5,7},{7,5},{8,10},{10,8},{9,1... | collective-permute-start | bytes 516104 | tf_op jit(solution)/shard_map/ppermute | solution.py:283
  34.6 0.0 collective-permute-done.8.near_ref
  34.7 1.5 %collective-permute-start.9 = (bf16[28,24,128]{2,1,0:T(8,128)(2,1)S(1)}, bf16[28,24,128]{2,1,0:T(8,128)(2,1)S(1)}, u32[]{:S(2)}, u32[]{:S(2)}) collective-permute-start(bf16[28,24,128]{2,1,0:T(8,128)(2,1)S(1)} %collective-permute-done.8.near_ref), channel_id=1, source_target_pairs={{0,2},{2,0},{1,3},{3,1},{4,6},{6,4},{5,7},{7,5},{8,10},{10,8},{9,1... | collective-permute-start | bytes 516104 | tf_op jit(solution)/shard_map/ppermute | solution.py:283
  36.1 0.0 collective-permute-done.5.far_ref
  36.1 0.3 mix.5.refs_1_
  36.4 0.0 collective-permute-done.10.refs_1_
  36.4 1.6 %collective-permute-start.12 = (bf16[21,24,384]{2,1,0:T(8,128)(2,1)S(1)}, bf16[21,24,384]{2,1,0:T(8,128)(2,1)S(1)}, u32[]{:S(2)}, u32[]{:S(2)}) collective-permute-start(bf16[21,24,384]{2,1,0:T(8,128)(2,1)S(1)} %collective-permute-done.10.refs_1_), channel_id=1, source_target_pairs={{0,16},{16,0},{1,17},{17,1},{2,18},{18,2},{3,19},{19,3},{4,20},{20... | collective-permute-start | bytes 1161224 | tf_op jit(solution)/shard_map/ppermute | solution.py:286
  38.0 3.4 %collective-permute-done.7.far_ref = bf16[28,24,128]{2,1,0:T(8,128)(2,1)S(1)} collective-permute-done((bf16[28,24,128]{2,1,0:T(8,128)(2,1)S(1)}, bf16[28,24,128]{2,1,0:T(8,128)(2,1)S(1)}, u32[]{:S(2)}, u32[]{:S(2)}) %collective-permute-start.7) | collective-permute-done | bytes 172064 | tf_op jit(solution)/shard_map/ppermute | solution.py:283
  41.4 0.3 mix.6.refs_2_
  41.7 0.0 copy-start
  41.7 0.0 copy-start.2
  41.7 1.5 %collective-permute-done.9.far_ref = bf16[28,24,128]{2,1,0:T(8,128)(2,1)S(1)} collective-permute-done((bf16[28,24,128]{2,1,0:T(8,128)(2,1)S(1)}, bf16[28,24,128]{2,1,0:T(8,128)(2,1)S(1)}, u32[]{:S(2)}, u32[]{:S(2)}) %collective-permute-start.9) | collective-permute-done | bytes 172064 | tf_op jit(solution)/shard_map/ppermute | solution.py:283
  43.2 0.3 mix.7.refs_3_
  43.5 0.0 collective-permute-done.11.refs_2_
  43.5 2.5 %collective-permute-done.12.refs_3_ = bf16[21,24,384]{2,1,0:T(8,128)(2,1)S(1)} collective-permute-done((bf16[21,24,384]{2,1,0:T(8,128)(2,1)S(1)}, bf16[21,24,384]{2,1,0:T(8,128)(2,1)S(1)}, u32[]{:S(2)}, u32[]{:S(2)}) %collective-permute-start.12) | collective-permute-done | bytes 387104 | tf_op jit(solution)/shard_map/ppermute | solution.py:286
  46.0 0.0 copy-done
  46.0 0.0 copy-done.2
  46.0 2.4 %turn.1.refs_4_ = bf16[24,128,384]{2,1,0:T(8,128)(2,1)S(1)} custom-call(s32[192]{0:T(256)S(1)} %copy-done.2, bf16[28,96,384]{2,1,0:T(8,128)(2,1)S(1)} %bitcast.2, bf16[21,24,384]{2,1,0:T(8,128)(2,1)S(1)} %pack.1.refs_0_, bf16[21,24,384]{2,1,0:T(8,128)(2,1)S(1)} %collective-permute-done.10.refs_1_, bf16[21,24,384]{2,1,0:T(8,128)(2,1)S(1)} %collective-permute-done.11.refs_2_, ...), custom_call_target="tpu_custom_call" | custom-call | tf_op jit(solution)/shard_map/turn/pallas_call | solution.py:190
  48.4 2.6 %contract.1 = bf16[2,24,64,384]{3,2,1,0:T(8,128)(2,1)} custom-call(bf16[24,32,128]{2,1,0:T(8,128)(2,1)S(1)} %mix.4.refs_0_, bf16[24,32,128]{2,1,0:T(8,128)(2,1)S(1)} %mix.5.refs_1_, bf16[24,32,128]{2,1,0:T(8,128)(2,1)S(1)} %mix.6.refs_2_, bf16[24,32,128]{2,1,0:T(8,128)(2,1)S(1)} %mix.7.refs_3_, bf16[24,128,384]{2,1,0:T(8,128)(2,1)S(1)} %turn.1.refs_4_), custom_call_target="tpu_custom_call" | custom-call | tf_op jit(solution)/shard_map/contract/pallas_call | solution.py:244
  (1 shorter events, 0.0 us)
Async XLA Ops:
  2.2 11.9 %collective-permute-start.2 = (bf16[7,24,384]{2,1,0:T(8,128)(2,1)}, bf16[7,24,384]{2,1,0:T(8,128)(2,1)S(1)}, u32[]{:S(2)}, u32[]{:S(2)}) collective-permute-start(bf16[7,24,384]{2,1,0:T(8,128)(2,1)} %get-tuple-element.22), channel_id=1, source_target_pairs={{0,8},{4,12},{8,0},{12,4},{1,9},{5,13},{9,1},{13,5},{2,10},{6,14},... | collective-permute-start | bytes 387080 | tf_op jit(solution)/shard_map/ppermute | solution.py:278
  2.5 11.5 %collective-permute-start.3 = (bf16[7,24,384]{2,1,0:T(8,128)(2,1)}, bf16[7,24,384]{2,1,0:T(8,128)(2,1)S(1)}, u32[]{:S(2)}, u32[]{:S(2)}) collective-permute-start(bf16[7,24,384]{2,1,0:T(8,128)(2,1)} %get-tuple-element.23), channel_id=1, source_target_pairs={{0,12},{4,0},{8,4},{12,8},{1,13},{5,1},{9,5},{13,9},{2,14},{6,2},{... | collective-permute-start | bytes 387080 | tf_op jit(solution)/shard_map/ppermute | solution.py:278
  3.0 11.3 %collective-permute-start.1 = (bf16[7,24,384]{2,1,0:T(8,128)(2,1)}, bf16[7,24,384]{2,1,0:T(8,128)(2,1)S(1)}, u32[]{:S(2)}, u32[]{:S(2)}) collective-permute-start(bf16[7,24,384]{2,1,0:T(8,128)(2,1)} %get-tuple-element.19), channel_id=1, source_target_pairs={{0,4},{4,8},{8,12},{12,0},{1,5},{5,9},{9,13},{13,1},{2,6},{6,10},{... | collective-permute-start | bytes 387080 | tf_op jit(solution)/shard_map/ppermute | solution.py:278
  6.4 0.7 %copy-start.1 = (s32[192]{0:T(256)S(1)}, s32[192]{0:T(256)}, u32[]{:S(2)}) copy-start(s32[192]{0:T(256)} %owner_ref.4) | copy-start | bytes 2308
  7.0 6.8 %copy-start.3 = (bf16[64,128]{1,0:T(8,128)(2,1)S(1)}, bf16[64,128]{1,0:T(8,128)(2,1)}, u32[]{:S(2)}) copy-start(bf16[64,128]{1,0:T(8,128)(2,1)} %param.9) | copy-start | bytes 49156
  7.0 6.8 %copy-start.4 = (bf16[64,128]{1,0:T(8,128)(2,1)S(1)}, bf16[64,128]{1,0:T(8,128)(2,1)}, u32[]{:S(2)}) copy-start(bf16[64,128]{1,0:T(8,128)(2,1)} %param.10) | copy-start | bytes 49156
  13.2 7.9 %collective-permute-start = (bf16[28,24,128]{2,1,0:T(8,128)(2,1)S(1)}, bf16[28,24,128]{2,1,0:T(8,128)(2,1)S(1)}, u32[]{:S(2)}, u32[]{:S(2)}) collective-permute-start(bf16[28,24,128]{2,1,0:T(8,128)(2,1)S(1)} %get-tuple-element.21.near_ref), channel_id=1, source_target_pairs={{0,2},{2,0},{1,3},{3,1},{4,6},{6,4},{5,7},{7,5},{8,10},{10,8},{9,1... | collective-permute-start | bytes 516104 | tf_op jit(solution)/shard_map/ppermute | solution.py:283
  14.3 7.6 %collective-permute-start.4 = (bf16[28,24,128]{2,1,0:T(8,128)(2,1)S(1)}, bf16[28,24,128]{2,1,0:T(8,128)(2,1)S(1)}, u32[]{:S(2)}, u32[]{:S(2)}) collective-permute-start(bf16[28,24,128]{2,1,0:T(8,128)(2,1)S(1)} %get-tuple-element.27), channel_id=1, source_target_pairs={{0,4},{4,8},{8,12},{12,0},{1,5},{5,9},{9,13},{13,1},{2,6},{6,10},{... | collective-permute-start | bytes 516104 | tf_op jit(solution)/shard_map/ppermute | solution.py:282
  15.6 27.9 %collective-permute-start.11 = (bf16[21,24,384]{2,1,0:T(8,128)(2,1)S(1)}, bf16[21,24,384]{2,1,0:T(8,128)(2,1)S(1)}, u32[]{:S(2)}, u32[]{:S(2)}) collective-permute-start(bf16[21,24,384]{2,1,0:T(8,128)(2,1)S(1)} %pack.1.refs_0_), channel_id=1, source_target_pairs={{0,16},{16,0},{1,17},{17,1},{2,18},{18,2},{3,19},{19,3},{4,20},{20... | collective-permute-start | bytes 1161224 | tf_op jit(solution)/shard_map/ppermute | solution.py:286
  17.2 19.2 %collective-permute-start.10 = (bf16[21,24,384]{2,1,0:T(8,128)(2,1)S(1)}, bf16[21,24,384]{2,1,0:T(8,128)(2,1)S(1)}, u32[]{:S(2)}, u32[]{:S(2)}) collective-permute-start(bf16[21,24,384]{2,1,0:T(8,128)(2,1)S(1)} %pack.1.refs_0_), channel_id=1, source_target_pairs={{0,2},{2,0},{1,3},{3,1},{4,6},{6,4},{5,7},{7,5},{8,10},{10,8},{9,1... | collective-permute-start | bytes 1161224 | tf_op jit(solution)/shard_map/ppermute | solution.py:285
  18.0 16.1 %collective-permute-start.6 = (bf16[28,24,128]{2,1,0:T(8,128)(2,1)S(1)}, bf16[28,24,128]{2,1,0:T(8,128)(2,1)S(1)}, u32[]{:S(2)}, u32[]{:S(2)}) collective-permute-start(bf16[28,24,128]{2,1,0:T(8,128)(2,1)S(1)} %get-tuple-element.28), channel_id=1, source_target_pairs={{0,8},{4,12},{8,0},{12,4},{1,9},{5,13},{9,1},{13,5},{2,10},{6,14},... | collective-permute-start | bytes 516104 | tf_op jit(solution)/shard_map/ppermute | solution.py:282
  21.1 13.6 %collective-permute-start.8 = (bf16[28,24,128]{2,1,0:T(8,128)(2,1)S(1)}, bf16[28,24,128]{2,1,0:T(8,128)(2,1)S(1)}, u32[]{:S(2)}, u32[]{:S(2)}) collective-permute-start(bf16[28,24,128]{2,1,0:T(8,128)(2,1)S(1)} %get-tuple-element.29), channel_id=1, source_target_pairs={{0,12},{4,0},{8,4},{12,8},{1,13},{5,1},{9,5},{13,9},{2,14},{6,2},{... | collective-permute-start | bytes 516104 | tf_op jit(solution)/shard_map/ppermute | solution.py:282
  21.8 14.3 %collective-permute-start.5 = (bf16[28,24,128]{2,1,0:T(8,128)(2,1)S(1)}, bf16[28,24,128]{2,1,0:T(8,128)(2,1)S(1)}, u32[]{:S(2)}, u32[]{:S(2)}) collective-permute-start(bf16[28,24,128]{2,1,0:T(8,128)(2,1)S(1)} %collective-permute-done.4.near_ref), channel_id=1, source_target_pairs={{0,2},{2,0},{1,3},{3,1},{4,6},{6,4},{5,7},{7,5},{8,10},{10,8},{9,1... | collective-permute-start | bytes 516104 | tf_op jit(solution)/shard_map/ppermute | solution.py:283
  34.1 7.3 %collective-permute-start.7 = (bf16[28,24,128]{2,1,0:T(8,128)(2,1)S(1)}, bf16[28,24,128]{2,1,0:T(8,128)(2,1)S(1)}, u32[]{:S(2)}, u32[]{:S(2)}) collective-permute-start(bf16[28,24,128]{2,1,0:T(8,128)(2,1)S(1)} %collective-permute-done.6.near_ref), channel_id=1, source_target_pairs={{0,2},{2,0},{1,3},{3,1},{4,6},{6,4},{5,7},{7,5},{8,10},{10,8},{9,1... | collective-permute-start | bytes 516104 | tf_op jit(solution)/shard_map/ppermute | solution.py:283
  34.7 8.6 %collective-permute-start.9 = (bf16[28,24,128]{2,1,0:T(8,128)(2,1)S(1)}, bf16[28,24,128]{2,1,0:T(8,128)(2,1)S(1)}, u32[]{:S(2)}, u32[]{:S(2)}) collective-permute-start(bf16[28,24,128]{2,1,0:T(8,128)(2,1)S(1)} %collective-permute-done.8.near_ref), channel_id=1, source_target_pairs={{0,2},{2,0},{1,3},{3,1},{4,6},{6,4},{5,7},{7,5},{8,10},{10,8},{9,1... | collective-permute-start | bytes 516104 | tf_op jit(solution)/shard_map/ppermute | solution.py:283
  36.4 9.6 %collective-permute-start.12 = (bf16[21,24,384]{2,1,0:T(8,128)(2,1)S(1)}, bf16[21,24,384]{2,1,0:T(8,128)(2,1)S(1)}, u32[]{:S(2)}, u32[]{:S(2)}) collective-permute-start(bf16[21,24,384]{2,1,0:T(8,128)(2,1)S(1)} %collective-permute-done.10.refs_1_), channel_id=1, source_target_pairs={{0,16},{16,0},{1,17},{17,1},{2,18},{18,2},{3,19},{19,3},{4,20},{20... | collective-permute-start | bytes 1161224 | tf_op jit(solution)/shard_map/ppermute | solution.py:286
  41.7 4.3 %copy-start = (bf16[96,28,384]{2,0,1:T(8,128)(2,1)S(1)}, bf16[96,28,384]{2,0,1:T(8,128)(2,1)}, u32[]{:S(2)}) copy-start(bf16[96,28,384]{2,0,1:T(8,128)(2,1)} %param.7) | copy-start | bytes 6193156
  41.7 4.3 %copy-start.2 = (s32[192]{0:T(256)S(1)}, s32[192]{0:T(256)}, u32[]{:S(2)}) copy-start(s32[192]{0:T(256)} %owner_ref.4) | copy-start | bytes 2308

commit v3 on v2

--- a/solution.py
+++ b/solution.py
@@ -136,120 +136,206 @@
 
 def pack_kernel(*refs):
     *parts, out_ref = refs
-    share = parts[0].shape[0]
+    rows = parts[0].shape[0]
     for i, part in enumerate(parts):
-        out_ref[i * share : (i + 1) * share] = part[...]
+        out_ref[i * rows : (i + 1) * rows] = part[...]
 
 
 def pack(parts):
-    share, per, degrees = parts[0].shape
+    rows, per, width = parts[0].shape
     return pl.pallas_call(
         pack_kernel,
-        out_shape=jax.ShapeDtypeStruct((len(parts) * share, per, degrees), BF16),
+        out_shape=jax.ShapeDtypeStruct((len(parts) * rows, per, width), BF16),
         compiler_params=pltpu.CompilerParams(vmem_limit_bytes=16 << 20),
         name="pack",
     )(*parts)
 
 
-def turn_kernel(sizes, owner_ref, legendre_ref, *refs):
-    *shares, out_ref, table = refs
-    per, lats, plane = sizes["per"], sizes["lat"], sizes["rep"] * sizes["ch"]
+def by_mode(rows, per, out_ref, scratch):
+    depth = out_ref.shape[1]
+    for i in range(scratch.shape[0]):
+        scratch[i, : depth * per, :] = rows[:, i * 128 : (i + 1) * 128]
+    for k in range(per):
+        for i in range(scratch.shape[0]):
+            out_ref[k, :, i * 128 : (i + 1) * 128] = scratch[
+                i, pl.ds(k, depth, stride=per), :
+            ].astype(BF16)
+
+
+def widened(rows, before, after):
+    blank = jnp.zeros((after - before, rows.shape[1]), F32)
+    parts = []
+    for i in range(rows.shape[0] // before):
+        parts += [rows[i * before : (i + 1) * before], blank]
+    return jnp.concatenate(parts, axis=0)
+
+
+def own_kernel(sizes, deep, owner_ref, legendre_ref, out_ref, picked, scratch):
+    per = sizes["per"]
     lat_rows, slab, degrees = legendre_ref.shape
-    deep = out_ref.shape[1] // lats
-    share = lat_rows // plane
-    tiles = degrees // 128
-    for s in range(lats):
-        end = (s * deep + lat_rows) * per
-        table[:, end : (s + 1) * deep * per, :] = jnp.zeros((tiles, (deep - lat_rows) * per, 128), F32)
+    share = lat_rows // (sizes["rep"] * sizes["ch"])
     row = owned_row(owner_ref, sizes, (0,)) - lax.axis_index("sub") * slab
     pick = (lax.broadcasted_iota(jnp.int32, (slab, 128), 0) == row).astype(F32)
     pick = pick.T[:per].astype(BF16)
     for t in range(lat_rows):
-        rows = jnp.dot(pick, legendre_ref[t], preferred_element_type=F32)
-        for i in range(tiles):
-            table[i, t * per : (t + 1) * per, :] = rows[:, i * 128 : (i + 1) * 128]
-    block = share * per
-    q = lax.axis_index("rep") * sizes["ch"] + lax.axis_index("ch")
-    for s in range(1, lats):
-        for d in range(plane):
-            values = shares[d][(s - 1) * share : s * share].astype(F32).reshape(block, degrees)
-            at = pl.multiple_of((s * deep + jnp.bitwise_xor(q, d) * share) * per, 8)
-            for i in range(tiles):
-                table[i, pl.ds(at, block), :] = values[:, i * 128 : (i + 1) * 128]
-    for k in range(per):
-        for i in range(tiles):
-            out_ref[k, :, i * 128 : (i + 1) * 128] = table[
-                i, pl.ds(k, lats * deep, stride=per), :
-            ].astype(BF16)
-
-
-def turn(by_latitude, ownership, shares, deep, sizes):
+        picked[t * per : (t + 1) * per, :] = jnp.dot(pick, legendre_ref[t], preferred_element_type=F32)
+    by_mode(widened(picked[...], share * per, deep * per), per, out_ref, scratch)
+
+
+def own_table(by_latitude, ownership, deep, sizes):
     lat_rows, _, degrees = by_latitude.shape
-    per, depth = sizes["per"], sizes["lat"] * deep
+    per = sizes["per"]
+    depth = sizes["rep"] * sizes["ch"] * deep
     vmem = pl.BlockSpec(memory_space=pltpu.VMEM)
     return pl.pallas_call(
-        functools.partial(turn_kernel, sizes),
-        in_specs=[pl.BlockSpec(memory_space=pltpu.SMEM)] + [vmem] * (1 + len(shares)),
+        functools.partial(own_kernel, sizes, deep),
+        in_specs=[pl.BlockSpec(memory_space=pltpu.SMEM), vmem],
         out_specs=vmem,
         out_shape=jax.ShapeDtypeStruct((per, depth, degrees), BF16),
+        scratch_shapes=[
+            pltpu.VMEM((lat_rows * per, degrees), F32),
+            pltpu.VMEM((degrees // 128, depth * per, 128), F32),
+        ],
+        compiler_params=pltpu.CompilerParams(vmem_limit_bytes=32 << 20),
+        cost_estimate=pl.CostEstimate(flops=1000, bytes_accessed=1000, transcendentals=0),
+        name="own_table",
+    )(ownership, by_latitude)
+
+
+def turn_kernel(share, deep, rows_ref, out_ref, scratch):
+    rows, per, width = rows_ref.shape
+    values = rows_ref[...].astype(F32).reshape(rows * per, width)
+    by_mode(widened(values, share * per, deep * per), per, out_ref, scratch)
+
+
+def turn(rows, share, deep):
+    total, per, degrees = rows.shape
+    depth = total // share * deep
+    return pl.pallas_call(
+        functools.partial(turn_kernel, share, deep),
+        out_shape=jax.ShapeDtypeStruct((per, depth, degrees), BF16),
         scratch_shapes=[pltpu.VMEM((degrees // 128, depth * per, 128), F32)],
-        compiler_params=pltpu.CompilerParams(vmem_limit_bytes=32 << 20),
+        compiler_params=pltpu.CompilerParams(vmem_limit_bytes=16 << 20),
+        cost_estimate=pl.CostEstimate(flops=3_000_000_000, bytes_accessed=1000, transcendentals=0),
         name="turn",
-    )(ownership, by_latitude, *shares)
-
-
-def mix_kernel(near_ref, far_ref, w_near, w_far, out_ref, spectra):
-    lat_rows, per, width = near_ref.shape
-    deep = out_ref.shape[1]
+    )(rows)
+
+
+def mix_kernel(sizes, shifts, deep, near_ref, far_ref, w_near, w_far, out_ref, scratch):
+    rows, per, width = near_ref.shape
+    plane = sizes["rep"] * sizes["ch"]
+    lat_rows = rows // len(shifts)
+    share = lat_rows // plane
+    q = lax.axis_index("rep") * sizes["ch"] + lax.axis_index("ch")
     nt = (((1,), (1,)), ((), ()))
-    a = near_ref[...].reshape(lat_rows * per, width)
-    b = far_ref[...].reshape(lat_rows * per, width)
-    mixed = lax.dot_general(a, w_near[...], nt, preferred_element_type=F32)
-    mixed += lax.dot_general(b, w_far[...], nt, preferred_element_type=F32)
-    spectra[: lat_rows * per, :] = mixed
-    spectra[lat_rows * per :, :] = jnp.zeros(((deep - lat_rows) * per, width), F32)
-    for k in range(per):
-        out_ref[k] = spectra[pl.ds(k, deep, stride=per), :].astype(BF16)
-
-
-def mix(near, far, w_near, w_far, deep):
-    lat_rows, per, width = near.shape
-    return pl.pallas_call(
-        mix_kernel,
-        out_shape=jax.ShapeDtypeStruct((per, deep, width), BF16),
-        scratch_shapes=[pltpu.VMEM((deep * per, width), F32)],
+    parts = []
+    for i, shift in enumerate(shifts):
+        for d in range(plane):
+            at = d if shift == 0 else jnp.bitwise_xor(q, d)
+            part = pl.ds(i * lat_rows + at * share, share)
+            a = near_ref[part].reshape(share * per, width)
+            b = far_ref[part].reshape(share * per, width)
+            mixed = lax.dot_general(a, w_near[...], nt, preferred_element_type=F32)
+            mixed += lax.dot_general(b, w_far[...], nt, preferred_element_type=F32)
+            parts.append(widened(mixed, share * per, deep * per))
+    by_mode(jnp.concatenate(parts, axis=0), per, out_ref, scratch)
+
+
+def mix(near, far, w_near, w_far, shifts, deep, sizes):
+    rows, per, width = near.shape
+    depth = len(shifts) * sizes["rep"] * sizes["ch"] * deep
+    return pl.pallas_call(
+        functools.partial(mix_kernel, sizes, shifts, deep),
+        out_shape=jax.ShapeDtypeStruct((per, depth, width), BF16),
+        scratch_shapes=[pltpu.VMEM((1, depth * per, width), F32)],
         compiler_params=pltpu.CompilerParams(vmem_limit_bytes=16 << 20),
         cost_estimate=pl.CostEstimate(
-            flops=100 * 2 * near.size * width, bytes_accessed=near.size * 4, transcendentals=0
+            flops=400 * 2 * near.size * width, bytes_accessed=near.size * 4, transcendentals=0
         ),
         name="mix",
     )(near, far, w_near, w_far)
 
 
-def contract_kernel(group, *refs):
-    *spectra, table, out_ref = refs
+def cross_kernel(near_ref, far_ref, w_near, w_far, *outs):
+    rows, per, width = near_ref.shape
+    lat_rows = rows // len(outs)
+    nt = (((1,), (1,)), ((), ()))
+    for i, out_ref in enumerate(outs):
+        part = slice(i * lat_rows, (i + 1) * lat_rows)
+        a = near_ref[part].reshape(lat_rows * per, width)
+        b = far_ref[part].reshape(lat_rows * per, width)
+        mixed = lax.dot_general(a, w_near[...], nt, preferred_element_type=F32)
+        mixed += lax.dot_general(b, w_far[...], nt, preferred_element_type=F32)
+        out_ref[...] = mixed.astype(BF16).reshape(lat_rows, per, width)
+
+
+def cross_parts(near, far, w_near, w_far, parts):
+    rows, per, width = near.shape
+    return pl.pallas_call(
+        cross_kernel,
+        out_shape=[jax.ShapeDtypeStruct((rows // parts, per, width), BF16)] * parts,
+        compiler_params=pltpu.CompilerParams(vmem_limit_bytes=16 << 20),
+        cost_estimate=pl.CostEstimate(flops=1_000_000_000, bytes_accessed=1000, transcendentals=0),
+        name="cross",
+    )(near, far, w_near, w_far)
+
+
+def arrange_kernel(sizes, shift, deep, rows_ref, out_ref, scratch):
+    lat_rows, per, width = rows_ref.shape
+    plane = sizes["rep"] * sizes["ch"]
+    share = lat_rows // plane
+    q = lax.axis_index("rep") * sizes["ch"] + lax.axis_index("ch")
+    parts = []
+    for d in range(plane):
+        at = d if shift == 0 else jnp.bitwise_xor(q, d)
+        part = rows_ref[pl.ds(at * share, share)].astype(F32).reshape(share * per, width)
+        parts.append(widened(part, share * per, deep * per))
+    by_mode(jnp.concatenate(parts, axis=0), per, out_ref, scratch)
+
+
+def arrange(rows, shift, deep, sizes):
+    _, per, width = rows.shape
+    depth = sizes["rep"] * sizes["ch"] * deep
+    return pl.pallas_call(
+        functools.partial(arrange_kernel, sizes, shift, deep),
+        out_shape=jax.ShapeDtypeStruct((per, depth, width), BF16),
+        scratch_shapes=[pltpu.VMEM((1, depth * per, width), F32)],
+        compiler_params=pltpu.CompilerParams(vmem_limit_bytes=16 << 20),
+        cost_estimate=pl.CostEstimate(flops=2_000_000_000, bytes_accessed=1000, transcendentals=0),
+        name="arrange",
+    )(rows)
+
+
+def contract_kernel(lats, plane, group, *refs):
+    *spectra, own = refs[: -plane - 1]
+    *tables, out_ref = refs[-plane - 1 :]
+    deep = own.shape[1] // plane
     half = out_ref.shape[2]
     for k in range(group):
         a = jnp.concatenate([part[k] for part in spectra], axis=0)
-        c = lax.dot_general(a, table[k], (((0,), (0,)), ((), ())), preferred_element_type=F32)
+        pieces = [own[k]]
+        for s in range(lats - 1):
+            pieces += [table[k, s * deep : (s + 1) * deep] for table in tables]
+        b = jnp.concatenate(pieces, axis=0)
+        c = lax.dot_general(a, b, (((0,), (0,)), ((), ())), preferred_element_type=F32)
         out_ref[0, k] = c[:half].astype(BF16)
         out_ref[1, k] = c[half:].astype(BF16)
 
 
-def contract(spectra, table):
-    per, deep, width = spectra[0].shape
-    _, depth, degrees = table.shape
+def contract(spectra, own, tables, lats):
+    per, _, width = spectra[0].shape
+    degrees = own.shape[2]
     group = 8
     block = lambda x: pl.BlockSpec((group, *x.shape[1:]), lambda i: (i, 0, 0))
     return pl.pallas_call(
-        functools.partial(contract_kernel, group),
+        functools.partial(contract_kernel, lats, len(tables), group),
         grid=(per // group,),
-        in_specs=[block(x) for x in (*spectra, table)],
+        in_specs=[block(x) for x in (*spectra, own, *tables)],
         out_specs=pl.BlockSpec((2, group, width // 2, degrees), lambda i: (0, i, 0, 0)),
         out_shape=jax.ShapeDtypeStruct((2, per, width // 2, degrees), BF16),
         compiler_params=pltpu.CompilerParams(vmem_limit_bytes=40 << 20),
         name="contract",
-    )(*spectra, table)
+    )(*spectra, own, *tables)
 
 
 def mixing_weights(w_real, w_imag):
@@ -270,25 +356,35 @@
 def fast(field, legendre, ownership, w_real, w_imag, sizes):
     lats, plane = sizes["lat"], sizes["rep"] * sizes["ch"]
     lat_rows = field.shape[0]
+    share, deep = lat_rows // plane, (lat_rows // plane + 7) // 8 * 8
     by_latitude = jnp.transpose(legendre, (1, 0, 2))
-    along = lambda s: [(i, (i + s) % lats) for i in range(lats)]
-    swap = [(0, 1), (1, 0)]
+    forward = lambda v, s: lax.ppermute(v, "lat", [(i, (i + s) % lats) for i in range(lats)])
+    across = lambda v: lax.ppermute(v, "ch", [(0, 1), (1, 0)])
+    beyond = lambda v: lax.ppermute(v, "rep", [(0, 1), (1, 0)])
+    after = lambda v, *before: lax.optimization_barrier((v, *before))[0]
     others = tuple(range(1, lats))
-    sent = pick_rows(by_latitude, ownership, sizes, others, lat_rows // plane)
-    landed = [lax.ppermute(sent[s - 1], "lat", along(s)) for s in others]
-    after_sent, _ = lax.optimization_barrier((ownership, sent[0]))
-    spectra = dft(field, after_sent, sizes)
-    landed, starts = lax.optimization_barrier((landed, spectra[1:]))
-    near = [spectra[0]] + [lax.ppermute(v, "lat", along(s)) for s, v in zip(others, starts)]
-    far = [lax.ppermute(v, "ch", swap) for v in near]
+    sent = pick_rows(by_latitude, ownership, sizes, others, share)
+    landed = [forward(v, s) for s, v in zip(others, sent)]
+    spectra = dft(field, after(ownership, sent[0]), sizes)
+    w_near, w_far = mixing_weights(w_real, w_imag)
+    own = own_table(by_latitude, ownership, deep, sizes)
     mine = pack(landed)
-    beside = lax.ppermute(mine, "ch", swap)
-    shares = [mine, beside, lax.ppermute(mine, "rep", swap), lax.ppermute(beside, "rep", swap)]
-    deep = (lat_rows + 15) // 16 * 16
-    table = turn(by_latitude, ownership, shares, deep, sizes)
-    w_near, w_far = mixing_weights(w_real, w_imag)
-    mixed = [mix(n, f, w_near, w_far, deep) for n, f in zip(near, far)]
-    return contract(mixed, table)
+    beside = across(mine)
+    beyond_mine = beyond(mine)
+    early = pack([spectra[0], spectra[1]])
+    far_early = across(early)
+    near2 = forward(spectra[2], 2)
+    near3 = forward(spectra[3], 3)
+    zero, *sums = cross_parts(early, far_early, w_near, w_far, 2)
+    mixed = [arrange(zero, 0, deep, sizes)]
+    sum1 = forward(sums[0], 1)
+    late = pack([near2, near3])
+    beyond_beside = beyond(beside)
+    far_late = across(after(late, sums[0]))
+    tables = [turn(v, share, deep) for v in (mine, beside, beyond_mine, beyond_beside)]
+    mixed_late = mix(late, far_late, w_near, w_far, (2, 3), deep, sizes)
+    mixed += [arrange(sum1, 1, deep, sizes), mixed_late]
+    return contract(mixed, own, tables, lats)
 
 
 def fourier_rows(flat_field, modes, lat_rows, chans, nlon):
@@ -364,6 +460,7 @@
     fits = (
         sizes["ch"] == 2
         and sizes["rep"] == 2
+        and sizes["lat"] == 4
         and 2 * chans == 128
         and lat_rows % plane == 0
         and lat_rows % 4 == 0

time: 51.1 us -> 47.3 us (0.926)
  the two profiles are of different devices: /device:TPU:26 before, /device:TPU:16 now
where the time goes in v3:
time: 47.3 us; the launch traced here: 47.1 us
  starting transfers between devices  19.4 us (41%)
  Pallas kernels  15.1 us (32%)
  waiting for transfers between devices  11.6 us (25%)
  local copies, waits for them, and re-layouts  0.69 us (1%)
    ppermute x6, starting transfers between devices, fast(): lax.ppermute(v, 'lat', [(i, (i + s) % lats) for i in range(lats)])  10.9 us
    ppermute x3, waiting for transfers between devices, fast(): across = lambda v: lax.ppermute(v, 'ch', [(0, 1), (1, 0)])  9.26 us
    pallas_call x1, Pallas kernels, dft(): pl.pallas_call(functools.partial(dft_kernel, sizes, step), in_specs=[pl.B...  6.97 us
    ppermute x3, starting transfers between devices, fast(): across = lambda v: lax.ppermute(v, 'ch', [(0, 1), (1, 0)])  6.39 us
    pallas_call x1, Pallas kernels, contract(): pl.pallas_call(functools.partial(contract_kernel, lats, len(tables), grou...  2.6 us
    pallas_call x1, Pallas kernels, pick_rows(): pl.pallas_call(functools.partial(pick_kernel, sizes, shifts), grid=(1,),...  2.19 us
    ppermute x2, starting transfers between devices, fast(): beyond = lambda v: lax.ppermute(v, 'rep', [(0, 1), (1, 0)])  2.1 us
    ppermute x2, waiting for transfers between devices, fast(): beyond = lambda v: lax.ppermute(v, 'rep', [(0, 1), (1, 0)])  1.98 us
  transfers between devices with their start and end apart: 11, of which 4 were waited for; matrix products, arithmetic and copies ran while one was open for 1% of the time, Pallas kernels for 21%

profile of v3, /device:TPU:16, one launch (start us, length us, event | category | flops | bytes accessed | tf_op | source)
XLA Modules:
  0.0 47.1 jit_solution(14291769326455448397)
XLA Ops:
  0.0 2.2 %pick_rows.1 = (bf16[7,24,384]{2,1,0:T(8,128)(2,1)}, bf16[7,24,384]{2,1,0:T(8,128)(2,1)}, bf16[7,24,384]{2,1,0:T(8,128)(2,1)}) custom-call(s32[192]{0:T(256)} %owner_ref.4, bf16[28,96,384]{2,1,0:T(8,128)(2,1)} %bitcast.1), custom_call_target="tpu_custom_call" | custom-call | flops 37158912 | bytes 516096 | tf_op jit(solution)/shard_map/pick_rows/pallas_call | solution.py:115
  2.2 0.0 collective-permute-start.6
  2.2 3.0 %collective-permute-start.7 = (bf16[7,24,384]{2,1,0:T(8,128)(2,1)}, bf16[7,24,384]{2,1,0:T(8,128)(2,1)S(1)}, u32[]{:S(2)}, u32[]{:S(2)}) collective-permute-start(bf16[7,24,384]{2,1,0:T(8,128)(2,1)} %get-tuple-element.26), channel_id=1, source_target_pairs={{0,12},{4,0},{8,4},{12,8},{1,13},{5,1},{9,5},{13,9},{2,14},{6,2},{... | collective-permute-start | bytes 387080 | tf_op jit(solution)/shard_map/ppermute | solution.py:361
  5.2 0.0 collective-permute-start.5
  5.2 0.0 copy-start.1
  5.2 0.7 %copy-done.1 = s32[192]{0:T(256)S(1)} copy-done((s32[192]{0:T(256)S(1)}, s32[192]{0:T(256)}, u32[]{:S(2)}) %copy-start.1) | copy-done | bytes 792
  5.9 0.0 copy-start.3
  5.9 0.0 copy-start.4
  5.9 0.0 copy-start
  5.9 0.0 copy-start.2
  5.9 7.0 %dft.1 = (bf16[28,24,128]{2,1,0:T(8,128)(2,1)S(1)}, bf16[28,24,128]{2,1,0:T(8,128)(2,1)S(1)}, bf16[28,24,128]{2,1,0:T(8,128)(2,1)}, bf16[28,24,128]{2,1,0:T(8,128)(2,1)S(1)}) custom-call(s32[192]{0:T(256)S(1)} %copy-done.1, bf16[2,1440,192]{2,1,0:T(8,128)(2,1)} %constant.14.clone.table_ref, f32[28,64,1440]{2,1,0:T(8,128)} %field_ref.1), custom_call_target="tpu_custom_call" | custom-call | flops 1321205760 | bytes 10321920 | tf_op jit(solution)/shard_map/dft/pallas_call | solution.py:79
  12.9 2.0 %collective-permute-start.2 = (bf16[28,24,128]{2,1,0:T(8,128)(2,1)}, bf16[28,24,128]{2,1,0:T(8,128)(2,1)S(1)}, u32[]{:S(2)}, u32[]{:S(2)}) collective-permute-start(bf16[28,24,128]{2,1,0:T(8,128)(2,1)} %get-tuple-element.22), channel_id=1, source_target_pairs={{0,8},{4,12},{8,0},{12,4},{1,9},{5,13},{9,1},{13,5},{2,10},{6,14},... | collective-permute-start | bytes 516104 | tf_op jit(solution)/shard_map/ppermute | solution.py:361
  14.9 1.6 %collective-permute-start = (bf16[56,24,128]{2,1,0:T(8,128)(2,1)S(1)}, bf16[56,24,128]{2,1,0:T(8,128)(2,1)S(1)}, u32[]{:S(2)}, u32[]{:S(2)}) collective-permute-start(bf16[56,24,128]{2,1,0:T(8,128)(2,1)S(1)} %pack.3.near_ref), channel_id=1, source_target_pairs={{0,2},{2,0},{1,3},{3,1},{4,6},{6,4},{5,7},{7,5},{8,10},{10,8},{9,1... | collective-permute-start | bytes 1032200 | tf_op jit(solution)/shard_map/ppermute | solution.py:362
  16.5 0.0 copy-done.3
  16.5 0.0 copy-done.4
  16.5 0.1 constant_dynamic-slice_fusion.1
  16.6 0.1 maximum_maximum_fusion.1.w_far
  16.7 0.0 copy-done
  16.7 0.0 copy-done.2
  16.7 1.2 %own_table.1.refs_3_ = bf16[24,32,384]{2,1,0:T(8,128)(2,1)S(1)} custom-call(s32[192]{0:T(256)S(1)} %copy-done.2, bf16[28,96,384]{2,1,0:T(8,128)(2,1)S(1)} %bitcast.2), custom_call_target="tpu_custom_call" | custom-call | flops 1000 | bytes 1000 | tf_op jit(solution)/shard_map/own_table/pallas_call | solution.py:190
  17.9 0.1 maximum_maximum_fusion.w_near
  18.0 0.0 collective-permute-done.6.refs_1_
  18.0 2.3 %collective-permute-start.3 = (bf16[28,24,128]{2,1,0:T(8,128)(2,1)S(1)}, bf16[28,24,128]{2,1,0:T(8,128)(2,1)S(1)}, u32[]{:S(2)}, u32[]{:S(2)}) collective-permute-start(bf16[28,24,128]{2,1,0:T(8,128)(2,1)S(1)} %get-tuple-element.23), channel_id=1, source_target_pairs={{0,12},{4,0},{8,4},{12,8},{1,13},{5,1},{9,5},{13,9},{2,14},{6,2},{... | collective-permute-start | bytes 516104 | tf_op jit(solution)/shard_map/ppermute | solution.py:361
  20.3 0.0 collective-permute-done.7.refs_2_
  20.3 0.3 collective-permute-done.5.refs_0_
  20.7 1.6 %collective-permute-start.9 = (bf16[21,24,384]{2,1,0:T(8,128)(2,1)S(1)}, bf16[21,24,384]{2,1,0:T(8,128)(2,1)S(1)}, u32[]{:S(2)}, u32[]{:S(2)}) collective-permute-start(bf16[21,24,384]{2,1,0:T(8,128)(2,1)S(1)} %pack.5.rows_ref), channel_id=1, source_target_pairs={{0,16},{16,0},{1,17},{17,1},{2,18},{18,2},{3,19},{19,3},{4,20},{20... | collective-permute-start | bytes 1161224 | tf_op jit(solution)/shard_map/ppermute | solution.py:363
  22.2 3.3 %collective-permute-start.8 = (bf16[21,24,384]{2,1,0:T(8,128)(2,1)S(1)}, bf16[21,24,384]{2,1,0:T(8,128)(2,1)S(1)}, u32[]{:S(2)}, u32[]{:S(2)}) collective-permute-start(bf16[21,24,384]{2,1,0:T(8,128)(2,1)S(1)} %pack.5.rows_ref), channel_id=1, source_target_pairs={{0,2},{2,0},{1,3},{3,1},{4,6},{6,4},{5,7},{7,5},{8,10},{10,8},{9,1... | collective-permute-start | bytes 1161224 | tf_op jit(solution)/shard_map/ppermute | solution.py:362
  25.6 0.2 turn.4.refs_4_
  25.8 0.0 collective-permute-done.2.refs_0_
  25.8 0.0 collective-permute-done.3.refs_1_
  25.9 0.0 collective-permute-done.far_ref
  25.9 0.3 cross.1
  26.2 3.6 %collective-permute-start.1 = (bf16[28,24,128]{2,1,0:T(8,128)(2,1)S(1)}, bf16[28,24,128]{2,1,0:T(8,128)(2,1)S(1)}, u32[]{:S(2)}, u32[]{:S(2)}) collective-permute-start(bf16[28,24,128]{2,1,0:T(8,128)(2,1)S(1)} %get-tuple-element.21), channel_id=1, source_target_pairs={{0,4},{4,8},{8,12},{12,0},{1,5},{5,9},{9,13},{13,1},{2,6},{6,10},{... | collective-permute-start | bytes 516104 | tf_op jit(solution)/shard_map/ppermute | solution.py:361
  29.8 1.5 %collective-permute-start.4 = (bf16[56,24,128]{2,1,0:T(8,128)(2,1)S(1)}, bf16[56,24,128]{2,1,0:T(8,128)(2,1)S(1)}, u32[]{:S(2)}, u32[]{:S(2)}) collective-permute-start(bf16[56,24,128]{2,1,0:T(8,128)(2,1)S(1)} %pack.4.near_ref), channel_id=1, source_target_pairs={{0,2},{2,0},{1,3},{3,1},{4,6},{6,4},{5,7},{7,5},{8,10},{10,8},{9,1... | collective-permute-start | bytes 1032200 | tf_op jit(solution)/shard_map/ppermute | solution.py:362
  31.3 0.1 arrange.2.refs_0_
  31.4 4.0 %collective-permute-done.8.rows_ref = bf16[21,24,384]{2,1,0:T(8,128)(2,1)S(1)} collective-permute-done((bf16[21,24,384]{2,1,0:T(8,128)(2,1)S(1)}, bf16[21,24,384]{2,1,0:T(8,128)(2,1)S(1)}, u32[]{:S(2)}, u32[]{:S(2)}) %collective-permute-start.8) | collective-permute-done | bytes 387104 | tf_op jit(solution)/shard_map/ppermute | solution.py:362
  35.4 0.5 %collective-permute-start.10 = (bf16[21,24,384]{2,1,0:T(8,128)(2,1)S(1)}, bf16[21,24,384]{2,1,0:T(8,128)(2,1)S(1)}, u32[]{:S(2)}, u32[]{:S(2)}) collective-permute-start(bf16[21,24,384]{2,1,0:T(8,128)(2,1)S(1)} %collective-permute-done.8.rows_ref), channel_id=1, source_target_pairs={{0,16},{16,0},{1,17},{17,1},{2,18},{18,2},{3,19},{19,3},{4,20},{20... | collective-permute-start | bytes 1161224 | tf_op jit(solution)/shard_map/ppermute | solution.py:363
  35.9 0.2 turn.5.refs_5_
  36.1 0.0 collective-permute-done.1.rows_ref
  36.2 0.1 arrange.3.refs_1_
  36.3 0.0 collective-permute-done.9.rows_ref
  36.3 0.2 turn.6.refs_6_
  36.5 5.2 %collective-permute-done.4.far_ref = bf16[56,24,128]{2,1,0:T(8,128)(2,1)S(1)} collective-permute-done((bf16[56,24,128]{2,1,0:T(8,128)(2,1)S(1)}, bf16[56,24,128]{2,1,0:T(8,128)(2,1)S(1)}, u32[]{:S(2)}, u32[]{:S(2)}) %collective-permute-start.4) | collective-permute-done | bytes 344096 | tf_op jit(solution)/shard_map/ppermute | solution.py:362
  41.7 0.6 %mix.1.refs_2_ = bf16[24,64,128]{2,1,0:T(8,128)(2,1)S(1)} custom-call(bf16[56,24,128]{2,1,0:T(8,128)(2,1)S(1)} %pack.4.near_ref, bf16[56,24,128]{2,1,0:T(8,128)(2,1)S(1)} %collective-permute-done.4.far_ref, bf16[128,128]{1,0:T(8,128)(2,1)S(1)} %maximum_maximum_fusion.w_near, bf16[128,128]{1,0:T(8,128)(2,1)S(1)} %maximum_maximum_fusion.1.w_far), custom_call_target="tpu_custom_call" | custom-call | flops 17616076800 | bytes 688128 | tf_op jit(solution)/shard_map/mix/pallas_call | solution.py:247
  42.3 2.0 %collective-permute-done.10.rows_ref = bf16[21,24,384]{2,1,0:T(8,128)(2,1)S(1)} collective-permute-done((bf16[21,24,384]{2,1,0:T(8,128)(2,1)S(1)}, bf16[21,24,384]{2,1,0:T(8,128)(2,1)S(1)}, u32[]{:S(2)}, u32[]{:S(2)}) %collective-permute-start.10) | collective-permute-done | bytes 387104 | tf_op jit(solution)/shard_map/ppermute | solution.py:363
  44.3 0.2 turn.7.refs_7_
  44.5 2.6 %contract.1 = bf16[2,24,64,384]{3,2,1,0:T(8,128)(2,1)} custom-call(bf16[24,32,128]{2,1,0:T(8,128)(2,1)S(1)} %arrange.2.refs_0_, bf16[24,32,128]{2,1,0:T(8,128)(2,1)S(1)} %arrange.3.refs_1_, bf16[24,64,128]{2,1,0:T(8,128)(2,1)S(1)} %mix.1.refs_2_, bf16[24,32,384]{2,1,0:T(8,128)(2,1)S(1)} %own_table.1.refs_3_, bf16[24,24,384]{2,1,0:T(8,128)(2,1)S(1)} %turn.4.refs_4_, ...), custom_call_target="tpu_custom_call" | custom-call | tf_op jit(solution)/shard_map/contract/pallas_call | solution.py:330
  (3 shorter events, 0.1 us)
Async XLA Ops:
  2.2 15.8 %collective-permute-start.6 = (bf16[7,24,384]{2,1,0:T(8,128)(2,1)}, bf16[7,24,384]{2,1,0:T(8,128)(2,1)S(1)}, u32[]{:S(2)}, u32[]{:S(2)}) collective-permute-start(bf16[7,24,384]{2,1,0:T(8,128)(2,1)} %get-tuple-element.25), channel_id=1, source_target_pairs={{0,8},{4,12},{8,0},{12,4},{1,9},{5,13},{9,1},{13,5},{2,10},{6,14},... | collective-permute-start | bytes 387080 | tf_op jit(solution)/shard_map/ppermute | solution.py:361
  2.2 18.1 %collective-permute-start.7 = (bf16[7,24,384]{2,1,0:T(8,128)(2,1)}, bf16[7,24,384]{2,1,0:T(8,128)(2,1)S(1)}, u32[]{:S(2)}, u32[]{:S(2)}) collective-permute-start(bf16[7,24,384]{2,1,0:T(8,128)(2,1)} %get-tuple-element.26), channel_id=1, source_target_pairs={{0,12},{4,0},{8,4},{12,8},{1,13},{5,1},{9,5},{13,9},{2,14},{6,2},{... | collective-permute-start | bytes 387080 | tf_op jit(solution)/shard_map/ppermute | solution.py:361
  5.2 15.4 %collective-permute-start.5 = (bf16[7,24,384]{2,1,0:T(8,128)(2,1)}, bf16[7,24,384]{2,1,0:T(8,128)(2,1)S(1)}, u32[]{:S(2)}, u32[]{:S(2)}) collective-permute-start(bf16[7,24,384]{2,1,0:T(8,128)(2,1)} %get-tuple-element.16), channel_id=1, source_target_pairs={{0,4},{4,8},{8,12},{12,0},{1,5},{5,9},{9,13},{13,1},{2,6},{6,10},{... | collective-permute-start | bytes 387080 | tf_op jit(solution)/shard_map/ppermute | solution.py:361
  5.2 0.7 %copy-start.1 = (s32[192]{0:T(256)S(1)}, s32[192]{0:T(256)}, u32[]{:S(2)}) copy-start(s32[192]{0:T(256)} %owner_ref.4) | copy-start | bytes 2308
  5.9 10.6 %copy-start.3 = (bf16[64,128]{1,0:T(8,128)(2,1)S(1)}, bf16[64,128]{1,0:T(8,128)(2,1)}, u32[]{:S(2)}) copy-start(bf16[64,128]{1,0:T(8,128)(2,1)} %param.9) | copy-start | bytes 49156
  5.9 10.6 %copy-start.4 = (bf16[64,128]{1,0:T(8,128)(2,1)S(1)}, bf16[64,128]{1,0:T(8,128)(2,1)}, u32[]{:S(2)}) copy-start(bf16[64,128]{1,0:T(8,128)(2,1)} %param.10) | copy-start | bytes 49156
  5.9 10.7 %copy-start = (bf16[96,28,384]{2,0,1:T(8,128)(2,1)S(1)}, bf16[96,28,384]{2,0,1:T(8,128)(2,1)}, u32[]{:S(2)}) copy-start(bf16[96,28,384]{2,0,1:T(8,128)(2,1)} %param.7) | copy-start | bytes 6193156
  5.9 10.7 %copy-start.2 = (s32[192]{0:T(256)S(1)}, s32[192]{0:T(256)}, u32[]{:S(2)}) copy-start(s32[192]{0:T(256)} %owner_ref.4) | copy-start | bytes 2308
  12.9 12.9 %collective-permute-start.2 = (bf16[28,24,128]{2,1,0:T(8,128)(2,1)}, bf16[28,24,128]{2,1,0:T(8,128)(2,1)S(1)}, u32[]{:S(2)}, u32[]{:S(2)}) collective-permute-start(bf16[28,24,128]{2,1,0:T(8,128)(2,1)} %get-tuple-element.22), channel_id=1, source_target_pairs={{0,8},{4,12},{8,0},{12,4},{1,9},{5,13},{9,1},{13,5},{2,10},{6,14},... | collective-permute-start | bytes 516104 | tf_op jit(solution)/shard_map/ppermute | solution.py:361
  14.9 10.9 %collective-permute-start = (bf16[56,24,128]{2,1,0:T(8,128)(2,1)S(1)}, bf16[56,24,128]{2,1,0:T(8,128)(2,1)S(1)}, u32[]{:S(2)}, u32[]{:S(2)}) collective-permute-start(bf16[56,24,128]{2,1,0:T(8,128)(2,1)S(1)} %pack.3.near_ref), channel_id=1, source_target_pairs={{0,2},{2,0},{1,3},{3,1},{4,6},{6,4},{5,7},{7,5},{8,10},{10,8},{9,1... | collective-permute-start | bytes 1032200 | tf_op jit(solution)/shard_map/ppermute | solution.py:362
  18.0 7.8 %collective-permute-start.3 = (bf16[28,24,128]{2,1,0:T(8,128)(2,1)S(1)}, bf16[28,24,128]{2,1,0:T(8,128)(2,1)S(1)}, u32[]{:S(2)}, u32[]{:S(2)}) collective-permute-start(bf16[28,24,128]{2,1,0:T(8,128)(2,1)S(1)} %get-tuple-element.23), channel_id=1, source_target_pairs={{0,12},{4,0},{8,4},{12,8},{1,13},{5,1},{9,5},{13,9},{2,14},{6,2},{... | collective-permute-start | bytes 516104 | tf_op jit(solution)/shard_map/ppermute | solution.py:361
  20.7 15.6 %collective-permute-start.9 = (bf16[21,24,384]{2,1,0:T(8,128)(2,1)S(1)}, bf16[21,24,384]{2,1,0:T(8,128)(2,1)S(1)}, u32[]{:S(2)}, u32[]{:S(2)}) collective-permute-start(bf16[21,24,384]{2,1,0:T(8,128)(2,1)S(1)} %pack.5.rows_ref), channel_id=1, source_target_pairs={{0,16},{16,0},{1,17},{17,1},{2,18},{18,2},{3,19},{19,3},{4,20},{20... | collective-permute-start | bytes 1161224 | tf_op jit(solution)/shard_map/ppermute | solution.py:363
  22.2 13.2 %collective-permute-start.8 = (bf16[21,24,384]{2,1,0:T(8,128)(2,1)S(1)}, bf16[21,24,384]{2,1,0:T(8,128)(2,1)S(1)}, u32[]{:S(2)}, u32[]{:S(2)}) collective-permute-start(bf16[21,24,384]{2,1,0:T(8,128)(2,1)S(1)} %pack.5.rows_ref), channel_id=1, source_target_pairs={{0,2},{2,0},{1,3},{3,1},{4,6},{6,4},{5,7},{7,5},{8,10},{10,8},{9,1... | collective-permute-start | bytes 1161224 | tf_op jit(solution)/shard_map/ppermute | solution.py:362
  26.2 9.9 %collective-permute-start.1 = (bf16[28,24,128]{2,1,0:T(8,128)(2,1)S(1)}, bf16[28,24,128]{2,1,0:T(8,128)(2,1)S(1)}, u32[]{:S(2)}, u32[]{:S(2)}) collective-permute-start(bf16[28,24,128]{2,1,0:T(8,128)(2,1)S(1)} %get-tuple-element.21), channel_id=1, source_target_pairs={{0,4},{4,8},{8,12},{12,0},{1,5},{5,9},{9,13},{13,1},{2,6},{6,10},{... | collective-permute-start | bytes 516104 | tf_op jit(solution)/shard_map/ppermute | solution.py:361
  29.8 11.9 %collective-permute-start.4 = (bf16[56,24,128]{2,1,0:T(8,128)(2,1)S(1)}, bf16[56,24,128]{2,1,0:T(8,128)(2,1)S(1)}, u32[]{:S(2)}, u32[]{:S(2)}) collective-permute-start(bf16[56,24,128]{2,1,0:T(8,128)(2,1)S(1)} %pack.4.near_ref), channel_id=1, source_target_pairs={{0,2},{2,0},{1,3},{3,1},{4,6},{6,4},{5,7},{7,5},{8,10},{10,8},{9,1... | collective-permute-start | bytes 1032200 | tf_op jit(solution)/shard_map/ppermute | solution.py:362
  35.4 8.9 %collective-permute-start.10 = (bf16[21,24,384]{2,1,0:T(8,128)(2,1)S(1)}, bf16[21,24,384]{2,1,0:T(8,128)(2,1)S(1)}, u32[]{:S(2)}, u32[]{:S(2)}) collective-permute-start(bf16[21,24,384]{2,1,0:T(8,128)(2,1)S(1)} %collective-permute-done.8.rows_ref), channel_id=1, source_target_pairs={{0,16},{16,0},{1,17},{17,1},{2,18},{18,2},{3,19},{19,3},{4,20},{20... | collective-permute-start | bytes 1161224 | tf_op jit(solution)/shard_map/ppermute | solution.py:363

commit v4 on v3

--- a/solution.py
+++ b/solution.py
@@ -13,11 +13,12 @@
 BF16 = jnp.bfloat16
 
 
-def twiddles(nlon, modes):
+def twiddles(nlon, modes, parts):
     phase = np.arange(nlon)[:, None] * np.arange(modes)[None, :] % nlon
     angle = phase * (2.0 * math.pi / nlon)
     scale = 1.0 / math.sqrt(nlon)
-    return np.stack([np.cos(angle) * scale, -np.sin(angle) * scale]).astype(BF16)
+    waves = np.stack([np.cos(angle) * scale, -np.sin(angle) * scale]).astype(BF16)
+    return np.moveaxis(waves.reshape(2, nlon, parts, modes // parts), 2, 0).copy()
 
 
 def position(shift, k, sizes):
@@ -37,29 +38,38 @@
     return row
 
 
-def dft_kernel(sizes, step, owner_ref, table_ref, field_ref, *refs):
+def choice(modes_ref, slab):
+    row = lax.broadcasted_iota(jnp.int32, (slab, 128), 0)
+    return (row == modes_ref[:1]).astype(F32)
+
+
+def dft_kernel(sizes, step, ahead, modes_ref, table_ref, field_ref, *refs):
     *outs, grid_values, chosen, arrived = refs
     per = sizes["per"]
     rows, chans, nlon = grid_values.shape
+    steps = rows // step
 
     def part_copy(i):
         part = pl.ds(i * step, step)
         return pltpu.make_async_copy(field_ref.at[part], grid_values.at[part], arrived.at[i])
 
-    for i in range(rows // step):
+    for i in range(ahead):
         part_copy(i).start()
 
-    row = owned_row(owner_ref, sizes, range(sizes["lat"]))
-    modes = table_ref.shape[2]
-    pick = (lax.broadcasted_iota(jnp.int32, (modes, 128), 0) == row).astype(F32).astype(BF16)
+    pick = choice(modes_ref, table_ref.shape[2]).astype(BF16)
     for r in range(2):
         chosen[:, r * 128 : (r + 1) * 128] = jnp.dot(
             table_ref[r], pick, preferred_element_type=F32
         ).astype(BF16)
 
-    @pl.loop(0, rows // step)
+    @pl.loop(0, steps)
     def _(i):
         part_copy(i).wait()
+
+        @pl.when(i + ahead < steps)
+        def _():
+            part_copy(i + ahead).start()
+
         values = grid_values[pl.ds(i * step, step)].reshape(step * chans, nlon).astype(BF16)
         spectrum = jnp.dot(values, chosen[...], preferred_element_type=F32)
         for t in range(step):
@@ -69,20 +79,17 @@
                 outs[shift][i * step + t] = turned[shift * per : (shift + 1) * per].astype(BF16)
 
 
-def dft(field, ownership, sizes):
+def dft(field, modes, sizes):
     lat_rows, chans, nlon = field.shape
-    modes = ownership.shape[0]
-    step = 4
-    per = sizes["per"]
-    table = jnp.asarray(twiddles(nlon, modes))
+    per, step, ahead = sizes["per"], 4, 7
+    slab = sizes["lat"] * per
+    waves = jnp.asarray(twiddles(nlon, slab * sizes["sub"], sizes["sub"]))
+    table = lax.dynamic_index_in_dim(waves, lax.axis_index("sub"), 0, keepdims=False)
+    held = pl.BlockSpec(memory_space=pl.ANY)
     vmem = pl.BlockSpec(memory_space=pltpu.VMEM)
     return pl.pallas_call(
-        functools.partial(dft_kernel, sizes, step),
-        in_specs=[
-            pl.BlockSpec(memory_space=pltpu.SMEM),
-            vmem,
-            pl.BlockSpec(memory_space=pl.ANY),
-        ],
+        functools.partial(dft_kernel, sizes, step, ahead),
+        in_specs=[vmem, vmem, held],
         out_specs=[vmem] * sizes["lat"],
         out_shape=[jax.ShapeDtypeStruct((lat_rows, per, 128), BF16)] * sizes["lat"],
         scratch_shapes=[
@@ -90,43 +97,53 @@
             pltpu.VMEM((nlon, 256), BF16),
             pltpu.SemaphoreType.DMA((lat_rows // step,)),
         ],
-        compiler_params=pltpu.CompilerParams(vmem_limit_bytes=52 << 20),
+        compiler_params=pltpu.CompilerParams(vmem_limit_bytes=48 << 20),
         cost_estimate=pl.CostEstimate(
             flops=2 * lat_rows * chans * nlon * 256, bytes_accessed=field.size * 4, transcendentals=0
         ),
         name="dft",
-    )(ownership, table, field)
-
-
-def pick_kernel(sizes, shifts, owner_ref, legendre_ref, *outs):
+    )(modes, table, field)
+
+
+def pick_kernel(sizes, ownership_ref, table_ref, modes_ref, *refs):
+    *outs, legendre_ref, owner_ref, arrived, known = refs
     per = sizes["per"]
-    row = owned_row(owner_ref, sizes, shifts) - lax.axis_index("sub") * legendre_ref.shape[1]
-    pick = (lax.broadcasted_iota(jnp.int32, (legendre_ref.shape[1], 128), 0) == row).astype(F32)
-    pick = pick.T[: len(shifts) * per].astype(BF16)
-    for t in range(legendre_ref.shape[0]):
-        rows = jnp.dot(pick, legendre_ref[t], preferred_element_type=F32)
-        for i in range(len(shifts)):
-            outs[i][t] = rows[i * per : (i + 1) * per].astype(BF16)
-
-
-def pick_rows(table, ownership, sizes, shifts, rows):
+    rows, slab, _ = legendre_ref.shape
+    share = lax.axis_index("rep") * sizes["ch"] + lax.axis_index("ch")
+    owners = pltpu.make_async_copy(ownership_ref, owner_ref, known)
+    owners.start()
+    values = pltpu.make_async_copy(table_ref.at[pl.ds(share * rows, rows)], legendre_ref, arrived)
+    values.start()
+    owners.wait()
+    row = owned_row(owner_ref, sizes, range(sizes["lat"])) - lax.axis_index("sub") * slab
+    modes_ref[...] = jnp.broadcast_to(row, modes_ref.shape)
+    pick = choice(modes_ref, slab).T[per : sizes["lat"] * per].astype(BF16)
+    values.wait()
+    for t in range(rows):
+        picked = jnp.dot(pick, legendre_ref[t], preferred_element_type=F32)
+        for i, out_ref in enumerate(outs):
+            out_ref[t] = picked[i * per : (i + 1) * per].astype(BF16)
+
+
+def pick_rows(table, ownership, sizes, rows):
     _, slab, degrees = table.shape
-    per = sizes["per"]
-    return pl.pallas_call(
-        functools.partial(pick_kernel, sizes, shifts),
-        grid=(1,),
-        in_specs=[
-            pl.BlockSpec(memory_space=pltpu.SMEM),
-            pl.BlockSpec(
-                (rows, slab, degrees),
-                lambda i: (lax.axis_index("rep") * sizes["ch"] + lax.axis_index("ch"), 0, 0),
-            ),
+    per, others = sizes["per"], sizes["lat"] - 1
+    held = pl.BlockSpec(memory_space=pl.ANY)
+    return pl.pallas_call(
+        functools.partial(pick_kernel, sizes),
+        in_specs=[held, held],
+        out_specs=[pl.BlockSpec(memory_space=pltpu.VMEM)] * (1 + others),
+        out_shape=[jax.ShapeDtypeStruct((8, 128), jnp.int32)]
+        + [jax.ShapeDtypeStruct((rows, per, degrees), BF16)] * others,
+        scratch_shapes=[
+            pltpu.VMEM((rows, slab, degrees), BF16),
+            pltpu.SMEM(ownership.shape, jnp.int32),
+            pltpu.SemaphoreType.DMA,
+            pltpu.SemaphoreType.DMA,
         ],
-        out_specs=[pl.BlockSpec((rows, per, degrees), lambda i: (0, 0, 0))] * len(shifts),
-        out_shape=[jax.ShapeDtypeStruct((rows, per, degrees), BF16)] * len(shifts),
-        compiler_params=pltpu.CompilerParams(vmem_limit_bytes=60 << 20),
+        compiler_params=pltpu.CompilerParams(vmem_limit_bytes=62 * 1000 * 1000),
         cost_estimate=pl.CostEstimate(
-            flops=2 * rows * slab * degrees * per * len(shifts),
+            flops=2 * rows * slab * degrees * per * others,
             bytes_accessed=rows * slab * degrees * 2,
             transcendentals=0,
         ),
@@ -170,26 +187,24 @@
     return jnp.concatenate(parts, axis=0)
 
 
-def own_kernel(sizes, deep, owner_ref, legendre_ref, out_ref, picked, scratch):
+def own_kernel(sizes, deep, modes_ref, legendre_ref, out_ref, picked, scratch):
     per = sizes["per"]
     lat_rows, slab, degrees = legendre_ref.shape
     share = lat_rows // (sizes["rep"] * sizes["ch"])
-    row = owned_row(owner_ref, sizes, (0,)) - lax.axis_index("sub") * slab
-    pick = (lax.broadcasted_iota(jnp.int32, (slab, 128), 0) == row).astype(F32)
-    pick = pick.T[:per].astype(BF16)
+    pick = choice(modes_ref, slab).T[:per].astype(BF16)
     for t in range(lat_rows):
         picked[t * per : (t + 1) * per, :] = jnp.dot(pick, legendre_ref[t], preferred_element_type=F32)
     by_mode(widened(picked[...], share * per, deep * per), per, out_ref, scratch)
 
 
-def own_table(by_latitude, ownership, deep, sizes):
+def own_table(by_latitude, modes, deep, sizes):
     lat_rows, _, degrees = by_latitude.shape
     per = sizes["per"]
     depth = sizes["rep"] * sizes["ch"] * deep
     vmem = pl.BlockSpec(memory_space=pltpu.VMEM)
     return pl.pallas_call(
         functools.partial(own_kernel, sizes, deep),
-        in_specs=[pl.BlockSpec(memory_space=pltpu.SMEM), vmem],
+        in_specs=[vmem, vmem],
         out_specs=vmem,
         out_shape=jax.ShapeDtypeStruct((per, depth, degrees), BF16),
         scratch_shapes=[
@@ -197,9 +212,9 @@
             pltpu.VMEM((degrees // 128, depth * per, 128), F32),
         ],
         compiler_params=pltpu.CompilerParams(vmem_limit_bytes=32 << 20),
-        cost_estimate=pl.CostEstimate(flops=1000, bytes_accessed=1000, transcendentals=0),
+        cost_estimate=pl.CostEstimate(flops=3_000_000_000, bytes_accessed=1000, transcendentals=0),
         name="own_table",
-    )(ownership, by_latitude)
+    )(modes, by_latitude)
 
 
 def turn_kernel(share, deep, rows_ref, out_ref, scratch):
@@ -216,7 +231,7 @@
         out_shape=jax.ShapeDtypeStruct((per, depth, degrees), BF16),
         scratch_shapes=[pltpu.VMEM((degrees // 128, depth * per, 128), F32)],
         compiler_params=pltpu.CompilerParams(vmem_limit_bytes=16 << 20),
-        cost_estimate=pl.CostEstimate(flops=3_000_000_000, bytes_accessed=1000, transcendentals=0),
+        cost_estimate=pl.CostEstimate(flops=1000, bytes_accessed=1000, transcendentals=0),
         name="turn",
     )(rows)
 
@@ -250,7 +265,7 @@
         scratch_shapes=[pltpu.VMEM((1, depth * per, width), F32)],
         compiler_params=pltpu.CompilerParams(vmem_limit_bytes=16 << 20),
         cost_estimate=pl.CostEstimate(
-            flops=400 * 2 * near.size * width, bytes_accessed=near.size * 4, transcendentals=0
+            flops=2 * 2 * near.size * width, bytes_accessed=near.size * 4, transcendentals=0
         ),
         name="mix",
     )(near, far, w_near, w_far)
@@ -275,7 +290,7 @@
         cross_kernel,
         out_shape=[jax.ShapeDtypeStruct((rows // parts, per, width), BF16)] * parts,
         compiler_params=pltpu.CompilerParams(vmem_limit_bytes=16 << 20),
-        cost_estimate=pl.CostEstimate(flops=1_000_000_000, bytes_accessed=1000, transcendentals=0),
+        cost_estimate=pl.CostEstimate(flops=1000, bytes_accessed=1000, transcendentals=0),
         name="cross",
     )(near, far, w_near, w_far)
 
@@ -301,12 +316,12 @@
         out_shape=jax.ShapeDtypeStruct((per, depth, width), BF16),
         scratch_shapes=[pltpu.VMEM((1, depth * per, width), F32)],
         compiler_params=pltpu.CompilerParams(vmem_limit_bytes=16 << 20),
-        cost_estimate=pl.CostEstimate(flops=2_000_000_000, bytes_accessed=1000, transcendentals=0),
+        cost_estimate=pl.CostEstimate(flops=4_000_000_000, bytes_accessed=1000, transcendentals=0),
         name="arrange",
     )(rows)
 
 
-def contract_kernel(lats, plane, group, *refs):
+def contract_kernel(order, plane, group, *refs):
     *spectra, own = refs[: -plane - 1]
     *tables, out_ref = refs[-plane - 1 :]
     deep = own.shape[1] // plane
@@ -314,21 +329,21 @@
     for k in range(group):
         a = jnp.concatenate([part[k] for part in spectra], axis=0)
         pieces = [own[k]]
-        for s in range(lats - 1):
-            pieces += [table[k, s * deep : (s + 1) * deep] for table in tables]
+        for s in order:
+            pieces += [table[k, (s - 1) * deep : s * deep] for table in tables]
         b = jnp.concatenate(pieces, axis=0)
         c = lax.dot_general(a, b, (((0,), (0,)), ((), ())), preferred_element_type=F32)
         out_ref[0, k] = c[:half].astype(BF16)
         out_ref[1, k] = c[half:].astype(BF16)
 
 
-def contract(spectra, own, tables, lats):
+def contract(spectra, own, tables, order):
     per, _, width = spectra[0].shape
     degrees = own.shape[2]
-    group = 8
+    group = 12
     block = lambda x: pl.BlockSpec((group, *x.shape[1:]), lambda i: (i, 0, 0))
     return pl.pallas_call(
-        functools.partial(contract_kernel, lats, len(tables), group),
+        functools.partial(contract_kernel, order, len(tables), group),
         grid=(per // group,),
         in_specs=[block(x) for x in (*spectra, own, *tables)],
         out_specs=pl.BlockSpec((2, group, width // 2, degrees), lambda i: (0, i, 0, 0)),
@@ -362,29 +377,29 @@
     across = lambda v: lax.ppermute(v, "ch", [(0, 1), (1, 0)])
     beyond = lambda v: lax.ppermute(v, "rep", [(0, 1), (1, 0)])
     after = lambda v, *before: lax.optimization_barrier((v, *before))[0]
-    others = tuple(range(1, lats))
-    sent = pick_rows(by_latitude, ownership, sizes, others, share)
-    landed = [forward(v, s) for s, v in zip(others, sent)]
-    spectra = dft(field, after(ownership, sent[0]), sizes)
+    modes, *sent = pick_rows(by_latitude, ownership, sizes, share)
+    landed = [forward(v, s) for s, v in enumerate(sent, 1)]
+    spectra = dft(field, modes, sizes)
     w_near, w_far = mixing_weights(w_real, w_imag)
-    own = own_table(by_latitude, ownership, deep, sizes)
+    own = own_table(by_latitude, modes, deep, sizes)
     mine = pack(landed)
     beside = across(mine)
     beyond_mine = beyond(mine)
-    early = pack([spectra[0], spectra[1]])
+    early = pack([spectra[0], spectra[2]])
     far_early = across(early)
-    near2 = forward(spectra[2], 2)
-    near3 = forward(spectra[3], 3)
+    near3 = forward(after(spectra[3], mine), 3)
+    near1 = forward(after(spectra[1], mine), 1)
     zero, *sums = cross_parts(early, far_early, w_near, w_far, 2)
     mixed = [arrange(zero, 0, deep, sizes)]
-    sum1 = forward(sums[0], 1)
-    late = pack([near2, near3])
+    sum2 = forward(sums[0], 2)
+    late0 = pack([near3, near1])
     beyond_beside = beyond(beside)
-    far_late = across(after(late, sums[0]))
+    far_late0 = across(late0)
+    far_late0 = after(far_late0, sum2)
     tables = [turn(v, share, deep) for v in (mine, beside, beyond_mine, beyond_beside)]
-    mixed_late = mix(late, far_late, w_near, w_far, (2, 3), deep, sizes)
-    mixed += [arrange(sum1, 1, deep, sizes), mixed_late]
-    return contract(mixed, own, tables, lats)
+    mixed.append(mix(late0, far_late0, w_near, w_far, (3, 1), deep, sizes))
+    mixed += [arrange(v, s, deep, sizes) for v, s in ((sum2, 2),)]
+    return contract(mixed, own, tables, (3, 1, 2))
 
 
 def fourier_rows(flat_field, modes, lat_rows, chans, nlon):
@@ -463,7 +478,7 @@
         and sizes["lat"] == 4
         and 2 * chans == 128
         and lat_rows % plane == 0
-        and lat_rows % 4 == 0
+        and lat_rows % 28 == 0
         and sizes["per"] % 8 == 0
         and sizes["lat"] * sizes["per"] <= 128
         and legendre.shape[2] % 128 == 0

time: 47.3 us -> 44.9 us (0.949)
  the two profiles are of different devices: /device:TPU:16 before, /device:TPU:0 now
where the time goes in v4:
time: 44.9 us; the launch traced here: 44.7 us
  starting transfers between devices  18.8 us (42%)
  waiting for transfers between devices  12.7 us (28%)
  Pallas kernels  12 us (27%)
  local copies, waits for them, and re-layouts  0.75 us (2%)
    ppermute x6, waiting for transfers between devices, fast(): lax.ppermute(v, 'lat', [(i, (i + s) % lats) for i in range(lats)])  12.4 us
    ppermute x6, starting transfers between devices, fast(): lax.ppermute(v, 'lat', [(i, (i + s) % lats) for i in range(lats)])  12 us
    pallas_call x1, Pallas kernels, dft(): pl.pallas_call(functools.partial(dft_kernel, sizes, step, ahead), in_spec...  5.01 us
    ppermute x3, starting transfers between devices, fast(): across = lambda v: lax.ppermute(v, 'ch', [(0, 1), (1, 0)])  3.71 us
    ppermute x2, starting transfers between devices, fast(): beyond = lambda v: lax.ppermute(v, 'rep', [(0, 1), (1, 0)])  3.1 us
    pallas_call x1, Pallas kernels, pick_rows(): pl.pallas_call(functools.partial(pick_kernel, sizes), in_specs=[held, hel...  2.19 us
    pallas_call x1, Pallas kernels, contract(): pl.pallas_call(functools.partial(contract_kernel, order, len(tables), gro...  2.08 us
  transfers between devices with their start and end apart: 11, of which 4 were waited for; matrix products, arithmetic and copies ran while one was open for 1% of the time, Pallas kernels for 17%

profile of v4, /device:TPU:0, one launch (start us, length us, event | category | flops | bytes accessed | tf_op | source)
XLA Modules:
  0.0 44.7 jit_solution(14367526550858011785)
XLA Ops:
  0.0 0.0 copy-start.2
  0.0 2.2 %pick_rows.1 = (s32[8,128]{1,0:T(8,128)}, bf16[7,24,384]{2,1,0:T(8,128)(2,1)}, bf16[7,24,384]{2,1,0:T(8,128)(2,1)}, bf16[7,24,384]{2,1,0:T(8,128)(2,1)}) custom-call(s32[192]{0:T(256)} %ownership_ref.1, bf16[28,96,384]{2,1,0:T(8,128)(2,1)} %bitcast.3), custom_call_target="tpu_custom_call" | custom-call | flops 37158912 | bytes 516096 | tf_op jit(solution)/shard_map/pick_rows/pallas_call | solution.py:132
  2.2 3.1 %collective-permute-start.1 = (bf16[7,24,384]{2,1,0:T(8,128)(2,1)}, bf16[7,24,384]{2,1,0:T(8,128)(2,1)S(1)}, u32[]{:S(2)}, u32[]{:S(2)}) collective-permute-start(bf16[7,24,384]{2,1,0:T(8,128)(2,1)} %get-tuple-element.23), channel_id=1, source_target_pairs={{0,4},{4,8},{8,12},{12,0},{1,5},{5,9},{9,13},{13,1},{2,6},{6,10},{... | collective-permute-start | bytes 387080 | tf_op jit(solution)/shard_map/ppermute | solution.py:376
  5.3 2.6 %collective-permute-start.2 = (bf16[7,24,384]{2,1,0:T(8,128)(2,1)}, bf16[7,24,384]{2,1,0:T(8,128)(2,1)S(1)}, u32[]{:S(2)}, u32[]{:S(2)}) collective-permute-start(bf16[7,24,384]{2,1,0:T(8,128)(2,1)} %get-tuple-element.24), channel_id=1, source_target_pairs={{0,8},{4,12},{8,0},{12,4},{1,9},{5,13},{9,1},{13,5},{2,10},{6,14},... | collective-permute-start | bytes 387080 | tf_op jit(solution)/shard_map/ppermute | solution.py:376
  7.9 1.3 %collective-permute-start.3 = (bf16[7,24,384]{2,1,0:T(8,128)(2,1)}, bf16[7,24,384]{2,1,0:T(8,128)(2,1)S(1)}, u32[]{:S(2)}, u32[]{:S(2)}) collective-permute-start(bf16[7,24,384]{2,1,0:T(8,128)(2,1)} %get-tuple-element.25), channel_id=1, source_target_pairs={{0,12},{4,0},{8,4},{12,8},{1,13},{5,1},{9,5},{13,9},{2,14},{6,2},{... | collective-permute-start | bytes 387080 | tf_op jit(solution)/shard_map/ppermute | solution.py:376
  9.2 0.0 copy-done.2
  9.3 0.0 copy-start.1
  9.3 0.7 %copy-done.1 = s32[8,128]{1,0:T(8,128)S(1)} copy-done((s32[8,128]{1,0:T(8,128)S(1)}, s32[8,128]{1,0:T(8,128)}, u32[]{:S(2)}) %copy-start.1) | copy-done | bytes 4120
  10.0 0.0 copy-start
  10.0 5.0 %dft.1 = (bf16[28,24,128]{2,1,0:T(8,128)(2,1)S(1)}, bf16[28,24,128]{2,1,0:T(8,128)(2,1)S(1)}, bf16[28,24,128]{2,1,0:T(8,128)(2,1)S(1)}, bf16[28,24,128]{2,1,0:T(8,128)(2,1)S(1)}) custom-call(s32[8,128]{1,0:T(8,128)S(1)} %copy-done.1, bf16[2,1440,96]{2,1,0:T(8,128)(2,1)S(1)} %dynamic-slice_bitcast_fusion.table_ref, f32[28,64,1440]{2,1,0:T(8,128)} %field_ref.1), custom_call_target="tpu_custom_call" | custom-call | flops 1321205760 | bytes 10321920 | tf_op jit(solution)/shard_map/dft/pallas_call | solution.py:90
  15.0 1.6 %collective-permute-start = (bf16[56,24,128]{2,1,0:T(8,128)(2,1)S(1)}, bf16[56,24,128]{2,1,0:T(8,128)(2,1)S(1)}, u32[]{:S(2)}, u32[]{:S(2)}) collective-permute-start(bf16[56,24,128]{2,1,0:T(8,128)(2,1)S(1)} %pack.3.near_ref), channel_id=1, source_target_pairs={{0,2},{2,0},{1,3},{3,1},{4,6},{6,4},{5,7},{7,5},{8,10},{10,8},{9,1... | collective-permute-start | bytes 1032200 | tf_op jit(solution)/shard_map/ppermute | solution.py:377
  16.6 0.0 collective-permute-done.1.refs_0_
  16.6 0.0 collective-permute-done.2.refs_1_
  16.6 0.0 collective-permute-done.3.refs_2_
  16.6 0.0 copy-start.3
  16.6 0.0 copy-start.4
  16.6 1.6 %collective-permute-start.8 = (bf16[21,24,384]{2,1,0:T(8,128)(2,1)S(1)}, bf16[21,24,384]{2,1,0:T(8,128)(2,1)S(1)}, u32[]{:S(2)}, u32[]{:S(2)}) collective-permute-start(bf16[21,24,384]{2,1,0:T(8,128)(2,1)S(1)} %pack.4.rows_ref), channel_id=1, source_target_pairs={{0,2},{2,0},{1,3},{3,1},{4,6},{6,4},{5,7},{7,5},{8,10},{10,8},{9,1... | collective-permute-start | bytes 1161224 | tf_op jit(solution)/shard_map/ppermute | solution.py:377
  18.2 0.0 copy-done
  18.2 0.6 %own_table.1.refs_3_ = bf16[24,32,384]{2,1,0:T(8,128)(2,1)S(1)} custom-call(s32[8,128]{1,0:T(8,128)S(1)} %copy-done.1, bf16[28,96,384]{2,1,0:T(8,128)(2,1)S(1)} %bitcast.4), custom_call_target="tpu_custom_call" | custom-call | flops 3000000000 | bytes 1000 | tf_op jit(solution)/shard_map/own_table/pallas_call | solution.py:205
  18.9 0.0 copy-done.3
  18.9 0.0 copy-done.4
  18.9 0.1 constant_dynamic-slice_fusion.1
  19.0 3.3 %collective-permute-start.5 = (bf16[28,24,128]{2,1,0:T(8,128)(2,1)S(1)}, bf16[28,24,128]{2,1,0:T(8,128)(2,1)S(1)}, u32[]{:S(2)}, u32[]{:S(2)}) collective-permute-start(bf16[28,24,128]{2,1,0:T(8,128)(2,1)S(1)} %get-tuple-element.28), channel_id=1, source_target_pairs={{0,4},{4,8},{8,12},{12,0},{1,5},{5,9},{9,13},{13,1},{2,6},{6,10},{... | collective-permute-start | bytes 516104 | tf_op jit(solution)/shard_map/ppermute | solution.py:376
  22.3 1.1 %collective-permute-start.4 = (bf16[28,24,128]{2,1,0:T(8,128)(2,1)S(1)}, bf16[28,24,128]{2,1,0:T(8,128)(2,1)S(1)}, u32[]{:S(2)}, u32[]{:S(2)}) collective-permute-start(bf16[28,24,128]{2,1,0:T(8,128)(2,1)S(1)} %get-tuple-element.26), channel_id=1, source_target_pairs={{0,12},{4,0},{8,4},{12,8},{1,13},{5,1},{9,5},{13,9},{2,14},{6,2},{... | collective-permute-start | bytes 516104 | tf_op jit(solution)/shard_map/ppermute | solution.py:376
  23.4 0.1 maximum_maximum_fusion.1.w_far
  23.5 1.6 %collective-permute-start.9 = (bf16[21,24,384]{2,1,0:T(8,128)(2,1)S(1)}, bf16[21,24,384]{2,1,0:T(8,128)(2,1)S(1)}, u32[]{:S(2)}, u32[]{:S(2)}) collective-permute-start(bf16[21,24,384]{2,1,0:T(8,128)(2,1)S(1)} %pack.4.rows_ref), channel_id=1, source_target_pairs={{0,16},{16,0},{1,17},{17,1},{2,18},{18,2},{3,19},{19,3},{4,20},{20... | collective-permute-start | bytes 1161224 | tf_op jit(solution)/shard_map/ppermute | solution.py:378
  25.1 0.1 maximum_maximum_fusion.w_near
  25.2 0.2 turn.4.refs_4_
  25.4 3.2 %collective-permute-done.5.refs_1_ = bf16[28,24,128]{2,1,0:T(8,128)(2,1)S(1)} collective-permute-done((bf16[28,24,128]{2,1,0:T(8,128)(2,1)S(1)}, bf16[28,24,128]{2,1,0:T(8,128)(2,1)S(1)}, u32[]{:S(2)}, u32[]{:S(2)}) %collective-permute-start.5) | collective-permute-done | bytes 172064 | tf_op jit(solution)/shard_map/ppermute | solution.py:376
  28.6 1.9 %collective-permute-done.4.refs_0_ = bf16[28,24,128]{2,1,0:T(8,128)(2,1)S(1)} collective-permute-done((bf16[28,24,128]{2,1,0:T(8,128)(2,1)S(1)}, bf16[28,24,128]{2,1,0:T(8,128)(2,1)S(1)}, u32[]{:S(2)}, u32[]{:S(2)}) %collective-permute-start.4) | collective-permute-done | bytes 172064 | tf_op jit(solution)/shard_map/ppermute | solution.py:376
  30.5 0.6 %collective-permute-start.6 = (bf16[56,24,128]{2,1,0:T(8,128)(2,1)S(1)}, bf16[56,24,128]{2,1,0:T(8,128)(2,1)S(1)}, u32[]{:S(2)}, u32[]{:S(2)}) collective-permute-start(bf16[56,24,128]{2,1,0:T(8,128)(2,1)S(1)} %pack.5.near_ref), channel_id=1, source_target_pairs={{0,2},{2,0},{1,3},{3,1},{4,6},{6,4},{5,7},{7,5},{8,10},{10,8},{9,1... | collective-permute-start | bytes 1032200 | tf_op jit(solution)/shard_map/ppermute | solution.py:377
  31.1 0.0 collective-permute-done.far_ref
  31.1 0.3 cross.1
  31.4 0.6 %collective-permute-start.7 = (bf16[28,24,128]{2,1,0:T(8,128)(2,1)S(1)}, bf16[28,24,128]{2,1,0:T(8,128)(2,1)S(1)}, u32[]{:S(2)}, u32[]{:S(2)}) collective-permute-start(bf16[28,24,128]{2,1,0:T(8,128)(2,1)S(1)} %get-tuple-element.29), channel_id=1, source_target_pairs={{0,8},{4,12},{8,0},{12,4},{1,9},{5,13},{9,1},{13,5},{2,10},{6,14},... | collective-permute-start | bytes 516104 | tf_op jit(solution)/shard_map/ppermute | solution.py:376
  32.0 0.3 collective-permute-done.8.rows_ref
  32.3 1.5 %collective-permute-start.10 = (bf16[21,24,384]{2,1,0:T(8,128)(2,1)S(1)}, bf16[21,24,384]{2,1,0:T(8,128)(2,1)S(1)}, u32[]{:S(2)}, u32[]{:S(2)}) collective-permute-start(bf16[21,24,384]{2,1,0:T(8,128)(2,1)S(1)} %collective-permute-done.8.rows_ref), channel_id=1, source_target_pairs={{0,16},{16,0},{1,17},{17,1},{2,18},{18,2},{3,19},{19,3},{4,20},{20... | collective-permute-start | bytes 1161224 | tf_op jit(solution)/shard_map/ppermute | solution.py:378
  33.8 0.1 arrange.2.refs_0_
  33.9 0.2 turn.5.refs_5_
  34.2 0.0 collective-permute-done.9.rows_ref
  34.2 0.2 turn.6.refs_6_
  34.4 7.3 %collective-permute-done.7.rows_ref = bf16[28,24,128]{2,1,0:T(8,128)(2,1)S(1)} collective-permute-done((bf16[28,24,128]{2,1,0:T(8,128)(2,1)S(1)}, bf16[28,24,128]{2,1,0:T(8,128)(2,1)S(1)}, u32[]{:S(2)}, u32[]{:S(2)}) %collective-permute-start.7) | collective-permute-done | bytes 172064 | tf_op jit(solution)/shard_map/ppermute | solution.py:376
  41.7 0.1 arrange.3.refs_2_
  41.8 0.0 collective-permute-done.6.far_ref
  41.8 0.6 %mix.1.refs_1_ = bf16[24,64,128]{2,1,0:T(8,128)(2,1)S(1)} custom-call(bf16[56,24,128]{2,1,0:T(8,128)(2,1)S(1)} %pack.5.near_ref, bf16[56,24,128]{2,1,0:T(8,128)(2,1)S(1)} %collective-permute-done.6.far_ref, bf16[128,128]{1,0:T(8,128)(2,1)S(1)} %maximum_maximum_fusion.w_near, bf16[128,128]{1,0:T(8,128)(2,1)S(1)} %maximum_maximum_fusion.1.w_far), custom_call_target="tpu_custom_call" | custom-call | flops 88080384 | bytes 688128 | tf_op jit(solution)/shard_map/mix/pallas_call | solution.py:262
  42.4 0.0 collective-permute-done.10.rows_ref
  42.4 0.2 turn.7.refs_7_
  42.6 2.1 %contract.1 = bf16[2,24,64,384]{3,2,1,0:T(8,128)(2,1)} custom-call(bf16[24,32,128]{2,1,0:T(8,128)(2,1)S(1)} %arrange.2.refs_0_, bf16[24,64,128]{2,1,0:T(8,128)(2,1)S(1)} %mix.1.refs_1_, bf16[24,32,128]{2,1,0:T(8,128)(2,1)S(1)} %arrange.3.refs_2_, bf16[24,32,384]{2,1,0:T(8,128)(2,1)S(1)} %own_table.1.refs_3_, bf16[24,24,384]{2,1,0:T(8,128)(2,1)S(1)} %turn.4.refs_4_, ...), custom_call_target="tpu_custom_call" | custom-call | tf_op jit(solution)/shard_map/contract/pallas_call | solution.py:345
  (4 shorter events, 0.1 us)
Async XLA Ops:
  0.0 9.2 %copy-start.2 = (bf16[2,2,1440,96]{3,2,1,0:T(8,128)(2,1)S(1)}, bf16[2,2,1440,96]{3,2,1,0:T(8,128)(2,1)}, u32[]{:S(2)}) copy-start(bf16[2,2,1440,96]{3,2,1,0:T(8,128)(2,1)} %constant.21.clone) | copy-start | bytes 3317764
  2.2 14.4 %collective-permute-start.1 = (bf16[7,24,384]{2,1,0:T(8,128)(2,1)}, bf16[7,24,384]{2,1,0:T(8,128)(2,1)S(1)}, u32[]{:S(2)}, u32[]{:S(2)}) collective-permute-start(bf16[7,24,384]{2,1,0:T(8,128)(2,1)} %get-tuple-element.23), channel_id=1, source_target_pairs={{0,4},{4,8},{8,12},{12,0},{1,5},{5,9},{9,13},{13,1},{2,6},{6,10},{... | collective-permute-start | bytes 387080 | tf_op jit(solution)/shard_map/ppermute | solution.py:376
  5.3 11.3 %collective-permute-start.2 = (bf16[7,24,384]{2,1,0:T(8,128)(2,1)}, bf16[7,24,384]{2,1,0:T(8,128)(2,1)S(1)}, u32[]{:S(2)}, u32[]{:S(2)}) collective-permute-start(bf16[7,24,384]{2,1,0:T(8,128)(2,1)} %get-tuple-element.24), channel_id=1, source_target_pairs={{0,8},{4,12},{8,0},{12,4},{1,9},{5,13},{9,1},{13,5},{2,10},{6,14},... | collective-permute-start | bytes 387080 | tf_op jit(solution)/shard_map/ppermute | solution.py:376
  7.9 8.7 %collective-permute-start.3 = (bf16[7,24,384]{2,1,0:T(8,128)(2,1)}, bf16[7,24,384]{2,1,0:T(8,128)(2,1)S(1)}, u32[]{:S(2)}, u32[]{:S(2)}) collective-permute-start(bf16[7,24,384]{2,1,0:T(8,128)(2,1)} %get-tuple-element.25), channel_id=1, source_target_pairs={{0,12},{4,0},{8,4},{12,8},{1,13},{5,1},{9,5},{13,9},{2,14},{6,2},{... | collective-permute-start | bytes 387080 | tf_op jit(solution)/shard_map/ppermute | solution.py:376
  9.3 0.7 %copy-start.1 = (s32[8,128]{1,0:T(8,128)S(1)}, s32[8,128]{1,0:T(8,128)}, u32[]{:S(2)}) copy-start(s32[8,128]{1,0:T(8,128)} %get-tuple-element.18.modes_ref) | copy-start | bytes 12292
  10.0 8.3 %copy-start = (bf16[96,28,384]{2,0,1:T(8,128)(2,1)S(1)}, bf16[96,28,384]{2,0,1:T(8,128)(2,1)}, u32[]{:S(2)}) copy-start(bf16[96,28,384]{2,0,1:T(8,128)(2,1)} %param.7) | copy-start | bytes 6193156
  15.0 16.1 %collective-permute-start = (bf16[56,24,128]{2,1,0:T(8,128)(2,1)S(1)}, bf16[56,24,128]{2,1,0:T(8,128)(2,1)S(1)}, u32[]{:S(2)}, u32[]{:S(2)}) collective-permute-start(bf16[56,24,128]{2,1,0:T(8,128)(2,1)S(1)} %pack.3.near_ref), channel_id=1, source_target_pairs={{0,2},{2,0},{1,3},{3,1},{4,6},{6,4},{5,7},{7,5},{8,10},{10,8},{9,1... | collective-permute-start | bytes 1032200 | tf_op jit(solution)/shard_map/ppermute | solution.py:377
  16.6 2.2 %copy-start.3 = (bf16[64,128]{1,0:T(8,128)(2,1)S(1)}, bf16[64,128]{1,0:T(8,128)(2,1)}, u32[]{:S(2)}) copy-start(bf16[64,128]{1,0:T(8,128)(2,1)} %param.9) | copy-start | bytes 49156
  16.6 2.2 %copy-start.4 = (bf16[64,128]{1,0:T(8,128)(2,1)S(1)}, bf16[64,128]{1,0:T(8,128)(2,1)}, u32[]{:S(2)}) copy-start(bf16[64,128]{1,0:T(8,128)(2,1)} %param.10) | copy-start | bytes 49156
  16.6 15.7 %collective-permute-start.8 = (bf16[21,24,384]{2,1,0:T(8,128)(2,1)S(1)}, bf16[21,24,384]{2,1,0:T(8,128)(2,1)S(1)}, u32[]{:S(2)}, u32[]{:S(2)}) collective-permute-start(bf16[21,24,384]{2,1,0:T(8,128)(2,1)S(1)} %pack.4.rows_ref), channel_id=1, source_target_pairs={{0,2},{2,0},{1,3},{3,1},{4,6},{6,4},{5,7},{7,5},{8,10},{10,8},{9,1... | collective-permute-start | bytes 1161224 | tf_op jit(solution)/shard_map/ppermute | solution.py:377
  19.0 9.6 %collective-permute-start.5 = (bf16[28,24,128]{2,1,0:T(8,128)(2,1)S(1)}, bf16[28,24,128]{2,1,0:T(8,128)(2,1)S(1)}, u32[]{:S(2)}, u32[]{:S(2)}) collective-permute-start(bf16[28,24,128]{2,1,0:T(8,128)(2,1)S(1)} %get-tuple-element.28), channel_id=1, source_target_pairs={{0,4},{4,8},{8,12},{12,0},{1,5},{5,9},{9,13},{13,1},{2,6},{6,10},{... | collective-permute-start | bytes 516104 | tf_op jit(solution)/shard_map/ppermute | solution.py:376
  22.3 8.2 %collective-permute-start.4 = (bf16[28,24,128]{2,1,0:T(8,128)(2,1)S(1)}, bf16[28,24,128]{2,1,0:T(8,128)(2,1)S(1)}, u32[]{:S(2)}, u32[]{:S(2)}) collective-permute-start(bf16[28,24,128]{2,1,0:T(8,128)(2,1)S(1)} %get-tuple-element.26), channel_id=1, source_target_pairs={{0,12},{4,0},{8,4},{12,8},{1,13},{5,1},{9,5},{13,9},{2,14},{6,2},{... | collective-permute-start | bytes 516104 | tf_op jit(solution)/shard_map/ppermute | solution.py:376
  23.5 10.7 %collective-permute-start.9 = (bf16[21,24,384]{2,1,0:T(8,128)(2,1)S(1)}, bf16[21,24,384]{2,1,0:T(8,128)(2,1)S(1)}, u32[]{:S(2)}, u32[]{:S(2)}) collective-permute-start(bf16[21,24,384]{2,1,0:T(8,128)(2,1)S(1)} %pack.4.rows_ref), channel_id=1, source_target_pairs={{0,16},{16,0},{1,17},{17,1},{2,18},{18,2},{3,19},{19,3},{4,20},{20... | collective-permute-start | bytes 1161224 | tf_op jit(solution)/shard_map/ppermute | solution.py:378
  30.5 11.3 %collective-permute-start.6 = (bf16[56,24,128]{2,1,0:T(8,128)(2,1)S(1)}, bf16[56,24,128]{2,1,0:T(8,128)(2,1)S(1)}, u32[]{:S(2)}, u32[]{:S(2)}) collective-permute-start(bf16[56,24,128]{2,1,0:T(8,128)(2,1)S(1)} %pack.5.near_ref), channel_id=1, source_target_pairs={{0,2},{2,0},{1,3},{3,1},{4,6},{6,4},{5,7},{7,5},{8,10},{10,8},{9,1... | collective-permute-start | bytes 1032200 | tf_op jit(solution)/shard_map/ppermute | solution.py:377
  31.4 10.2 %collective-permute-start.7 = (bf16[28,24,128]{2,1,0:T(8,128)(2,1)S(1)}, bf16[28,24,128]{2,1,0:T(8,128)(2,1)S(1)}, u32[]{:S(2)}, u32[]{:S(2)}) collective-permute-start(bf16[28,24,128]{2,1,0:T(8,128)(2,1)S(1)} %get-tuple-element.29), channel_id=1, source_target_pairs={{0,8},{4,12},{8,0},{12,4},{1,9},{5,13},{9,1},{13,5},{2,10},{6,14},... | collective-permute-start | bytes 516104 | tf_op jit(solution)/shard_map/ppermute | solution.py:376
  32.3 10.0 %collective-permute-start.10 = (bf16[21,24,384]{2,1,0:T(8,128)(2,1)S(1)}, bf16[21,24,384]{2,1,0:T(8,128)(2,1)S(1)}, u32[]{:S(2)}, u32[]{:S(2)}) collective-permute-start(bf16[21,24,384]{2,1,0:T(8,128)(2,1)S(1)} %collective-permute-done.8.rows_ref), channel_id=1, source_target_pairs={{0,16},{16,0},{1,17},{17,1},{2,18},{18,2},{3,19},{19,3},{4,20},{20... | collective-permute-start | bytes 1161224 | tf_op jit(solution)/shard_map/ppermute | solution.py:378

commit v5 on v4

--- a/solution.py
+++ b/solution.py
@@ -131,8 +131,10 @@
     held = pl.BlockSpec(memory_space=pl.ANY)
     return pl.pallas_call(
         functools.partial(pick_kernel, sizes),
+        grid=(1,),
         in_specs=[held, held],
-        out_specs=[pl.BlockSpec(memory_space=pltpu.VMEM)] * (1 + others),
+        out_specs=[pl.BlockSpec((8, 128), lambda i: (0, 0))]
+        + [pl.BlockSpec((rows, per, degrees), lambda i: (0, 0, 0))] * others,
         out_shape=[jax.ShapeDtypeStruct((8, 128), jnp.int32)]
         + [jax.ShapeDtypeStruct((rows, per, degrees), BF16)] * others,
         scratch_shapes=[
@@ -141,7 +143,7 @@
             pltpu.SemaphoreType.DMA,
             pltpu.SemaphoreType.DMA,
         ],
-        compiler_params=pltpu.CompilerParams(vmem_limit_bytes=62 * 1000 * 1000),
+        compiler_params=pltpu.CompilerParams(vmem_limit_bytes=56 * 1000 * 1000),
         cost_estimate=pl.CostEstimate(
             flops=2 * rows * slab * degrees * per * others,
             bytes_accessed=rows * slab * degrees * 2,
@@ -209,7 +211,7 @@
         out_shape=jax.ShapeDtypeStruct((per, depth, degrees), BF16),
         scratch_shapes=[
             pltpu.VMEM((lat_rows * per, degrees), F32),
-            pltpu.VMEM((degrees // 128, depth * per, 128), F32),
+            pltpu.VMEM((degrees // 128, (depth + 1) * per, 128), F32),
         ],
         compiler_params=pltpu.CompilerParams(vmem_limit_bytes=32 << 20),
         cost_estimate=pl.CostEstimate(flops=3_000_000_000, bytes_accessed=1000, transcendentals=0),
@@ -229,7 +231,7 @@
     return pl.pallas_call(
         functools.partial(turn_kernel, share, deep),
         out_shape=jax.ShapeDtypeStruct((per, depth, degrees), BF16),
-        scratch_shapes=[pltpu.VMEM((degrees // 128, depth * per, 128), F32)],
+        scratch_shapes=[pltpu.VMEM((degrees // 128, (depth + 1) * per, 128), F32)],
         compiler_params=pltpu.CompilerParams(vmem_limit_bytes=16 << 20),
         cost_estimate=pl.CostEstimate(flops=1000, bytes_accessed=1000, transcendentals=0),
         name="turn",
@@ -243,6 +245,7 @@
     share = lat_rows // plane
     q = lax.axis_index("rep") * sizes["ch"] + lax.axis_index("ch")
     nt = (((1,), (1,)), ((), ()))
+    w_both = jnp.concatenate([w_near[...], w_far[...]], axis=1)
     parts = []
     for i, shift in enumerate(shifts):
         for d in range(plane):
@@ -250,8 +253,8 @@
             part = pl.ds(i * lat_rows + at * share, share)
             a = near_ref[part].reshape(share * per, width)
             b = far_ref[part].reshape(share * per, width)
-            mixed = lax.dot_general(a, w_near[...], nt, preferred_element_type=F32)
-            mixed += lax.dot_general(b, w_far[...], nt, preferred_element_type=F32)
+            both = jnp.concatenate([a, b], axis=1)
+            mixed = lax.dot_general(both, w_both, nt, preferred_element_type=F32)
             parts.append(widened(mixed, share * per, deep * per))
     by_mode(jnp.concatenate(parts, axis=0), per, out_ref, scratch)
 
@@ -262,7 +265,7 @@
     return pl.pallas_call(
         functools.partial(mix_kernel, sizes, shifts, deep),
         out_shape=jax.ShapeDtypeStruct((per, depth, width), BF16),
-        scratch_shapes=[pltpu.VMEM((1, depth * per, width), F32)],
+        scratch_shapes=[pltpu.VMEM((1, (depth + 1) * per, width), F32)],
         compiler_params=pltpu.CompilerParams(vmem_limit_bytes=16 << 20),
         cost_estimate=pl.CostEstimate(
             flops=2 * 2 * near.size * width, bytes_accessed=near.size * 4, transcendentals=0
@@ -275,12 +278,13 @@
     rows, per, width = near_ref.shape
     lat_rows = rows // len(outs)
     nt = (((1,), (1,)), ((), ()))
+    w_both = jnp.concatenate([w_near[...], w_far[...]], axis=1)
     for i, out_ref in enumerate(outs):
         part = slice(i * lat_rows, (i + 1) * lat_rows)
         a = near_ref[part].reshape(lat_rows * per, width)
         b = far_ref[part].reshape(lat_rows * per, width)
-        mixed = lax.dot_general(a, w_near[...], nt, preferred_element_type=F32)
-        mixed += lax.dot_general(b, w_far[...], nt, preferred_element_type=F32)
+        both = jnp.concatenate([a, b], axis=1)
+        mixed = lax.dot_general(both, w_both, nt, preferred_element_type=F32)
         out_ref[...] = mixed.astype(BF16).reshape(lat_rows, per, width)
 
 
@@ -314,7 +318,7 @@
     return pl.pallas_call(
         functools.partial(arrange_kernel, sizes, shift, deep),
         out_shape=jax.ShapeDtypeStruct((per, depth, width), BF16),
-        scratch_shapes=[pltpu.VMEM((1, depth * per, width), F32)],
+        scratch_shapes=[pltpu.VMEM((1, (depth + 1) * per, width), F32)],
         compiler_params=pltpu.CompilerParams(vmem_limit_bytes=16 << 20),
         cost_estimate=pl.CostEstimate(flops=4_000_000_000, bytes_accessed=1000, transcendentals=0),
         name="arrange",
@@ -322,32 +326,46 @@
 
 
 def contract_kernel(order, plane, group, *refs):
-    *spectra, own = refs[: -plane - 1]
-    *tables, out_ref = refs[-plane - 1 :]
+    *spectra, own = refs[: -plane - 3]
+    *tables, out_ref, mixed, left = refs[-plane - 3 :]
     deep = own.shape[1] // plane
-    half = out_ref.shape[2]
-    for k in range(group):
-        a = jnp.concatenate([part[k] for part in spectra], axis=0)
-        pieces = [own[k]]
-        for s in order:
-            pieces += [table[k, (s - 1) * deep : s * deep] for table in tables]
-        b = jnp.concatenate(pieces, axis=0)
-        c = lax.dot_general(a, b, (((0,), (0,)), ((), ())), preferred_element_type=F32)
-        out_ref[0, k] = c[:half].astype(BF16)
-        out_ref[1, k] = c[half:].astype(BF16)
+    _, per, half, _ = mixed.shape
+
+    def part_copy(i):
+        part = pl.ds(i * group, group)
+        return pltpu.make_async_copy(mixed.at[:, part], out_ref.at[:, part], left.at[i])
+
+    @pl.loop(0, per // group, unroll=True)
+    def _(i):
+        for j in range(group):
+            k = i * group + j
+            a = jnp.concatenate([part[k] for part in spectra], axis=0)
+            pieces = [own[k]]
+            for s in order:
+                pieces += [table[k, (s - 1) * deep : s * deep] for table in tables]
+            b = jnp.concatenate(pieces, axis=0)
+            c = lax.dot_general(a, b, (((0,), (0,)), ((), ())), preferred_element_type=F32)
+            mixed[0, k] = c[:half].astype(BF16)
+            mixed[1, k] = c[half:].astype(BF16)
+        part_copy(i).start()
+
+    @pl.loop(0, per // group)
+    def _(i):
+        part_copy(i).wait()
 
 
 def contract(spectra, own, tables, order):
     per, _, width = spectra[0].shape
     degrees = own.shape[2]
-    group = 12
-    block = lambda x: pl.BlockSpec((group, *x.shape[1:]), lambda i: (i, 0, 0))
+    group = 6
+    vmem = pl.BlockSpec(memory_space=pltpu.VMEM)
+    shape = (2, per, width // 2, degrees)
     return pl.pallas_call(
         functools.partial(contract_kernel, order, len(tables), group),
-        grid=(per // group,),
-        in_specs=[block(x) for x in (*spectra, own, *tables)],
-        out_specs=pl.BlockSpec((2, group, width // 2, degrees), lambda i: (0, i, 0, 0)),
-        out_shape=jax.ShapeDtypeStruct((2, per, width // 2, degrees), BF16),
+        in_specs=[vmem] * (len(spectra) + 1 + len(tables)),
+        out_specs=pl.BlockSpec(memory_space=pl.ANY),
+        out_shape=jax.ShapeDtypeStruct(shape, BF16),
+        scratch_shapes=[pltpu.VMEM(shape, BF16), pltpu.SemaphoreType.DMA((per // group,))],
         compiler_params=pltpu.CompilerParams(vmem_limit_bytes=40 << 20),
         name="contract",
     )(*spectra, own, *tables)
@@ -381,23 +399,26 @@
     landed = [forward(v, s) for s, v in enumerate(sent, 1)]
     spectra = dft(field, modes, sizes)
     w_near, w_far = mixing_weights(w_real, w_imag)
-    own = own_table(by_latitude, modes, deep, sizes)
     mine = pack(landed)
     beside = across(mine)
     beyond_mine = beyond(mine)
     early = pack([spectra[0], spectra[2]])
     far_early = across(early)
+    own = own_table(by_latitude, after(modes, far_early), deep, sizes)
     near3 = forward(after(spectra[3], mine), 3)
     near1 = forward(after(spectra[1], mine), 1)
     zero, *sums = cross_parts(early, far_early, w_near, w_far, 2)
     mixed = [arrange(zero, 0, deep, sizes)]
     sum2 = forward(sums[0], 2)
-    late0 = pack([near3, near1])
+    late0 = near3
+    late1 = near1
     beyond_beside = beyond(beside)
     far_late0 = across(late0)
-    far_late0 = after(far_late0, sum2)
+    far_late1 = across(late1)
+    far_late1 = after(far_late1, sum2)
     tables = [turn(v, share, deep) for v in (mine, beside, beyond_mine, beyond_beside)]
-    mixed.append(mix(late0, far_late0, w_near, w_far, (3, 1), deep, sizes))
+    mixed.append(mix(late0, far_late0, w_near, w_far, (3,), deep, sizes))
+    mixed.append(mix(late1, far_late1, w_near, w_far, (1,), deep, sizes))
     mixed += [arrange(v, s, deep, sizes) for v, s in ((sum2, 2),)]
     return contract(mixed, own, tables, (3, 1, 2))
 

time: 44.9 us -> 43.3 us (0.964)
  waiting for transfers between devices: 12.7 us -> 9.94 us
  starting transfers between devices: 18.8 us -> 21.2 us
  Pallas kernels: 12 us -> 10.8 us
    ppermute x6, waiting for transfers between devices: 12.4 us -> 3.75 us  [fast(): lax.ppermute(v, 'lat', [(i, (i + s) % lats) for i in range(lats)])]
    ppermute x3 -> x4, waiting for transfers between devices: 0.29 us -> 6.05 us  [fast(): across = lambda v: lax.ppermute(v, 'ch', [(0, 1), (1, 0)])]
    ppermute x3 -> x4, starting transfers between devices: 3.71 us -> 6.11 us  [fast(): across = lambda v: lax.ppermute(v, 'ch', [(0, 1), (1, 0)])]
    pallas_call x1, Pallas kernels: 2.19 us -> 1.46 us  [pick_rows(): pl.pallas_call(functools.partial(pick_kernel, sizes), grid=(1,), in_specs...]
  transfers between devices with their start and end apart: 11 -> 12, of which waited for: 4 -> 7; matrix products, arithmetic and copies ran while one was open for 1% -> 1% of each run, Pallas kernels for 17% -> 17%
where the time goes in v5:
time: 43.3 us; the launch traced here: 43.2 us
  starting transfers between devices  21.2 us (49%)
  Pallas kernels  10.8 us (25%)
  waiting for transfers between devices  9.94 us (23%)
  local copies, waits for them, and re-layouts  0.75 us (2%)
    ppermute x6, starting transfers between devices, fast(): lax.ppermute(v, 'lat', [(i, (i + s) % lats) for i in range(lats)])  12 us
    ppermute x4, starting transfers between devices, fast(): across = lambda v: lax.ppermute(v, 'ch', [(0, 1), (1, 0)])  6.11 us
    ppermute x4, waiting for transfers between devices, fast(): across = lambda v: lax.ppermute(v, 'ch', [(0, 1), (1, 0)])  6.05 us
    pallas_call x1, Pallas kernels, dft(): pl.pallas_call(functools.partial(dft_kernel, sizes, step, ahead), in_spec...  4.91 us
    ppermute x6, waiting for transfers between devices, fast(): lax.ppermute(v, 'lat', [(i, (i + s) % lats) for i in range(lats)])  3.75 us
    ppermute x2, starting transfers between devices, fast(): beyond = lambda v: lax.ppermute(v, 'rep', [(0, 1), (1, 0)])  3.11 us
    pallas_call x1, Pallas kernels, contract(): pl.pallas_call(functools.partial(contract_kernel, order, len(tables), gro...  1.79 us
    pallas_call x1, Pallas kernels, pick_rows(): pl.pallas_call(functools.partial(pick_kernel, sizes), grid=(1,), in_specs...  1.46 us
  transfers between devices with their start and end apart: 12, of which 7 were waited for; matrix products, arithmetic and copies ran while one was open for 1% of the time, Pallas kernels for 17%

profile of v5, /device:TPU:0, one launch (start us, length us, event | category | flops | bytes accessed | tf_op | source)
XLA Modules:
  0.0 43.2 jit_solution(17919235426475148054)
XLA Ops:
  0.0 0.0 copy-start.1
  0.0 0.7 %copy-done.1 = s32[192]{0:T(256)S(1)} copy-done((s32[192]{0:T(256)S(1)}, s32[192]{0:T(256)}, u32[]{:S(2)}) %copy-start.1) | copy-done | bytes 792
  0.7 0.0 copy-start.2
  0.7 1.5 %pick_rows.1 = (s32[8,128]{1,0:T(8,128)S(1)}, bf16[7,24,384]{2,1,0:T(8,128)(2,1)S(1)}, bf16[7,24,384]{2,1,0:T(8,128)(2,1)S(1)}, bf16[7,24,384]{2,1,0:T(8,128)(2,1)S(1)}) custom-call(s32[192]{0:T(256)S(1)} %copy-done.1, bf16[28,96,384]{2,1,0:T(8,128)(2,1)} %bitcast.3), custom_call_target="tpu_custom_call" | custom-call | flops 37158912 | bytes 516096 | tf_op jit(solution)/shard_map/pick_rows/pallas_call | solution.py:132
  2.2 3.1 %collective-permute-start.1 = (bf16[7,24,384]{2,1,0:T(8,128)(2,1)S(1)}, bf16[7,24,384]{2,1,0:T(8,128)(2,1)S(1)}, u32[]{:S(2)}, u32[]{:S(2)}) collective-permute-start(bf16[7,24,384]{2,1,0:T(8,128)(2,1)S(1)} %get-tuple-element.24), channel_id=1, source_target_pairs={{0,4},{4,8},{8,12},{12,0},{1,5},{5,9},{9,13},{13,1},{2,6},{6,10},{... | collective-permute-start | bytes 387080 | tf_op jit(solution)/shard_map/ppermute | solution.py:394
  5.2 2.6 %collective-permute-start.2 = (bf16[7,24,384]{2,1,0:T(8,128)(2,1)S(1)}, bf16[7,24,384]{2,1,0:T(8,128)(2,1)S(1)}, u32[]{:S(2)}, u32[]{:S(2)}) collective-permute-start(bf16[7,24,384]{2,1,0:T(8,128)(2,1)S(1)} %get-tuple-element.25), channel_id=1, source_target_pairs={{0,8},{4,12},{8,0},{12,4},{1,9},{5,13},{9,1},{13,5},{2,10},{6,14},... | collective-permute-start | bytes 387080 | tf_op jit(solution)/shard_map/ppermute | solution.py:394
  7.8 1.3 %collective-permute-start.3 = (bf16[7,24,384]{2,1,0:T(8,128)(2,1)S(1)}, bf16[7,24,384]{2,1,0:T(8,128)(2,1)S(1)}, u32[]{:S(2)}, u32[]{:S(2)}) collective-permute-start(bf16[7,24,384]{2,1,0:T(8,128)(2,1)S(1)} %get-tuple-element.26), channel_id=1, source_target_pairs={{0,12},{4,0},{8,4},{12,8},{1,13},{5,1},{9,5},{13,9},{2,14},{6,2},{... | collective-permute-start | bytes 387080 | tf_op jit(solution)/shard_map/ppermute | solution.py:394
  9.2 0.0 copy-done.2
  9.2 0.0 copy-start.3
  9.2 0.0 copy-start.4
  9.2 4.9 %dft.1 = (bf16[28,24,128]{2,1,0:T(8,128)(2,1)S(1)}, bf16[28,24,128]{2,1,0:T(8,128)(2,1)S(1)}, bf16[28,24,128]{2,1,0:T(8,128)(2,1)S(1)}, bf16[28,24,128]{2,1,0:T(8,128)(2,1)S(1)}) custom-call(s32[8,128]{1,0:T(8,128)S(1)} %get-tuple-element.32.modes_ref, bf16[2,1440,96]{2,1,0:T(8,128)(2,1)S(1)} %dynamic-slice_bitcast_fusion.table_ref, f32[28,64,1440]{2,1,0:T(8,128)} %field_ref.1), custom_call_target="tpu_custom_call" | custom-call | flops 1321205760 | bytes 10321920 | tf_op jit(solution)/shard_map/dft/pallas_call | solution.py:90
  14.2 1.6 %collective-permute-start = (bf16[56,24,128]{2,1,0:T(8,128)(2,1)S(1)}, bf16[56,24,128]{2,1,0:T(8,128)(2,1)S(1)}, u32[]{:S(2)}, u32[]{:S(2)}) collective-permute-start(bf16[56,24,128]{2,1,0:T(8,128)(2,1)S(1)} %pack.2.near_ref), channel_id=1, source_target_pairs={{0,2},{2,0},{1,3},{3,1},{4,6},{6,4},{5,7},{7,5},{8,10},{10,8},{9,1... | collective-permute-start | bytes 1032200 | tf_op jit(solution)/shard_map/ppermute | solution.py:395
  15.8 0.0 copy-done.3
  15.8 0.0 copy-done.4
  15.8 0.1 constant_dynamic-slice_fusion.1
  15.9 0.0 collective-permute-done.1.refs_0_
  15.9 0.5 %collective-permute-done.2.refs_1_ = bf16[7,24,384]{2,1,0:T(8,128)(2,1)S(1)} collective-permute-done((bf16[7,24,384]{2,1,0:T(8,128)(2,1)S(1)}, bf16[7,24,384]{2,1,0:T(8,128)(2,1)S(1)}, u32[]{:S(2)}, u32[]{:S(2)}) %collective-permute-start.2) | collective-permute-done | bytes 129056 | tf_op jit(solution)/shard_map/ppermute | solution.py:394
  16.3 0.0 collective-permute-done.3.refs_2_
  16.4 3.3 %collective-permute-start.6 = (bf16[28,24,128]{2,1,0:T(8,128)(2,1)S(1)}, bf16[28,24,128]{2,1,0:T(8,128)(2,1)S(1)}, u32[]{:S(2)}, u32[]{:S(2)}) collective-permute-start(bf16[28,24,128]{2,1,0:T(8,128)(2,1)S(1)} %get-tuple-element.29), channel_id=1, source_target_pairs={{0,4},{4,8},{8,12},{12,0},{1,5},{5,9},{9,13},{13,1},{2,6},{6,10},{... | collective-permute-start | bytes 516104 | tf_op jit(solution)/shard_map/ppermute | solution.py:394
  19.7 1.1 %collective-permute-start.4 = (bf16[28,24,128]{2,1,0:T(8,128)(2,1)S(1)}, bf16[28,24,128]{2,1,0:T(8,128)(2,1)S(1)}, u32[]{:S(2)}, u32[]{:S(2)}) collective-permute-start(bf16[28,24,128]{2,1,0:T(8,128)(2,1)S(1)} %get-tuple-element.27), channel_id=1, source_target_pairs={{0,12},{4,0},{8,4},{12,8},{1,13},{5,1},{9,5},{13,9},{2,14},{6,2},{... | collective-permute-start | bytes 516104 | tf_op jit(solution)/shard_map/ppermute | solution.py:394
  20.8 0.1 maximum_maximum_fusion.1.w_far
  20.9 1.6 %collective-permute-start.9 = (bf16[21,24,384]{2,1,0:T(8,128)(2,1)S(1)}, bf16[21,24,384]{2,1,0:T(8,128)(2,1)S(1)}, u32[]{:S(2)}, u32[]{:S(2)}) collective-permute-start(bf16[21,24,384]{2,1,0:T(8,128)(2,1)S(1)} %pack.3.rows_ref), channel_id=1, source_target_pairs={{0,2},{2,0},{1,3},{3,1},{4,6},{6,4},{5,7},{7,5},{8,10},{10,8},{9,1... | collective-permute-start | bytes 1161224 | tf_op jit(solution)/shard_map/ppermute | solution.py:395
  22.4 0.1 maximum_maximum_fusion.w_near
  22.5 1.6 %collective-permute-start.10 = (bf16[21,24,384]{2,1,0:T(8,128)(2,1)S(1)}, bf16[21,24,384]{2,1,0:T(8,128)(2,1)S(1)}, u32[]{:S(2)}, u32[]{:S(2)}) collective-permute-start(bf16[21,24,384]{2,1,0:T(8,128)(2,1)S(1)} %pack.3.rows_ref), channel_id=1, source_target_pairs={{0,16},{16,0},{1,17},{17,1},{2,18},{18,2},{3,19},{19,3},{4,20},{20... | collective-permute-start | bytes 1161224 | tf_op jit(solution)/shard_map/ppermute | solution.py:396
  24.1 0.2 turn.4.refs_5_
  24.3 1.7 %collective-permute-done.6.near_ref = bf16[28,24,128]{2,1,0:T(8,128)(2,1)S(1)} collective-permute-done((bf16[28,24,128]{2,1,0:T(8,128)(2,1)S(1)}, bf16[28,24,128]{2,1,0:T(8,128)(2,1)S(1)}, u32[]{:S(2)}, u32[]{:S(2)}) %collective-permute-start.6) | collective-permute-done | bytes 172064 | tf_op jit(solution)/shard_map/ppermute | solution.py:394
  26.0 1.5 %collective-permute-start.7 = (bf16[28,24,128]{2,1,0:T(8,128)(2,1)S(1)}, bf16[28,24,128]{2,1,0:T(8,128)(2,1)S(1)}, u32[]{:S(2)}, u32[]{:S(2)}) collective-permute-start(bf16[28,24,128]{2,1,0:T(8,128)(2,1)S(1)} %collective-permute-done.6.near_ref), channel_id=1, source_target_pairs={{0,2},{2,0},{1,3},{3,1},{4,6},{6,4},{5,7},{7,5},{8,10},{10,8},{9,1... | collective-permute-start | bytes 516104 | tf_op jit(solution)/shard_map/ppermute | solution.py:395
  27.5 0.6 %collective-permute-done.4.near_ref = bf16[28,24,128]{2,1,0:T(8,128)(2,1)S(1)} collective-permute-done((bf16[28,24,128]{2,1,0:T(8,128)(2,1)S(1)}, bf16[28,24,128]{2,1,0:T(8,128)(2,1)S(1)}, u32[]{:S(2)}, u32[]{:S(2)}) %collective-permute-start.4) | collective-permute-done | bytes 172064 | tf_op jit(solution)/shard_map/ppermute | solution.py:394
  28.1 1.5 %collective-permute-start.5 = (bf16[28,24,128]{2,1,0:T(8,128)(2,1)S(1)}, bf16[28,24,128]{2,1,0:T(8,128)(2,1)S(1)}, u32[]{:S(2)}, u32[]{:S(2)}) collective-permute-start(bf16[28,24,128]{2,1,0:T(8,128)(2,1)S(1)} %collective-permute-done.4.near_ref), channel_id=1, source_target_pairs={{0,2},{2,0},{1,3},{3,1},{4,6},{6,4},{5,7},{7,5},{8,10},{10,8},{9,1... | collective-permute-start | bytes 516104 | tf_op jit(solution)/shard_map/ppermute | solution.py:395
  29.6 0.0 collective-permute-done.far_ref
  29.6 0.3 cross.1
  30.0 0.0 copy-start
  30.0 0.1 arrange.2.refs_0_
  30.1 0.6 %collective-permute-start.8 = (bf16[28,24,128]{2,1,0:T(8,128)(2,1)S(1)}, bf16[28,24,128]{2,1,0:T(8,128)(2,1)S(1)}, u32[]{:S(2)}, u32[]{:S(2)}) collective-permute-start(bf16[28,24,128]{2,1,0:T(8,128)(2,1)S(1)} %get-tuple-element.30), channel_id=1, source_target_pairs={{0,8},{4,12},{8,0},{12,4},{1,9},{5,13},{9,1},{13,5},{2,10},{6,14},... | collective-permute-start | bytes 516104 | tf_op jit(solution)/shard_map/ppermute | solution.py:394
  30.7 2.2 %collective-permute-done.9.rows_ref = bf16[21,24,384]{2,1,0:T(8,128)(2,1)S(1)} collective-permute-done((bf16[21,24,384]{2,1,0:T(8,128)(2,1)S(1)}, bf16[21,24,384]{2,1,0:T(8,128)(2,1)S(1)}, u32[]{:S(2)}, u32[]{:S(2)}) %collective-permute-start.9) | collective-permute-done | bytes 387104 | tf_op jit(solution)/shard_map/ppermute | solution.py:395
  32.9 1.5 %collective-permute-start.11 = (bf16[21,24,384]{2,1,0:T(8,128)(2,1)S(1)}, bf16[21,24,384]{2,1,0:T(8,128)(2,1)S(1)}, u32[]{:S(2)}, u32[]{:S(2)}) collective-permute-start(bf16[21,24,384]{2,1,0:T(8,128)(2,1)S(1)} %collective-permute-done.9.rows_ref), channel_id=1, source_target_pairs={{0,16},{16,0},{1,17},{17,1},{2,18},{18,2},{3,19},{19,3},{4,20},{20... | collective-permute-start | bytes 1161224 | tf_op jit(solution)/shard_map/ppermute | solution.py:396
  34.4 0.0 copy-done
  34.4 0.6 %own_table.1.refs_4_ = bf16[24,32,384]{2,1,0:T(8,128)(2,1)S(1)} custom-call(s32[8,128]{1,0:T(8,128)S(1)} %get-tuple-element.32.modes_ref, bf16[28,96,384]{2,1,0:T(8,128)(2,1)S(1)} %bitcast.4), custom_call_target="tpu_custom_call" | custom-call | flops 3000000000 | bytes 1000 | tf_op jit(solution)/shard_map/own_table/pallas_call | solution.py:207
  35.0 3.9 %collective-permute-done.5.far_ref = bf16[28,24,128]{2,1,0:T(8,128)(2,1)S(1)} collective-permute-done((bf16[28,24,128]{2,1,0:T(8,128)(2,1)S(1)}, bf16[28,24,128]{2,1,0:T(8,128)(2,1)S(1)}, u32[]{:S(2)}, u32[]{:S(2)}) %collective-permute-start.5) | collective-permute-done | bytes 172064 | tf_op jit(solution)/shard_map/ppermute | solution.py:395
  38.9 0.3 mix.2.refs_1_
  39.2 0.2 turn.5.refs_6_
  39.4 0.0 collective-permute-done.10.rows_ref
  39.4 0.2 turn.6.refs_7_
  39.7 0.0 collective-permute-done.7.far_ref
  39.7 1.0 %collective-permute-done.8.rows_ref = bf16[28,24,128]{2,1,0:T(8,128)(2,1)S(1)} collective-permute-done((bf16[28,24,128]{2,1,0:T(8,128)(2,1)S(1)}, bf16[28,24,128]{2,1,0:T(8,128)(2,1)S(1)}, u32[]{:S(2)}, u32[]{:S(2)}) %collective-permute-start.8) | collective-permute-done | bytes 172064 | tf_op jit(solution)/shard_map/ppermute | solution.py:394
  40.7 0.3 mix.3.refs_2_
  40.9 0.1 arrange.3.refs_3_
  41.0 0.1 collective-permute-done.11.rows_ref
  41.2 0.2 turn.7.refs_8_
  41.4 1.8 %contract.1 = bf16[2,24,64,384]{3,2,1,0:T(8,128)(2,1)} custom-call(bf16[24,32,128]{2,1,0:T(8,128)(2,1)S(1)} %arrange.2.refs_0_, bf16[24,32,128]{2,1,0:T(8,128)(2,1)S(1)} %mix.2.refs_1_, bf16[24,32,128]{2,1,0:T(8,128)(2,1)S(1)} %mix.3.refs_2_, bf16[24,32,128]{2,1,0:T(8,128)(2,1)S(1)} %arrange.3.refs_3_, bf16[24,32,384]{2,1,0:T(8,128)(2,1)S(1)} %own_table.1.refs_4_, ...), custom_call_target="tpu_custom_call" | custom-call | tf_op jit(solution)/shard_map/contract/pallas_call | solution.py:363
  (3 shorter events, 0.1 us)
Async XLA Ops:
  0.0 0.7 %copy-start.1 = (s32[192]{0:T(256)S(1)}, s32[192]{0:T(256)}, u32[]{:S(2)}) copy-start(s32[192]{0:T(256)} %ownership_ref.1) | copy-start | bytes 2308
  0.7 8.5 %copy-start.2 = (bf16[2,2,1440,96]{3,2,1,0:T(8,128)(2,1)S(1)}, bf16[2,2,1440,96]{3,2,1,0:T(8,128)(2,1)}, u32[]{:S(2)}) copy-start(bf16[2,2,1440,96]{3,2,1,0:T(8,128)(2,1)} %constant.21.clone) | copy-start | bytes 3317764
  2.2 13.7 %collective-permute-start.1 = (bf16[7,24,384]{2,1,0:T(8,128)(2,1)S(1)}, bf16[7,24,384]{2,1,0:T(8,128)(2,1)S(1)}, u32[]{:S(2)}, u32[]{:S(2)}) collective-permute-start(bf16[7,24,384]{2,1,0:T(8,128)(2,1)S(1)} %get-tuple-element.24), channel_id=1, source_target_pairs={{0,4},{4,8},{8,12},{12,0},{1,5},{5,9},{9,13},{13,1},{2,6},{6,10},{... | collective-permute-start | bytes 387080 | tf_op jit(solution)/shard_map/ppermute | solution.py:394
  5.2 11.1 %collective-permute-start.2 = (bf16[7,24,384]{2,1,0:T(8,128)(2,1)S(1)}, bf16[7,24,384]{2,1,0:T(8,128)(2,1)S(1)}, u32[]{:S(2)}, u32[]{:S(2)}) collective-permute-start(bf16[7,24,384]{2,1,0:T(8,128)(2,1)S(1)} %get-tuple-element.25), channel_id=1, source_target_pairs={{0,8},{4,12},{8,0},{12,4},{1,9},{5,13},{9,1},{13,5},{2,10},{6,14},... | collective-permute-start | bytes 387080 | tf_op jit(solution)/shard_map/ppermute | solution.py:394
  7.8 8.5 %collective-permute-start.3 = (bf16[7,24,384]{2,1,0:T(8,128)(2,1)S(1)}, bf16[7,24,384]{2,1,0:T(8,128)(2,1)S(1)}, u32[]{:S(2)}, u32[]{:S(2)}) collective-permute-start(bf16[7,24,384]{2,1,0:T(8,128)(2,1)S(1)} %get-tuple-element.26), channel_id=1, source_target_pairs={{0,12},{4,0},{8,4},{12,8},{1,13},{5,1},{9,5},{13,9},{2,14},{6,2},{... | collective-permute-start | bytes 387080 | tf_op jit(solution)/shard_map/ppermute | solution.py:394
  9.2 6.5 %copy-start.3 = (bf16[64,128]{1,0:T(8,128)(2,1)S(1)}, bf16[64,128]{1,0:T(8,128)(2,1)}, u32[]{:S(2)}) copy-start(bf16[64,128]{1,0:T(8,128)(2,1)} %param.9) | copy-start | bytes 49156
  9.2 6.5 %copy-start.4 = (bf16[64,128]{1,0:T(8,128)(2,1)S(1)}, bf16[64,128]{1,0:T(8,128)(2,1)}, u32[]{:S(2)}) copy-start(bf16[64,128]{1,0:T(8,128)(2,1)} %param.10) | copy-start | bytes 49156
  14.2 15.4 %collective-permute-start = (bf16[56,24,128]{2,1,0:T(8,128)(2,1)S(1)}, bf16[56,24,128]{2,1,0:T(8,128)(2,1)S(1)}, u32[]{:S(2)}, u32[]{:S(2)}) collective-permute-start(bf16[56,24,128]{2,1,0:T(8,128)(2,1)S(1)} %pack.2.near_ref), channel_id=1, source_target_pairs={{0,2},{2,0},{1,3},{3,1},{4,6},{6,4},{5,7},{7,5},{8,10},{10,8},{9,1... | collective-permute-start | bytes 1032200 | tf_op jit(solution)/shard_map/ppermute | solution.py:395
  16.4 9.6 %collective-permute-start.6 = (bf16[28,24,128]{2,1,0:T(8,128)(2,1)S(1)}, bf16[28,24,128]{2,1,0:T(8,128)(2,1)S(1)}, u32[]{:S(2)}, u32[]{:S(2)}) collective-permute-start(bf16[28,24,128]{2,1,0:T(8,128)(2,1)S(1)} %get-tuple-element.29), channel_id=1, source_target_pairs={{0,4},{4,8},{8,12},{12,0},{1,5},{5,9},{9,13},{13,1},{2,6},{6,10},{... | collective-permute-start | bytes 516104 | tf_op jit(solution)/shard_map/ppermute | solution.py:394
  19.7 8.5 %collective-permute-start.4 = (bf16[28,24,128]{2,1,0:T(8,128)(2,1)S(1)}, bf16[28,24,128]{2,1,0:T(8,128)(2,1)S(1)}, u32[]{:S(2)}, u32[]{:S(2)}) collective-permute-start(bf16[28,24,128]{2,1,0:T(8,128)(2,1)S(1)} %get-tuple-element.27), channel_id=1, source_target_pairs={{0,12},{4,0},{8,4},{12,8},{1,13},{5,1},{9,5},{13,9},{2,14},{6,2},{... | collective-permute-start | bytes 516104 | tf_op jit(solution)/shard_map/ppermute | solution.py:394
  20.9 12.0 %collective-permute-start.9 = (bf16[21,24,384]{2,1,0:T(8,128)(2,1)S(1)}, bf16[21,24,384]{2,1,0:T(8,128)(2,1)S(1)}, u32[]{:S(2)}, u32[]{:S(2)}) collective-permute-start(bf16[21,24,384]{2,1,0:T(8,128)(2,1)S(1)} %pack.3.rows_ref), channel_id=1, source_target_pairs={{0,2},{2,0},{1,3},{3,1},{4,6},{6,4},{5,7},{7,5},{8,10},{10,8},{9,1... | collective-permute-start | bytes 1161224 | tf_op jit(solution)/shard_map/ppermute | solution.py:395
  22.5 16.9 %collective-permute-start.10 = (bf16[21,24,384]{2,1,0:T(8,128)(2,1)S(1)}, bf16[21,24,384]{2,1,0:T(8,128)(2,1)S(1)}, u32[]{:S(2)}, u32[]{:S(2)}) collective-permute-start(bf16[21,24,384]{2,1,0:T(8,128)(2,1)S(1)} %pack.3.rows_ref), channel_id=1, source_target_pairs={{0,16},{16,0},{1,17},{17,1},{2,18},{18,2},{3,19},{19,3},{4,20},{20... | collective-permute-start | bytes 1161224 | tf_op jit(solution)/shard_map/ppermute | solution.py:396
  26.0 13.6 %collective-permute-start.7 = (bf16[28,24,128]{2,1,0:T(8,128)(2,1)S(1)}, bf16[28,24,128]{2,1,0:T(8,128)(2,1)S(1)}, u32[]{:S(2)}, u32[]{:S(2)}) collective-permute-start(bf16[28,24,128]{2,1,0:T(8,128)(2,1)S(1)} %collective-permute-done.6.near_ref), channel_id=1, source_target_pairs={{0,2},{2,0},{1,3},{3,1},{4,6},{6,4},{5,7},{7,5},{8,10},{10,8},{9,1... | collective-permute-start | bytes 516104 | tf_op jit(solution)/shard_map/ppermute | solution.py:395
  28.1 10.8 %collective-permute-start.5 = (bf16[28,24,128]{2,1,0:T(8,128)(2,1)S(1)}, bf16[28,24,128]{2,1,0:T(8,128)(2,1)S(1)}, u32[]{:S(2)}, u32[]{:S(2)}) collective-permute-start(bf16[28,24,128]{2,1,0:T(8,128)(2,1)S(1)} %collective-permute-done.4.near_ref), channel_id=1, source_target_pairs={{0,2},{2,0},{1,3},{3,1},{4,6},{6,4},{5,7},{7,5},{8,10},{10,8},{9,1... | collective-permute-start | bytes 516104 | tf_op jit(solution)/shard_map/ppermute | solution.py:395
  30.0 4.4 %copy-start = (bf16[96,28,384]{2,0,1:T(8,128)(2,1)S(1)}, bf16[96,28,384]{2,0,1:T(8,128)(2,1)}, u32[]{:S(2)}) copy-start(bf16[96,28,384]{2,0,1:T(8,128)(2,1)} %param.7) | copy-start | bytes 6193156
  30.1 10.6 %collective-permute-start.8 = (bf16[28,24,128]{2,1,0:T(8,128)(2,1)S(1)}, bf16[28,24,128]{2,1,0:T(8,128)(2,1)S(1)}, u32[]{:S(2)}, u32[]{:S(2)}) collective-permute-start(bf16[28,24,128]{2,1,0:T(8,128)(2,1)S(1)} %get-tuple-element.30), channel_id=1, source_target_pairs={{0,8},{4,12},{8,0},{12,4},{1,9},{5,13},{9,1},{13,5},{2,10},{6,14},... | collective-permute-start | bytes 516104 | tf_op jit(solution)/shard_map/ppermute | solution.py:394
  32.9 8.3 %collective-permute-start.11 = (bf16[21,24,384]{2,1,0:T(8,128)(2,1)S(1)}, bf16[21,24,384]{2,1,0:T(8,128)(2,1)S(1)}, u32[]{:S(2)}, u32[]{:S(2)}) collective-permute-start(bf16[21,24,384]{2,1,0:T(8,128)(2,1)S(1)} %collective-permute-done.9.rows_ref), channel_id=1, source_target_pairs={{0,16},{16,0},{1,17},{17,1},{2,18},{18,2},{3,19},{19,3},{4,20},{20... | collective-permute-start | bytes 1161224 | tf_op jit(solution)/shard_map/ppermute | solution.py:396

commit v6 on v5

--- a/solution.py
+++ b/solution.py
@@ -238,14 +238,14 @@
     )(rows)
 
 
-def mix_kernel(sizes, shifts, deep, near_ref, far_ref, w_near, w_far, out_ref, scratch):
+def mix_kernel(sizes, shifts, deep, near_ref, far_ref, weights, out_ref, scratch):
     rows, per, width = near_ref.shape
     plane = sizes["rep"] * sizes["ch"]
     lat_rows = rows // len(shifts)
     share = lat_rows // plane
     q = lax.axis_index("rep") * sizes["ch"] + lax.axis_index("ch")
     nt = (((1,), (1,)), ((), ()))
-    w_both = jnp.concatenate([w_near[...], w_far[...]], axis=1)
+    w_both = weights[...]
     parts = []
     for i, shift in enumerate(shifts):
         for d in range(plane):
@@ -259,7 +259,7 @@
     by_mode(jnp.concatenate(parts, axis=0), per, out_ref, scratch)
 
 
-def mix(near, far, w_near, w_far, shifts, deep, sizes):
+def mix(near, far, weights, shifts, deep, sizes):
     rows, per, width = near.shape
     depth = len(shifts) * sizes["rep"] * sizes["ch"] * deep
     return pl.pallas_call(
@@ -271,14 +271,14 @@
             flops=2 * 2 * near.size * width, bytes_accessed=near.size * 4, transcendentals=0
         ),
         name="mix",
-    )(near, far, w_near, w_far)
-
-
-def cross_kernel(near_ref, far_ref, w_near, w_far, *outs):
+    )(near, far, weights)
+
+
+def cross_kernel(near_ref, far_ref, weights, *outs):
     rows, per, width = near_ref.shape
     lat_rows = rows // len(outs)
     nt = (((1,), (1,)), ((), ()))
-    w_both = jnp.concatenate([w_near[...], w_far[...]], axis=1)
+    w_both = weights[...]
     for i, out_ref in enumerate(outs):
         part = slice(i * lat_rows, (i + 1) * lat_rows)
         a = near_ref[part].reshape(lat_rows * per, width)
@@ -288,7 +288,7 @@
         out_ref[...] = mixed.astype(BF16).reshape(lat_rows, per, width)
 
 
-def cross_parts(near, far, w_near, w_far, parts):
+def cross_parts(near, far, weights, parts):
     rows, per, width = near.shape
     return pl.pallas_call(
         cross_kernel,
@@ -296,7 +296,7 @@
         compiler_params=pltpu.CompilerParams(vmem_limit_bytes=16 << 20),
         cost_estimate=pl.CostEstimate(flops=1000, bytes_accessed=1000, transcendentals=0),
         name="cross",
-    )(near, far, w_near, w_far)
+    )(near, far, weights)
 
 
 def arrange_kernel(sizes, shift, deep, rows_ref, out_ref, scratch):
@@ -373,17 +373,32 @@
 
 def mixing_weights(w_real, w_imag):
     half = w_real.shape[0]
-    x = lax.axis_index("ch")
-    out = []
-    for side in (x, 1 - x):
-        wr = lax.dynamic_slice_in_dim(w_real, side * half, half, 1)
-        wi = lax.dynamic_slice_in_dim(w_imag, side * half, half, 1)
-        out.append(
-            jnp.concatenate(
-                [jnp.concatenate([wr, -wi], axis=1), jnp.concatenate([wi, wr], axis=1)], axis=0
-            )
-        )
-    return out
+    first = lax.axis_index("ch") == 0
+    columns = [[], []]
+    sides = []
+    for w in (w_real.astype(F32), w_imag.astype(F32)):
+        low, high = w[:, :half], w[:, half:]
+        sides.append((jnp.where(first, low, high), jnp.where(first, high, low)))
+    for side in range(2):
+        real, imag = sides[0][side], sides[1][side]
+        columns[0] += [real, -imag]
+        columns[1] += [imag, real]
+    return jnp.concatenate([jnp.concatenate(row, axis=1) for row in columns], axis=0)
+
+
+def weigh_kernel(w_real, w_imag, out_ref):
+    out_ref[...] = mixing_weights(w_real[...], w_imag[...]).astype(BF16)
+
+
+def weigh(w_real, w_imag):
+    half, chans = w_real.shape
+    return pl.pallas_call(
+        weigh_kernel,
+        out_shape=jax.ShapeDtypeStruct((2 * half, 2 * chans), BF16),
+        compiler_params=pltpu.CompilerParams(vmem_limit_bytes=16 << 20),
+        cost_estimate=pl.CostEstimate(flops=3_000_000_000, bytes_accessed=1000, transcendentals=0),
+        name="weigh",
+    )(w_real, w_imag)
 
 
 def fast(field, legendre, ownership, w_real, w_imag, sizes):
@@ -398,7 +413,7 @@
     modes, *sent = pick_rows(by_latitude, ownership, sizes, share)
     landed = [forward(v, s) for s, v in enumerate(sent, 1)]
     spectra = dft(field, modes, sizes)
-    w_near, w_far = mixing_weights(w_real, w_imag)
+    weights = weigh(w_real, w_imag)
     mine = pack(landed)
     beside = across(mine)
     beyond_mine = beyond(mine)
@@ -407,7 +422,7 @@
     own = own_table(by_latitude, after(modes, far_early), deep, sizes)
     near3 = forward(after(spectra[3], mine), 3)
     near1 = forward(after(spectra[1], mine), 1)
-    zero, *sums = cross_parts(early, far_early, w_near, w_far, 2)
+    zero, *sums = cross_parts(early, far_early, weights, 2)
     mixed = [arrange(zero, 0, deep, sizes)]
     sum2 = forward(sums[0], 2)
     late0 = near3
@@ -417,8 +432,8 @@
     far_late1 = across(late1)
     far_late1 = after(far_late1, sum2)
     tables = [turn(v, share, deep) for v in (mine, beside, beyond_mine, beyond_beside)]
-    mixed.append(mix(late0, far_late0, w_near, w_far, (3,), deep, sizes))
-    mixed.append(mix(late1, far_late1, w_near, w_far, (1,), deep, sizes))
+    mixed.append(mix(late0, far_late0, weights, (3,), deep, sizes))
+    mixed.append(mix(late1, far_late1, weights, (1,), deep, sizes))
     mixed += [arrange(v, s, deep, sizes) for v, s in ((sum2, 2),)]
     return contract(mixed, own, tables, (3, 1, 2))
 

time: 43.3 us -> 43.4 us (level)
  waiting for transfers between devices: 9.94 us -> 12.2 us
  starting transfers between devices: 21.2 us -> 19.2 us
    ppermute x6, waiting for transfers between devices: 3.75 us -> 6.12 us  [fast(): lax.ppermute(v, 'lat', [(i, (i + s) % lats) for i in range(lats)])]
    ppermute x4, starting transfers between devices: 6.11 us -> 4.19 us  [fast(): across = lambda v: lax.ppermute(v, 'ch', [(0, 1), (1, 0)])]
  transfers between devices with their start and end apart: 12 -> 12, of which waited for: 7 -> 7; matrix products, arithmetic and copies ran while one was open for 1% -> 0% of each run, Pallas kernels for 17% -> 17%
where the time goes in v6:
time: 43.4 us; the launch traced here: 43.3 us
  starting transfers between devices  19.2 us (44%)
  waiting for transfers between devices  12.2 us (28%)
  Pallas kernels  11 us (25%)
  local copies, waits for them, and re-layouts  0.75 us (2%)
    ppermute x6, starting transfers between devices, fast(): lax.ppermute(v, 'lat', [(i, (i + s) % lats) for i in range(lats)])  11.9 us
    ppermute x6, waiting for transfers between devices, fast(): lax.ppermute(v, 'lat', [(i, (i + s) % lats) for i in range(lats)])  6.12 us
    ppermute x4, waiting for transfers between devices, fast(): across = lambda v: lax.ppermute(v, 'ch', [(0, 1), (1, 0)])  5.78 us
    pallas_call x1, Pallas kernels, dft(): pl.pallas_call(functools.partial(dft_kernel, sizes, step, ahead), in_spec...  4.91 us
    ppermute x4, starting transfers between devices, fast(): across = lambda v: lax.ppermute(v, 'ch', [(0, 1), (1, 0)])  4.19 us
    ppermute x2, starting transfers between devices, fast(): beyond = lambda v: lax.ppermute(v, 'rep', [(0, 1), (1, 0)])  3.11 us
    pallas_call x1, Pallas kernels, contract(): pl.pallas_call(functools.partial(contract_kernel, order, len(tables), gro...  1.79 us
    pallas_call x1, Pallas kernels, pick_rows(): pl.pallas_call(functools.partial(pick_kernel, sizes), grid=(1,), in_specs...  1.46 us
  transfers between devices with their start and end apart: 12, of which 7 were waited for; matrix products, arithmetic and copies ran while one was open for 0% of the time, Pallas kernels for 17%

profile of v6, /device:TPU:0, one launch (start us, length us, event | category | flops | bytes accessed | tf_op | source)
XLA Modules:
  0.0 43.3 jit_solution(473971650323691077)
XLA Ops:
  0.0 0.0 copy-start.1
  0.0 0.7 %copy-done.1 = s32[192]{0:T(256)S(1)} copy-done((s32[192]{0:T(256)S(1)}, s32[192]{0:T(256)}, u32[]{:S(2)}) %copy-start.1) | copy-done | bytes 792
  0.7 0.0 copy-start.4
  0.7 1.5 %pick_rows.1 = (s32[8,128]{1,0:T(8,128)S(1)}, bf16[7,24,384]{2,1,0:T(8,128)(2,1)S(1)}, bf16[7,24,384]{2,1,0:T(8,128)(2,1)S(1)}, bf16[7,24,384]{2,1,0:T(8,128)(2,1)S(1)}) custom-call(s32[192]{0:T(256)S(1)} %copy-done.1, bf16[28,96,384]{2,1,0:T(8,128)(2,1)} %bitcast.3), custom_call_target="tpu_custom_call" | custom-call | flops 37158912 | bytes 516096 | tf_op jit(solution)/shard_map/pick_rows/pallas_call | solution.py:132
  2.2 3.1 %collective-permute-start.1 = (bf16[7,24,384]{2,1,0:T(8,128)(2,1)S(1)}, bf16[7,24,384]{2,1,0:T(8,128)(2,1)S(1)}, u32[]{:S(2)}, u32[]{:S(2)}) collective-permute-start(bf16[7,24,384]{2,1,0:T(8,128)(2,1)S(1)} %get-tuple-element.24), channel_id=1, source_target_pairs={{0,4},{4,8},{8,12},{12,0},{1,5},{5,9},{9,13},{13,1},{2,6},{6,10},{... | collective-permute-start | bytes 387080 | tf_op jit(solution)/shard_map/ppermute | solution.py:409
  5.2 2.6 %collective-permute-start.2 = (bf16[7,24,384]{2,1,0:T(8,128)(2,1)S(1)}, bf16[7,24,384]{2,1,0:T(8,128)(2,1)S(1)}, u32[]{:S(2)}, u32[]{:S(2)}) collective-permute-start(bf16[7,24,384]{2,1,0:T(8,128)(2,1)S(1)} %get-tuple-element.25), channel_id=1, source_target_pairs={{0,8},{4,12},{8,0},{12,4},{1,9},{5,13},{9,1},{13,5},{2,10},{6,14},... | collective-permute-start | bytes 387080 | tf_op jit(solution)/shard_map/ppermute | solution.py:409
  7.8 1.3 %collective-permute-start.3 = (bf16[7,24,384]{2,1,0:T(8,128)(2,1)S(1)}, bf16[7,24,384]{2,1,0:T(8,128)(2,1)S(1)}, u32[]{:S(2)}, u32[]{:S(2)}) collective-permute-start(bf16[7,24,384]{2,1,0:T(8,128)(2,1)S(1)} %get-tuple-element.26), channel_id=1, source_target_pairs={{0,12},{4,0},{8,4},{12,8},{1,13},{5,1},{9,5},{13,9},{2,14},{6,2},{... | collective-permute-start | bytes 387080 | tf_op jit(solution)/shard_map/ppermute | solution.py:409
  9.2 0.0 copy-done.4
  9.2 0.0 copy-start.2
  9.2 0.0 copy-start.3
  9.2 4.9 %dft.1 = (bf16[28,24,128]{2,1,0:T(8,128)(2,1)S(1)}, bf16[28,24,128]{2,1,0:T(8,128)(2,1)S(1)}, bf16[28,24,128]{2,1,0:T(8,128)(2,1)S(1)}, bf16[28,24,128]{2,1,0:T(8,128)(2,1)S(1)}) custom-call(s32[8,128]{1,0:T(8,128)S(1)} %get-tuple-element.32.modes_ref, bf16[2,1440,96]{2,1,0:T(8,128)(2,1)S(1)} %dynamic-slice_bitcast_fusion.table_ref, f32[28,64,1440]{2,1,0:T(8,128)} %field_ref.1), custom_call_target="tpu_custom_call" | custom-call | flops 1321205760 | bytes 10321920 | tf_op jit(solution)/shard_map/dft/pallas_call | solution.py:90
  14.2 1.6 %collective-permute-start = (bf16[56,24,128]{2,1,0:T(8,128)(2,1)S(1)}, bf16[56,24,128]{2,1,0:T(8,128)(2,1)S(1)}, u32[]{:S(2)}, u32[]{:S(2)}) collective-permute-start(bf16[56,24,128]{2,1,0:T(8,128)(2,1)S(1)} %pack.2.near_ref), channel_id=1, source_target_pairs={{0,2},{2,0},{1,3},{3,1},{4,6},{6,4},{5,7},{7,5},{8,10},{10,8},{9,1... | collective-permute-start | bytes 1032200 | tf_op jit(solution)/shard_map/ppermute | solution.py:410
  15.8 0.0 collective-permute-done.1.refs_0_
  15.8 0.6 %collective-permute-done.2.refs_1_ = bf16[7,24,384]{2,1,0:T(8,128)(2,1)S(1)} collective-permute-done((bf16[7,24,384]{2,1,0:T(8,128)(2,1)S(1)}, bf16[7,24,384]{2,1,0:T(8,128)(2,1)S(1)}, u32[]{:S(2)}, u32[]{:S(2)}) %collective-permute-start.2) | collective-permute-done | bytes 129056 | tf_op jit(solution)/shard_map/ppermute | solution.py:409
  16.3 0.0 collective-permute-done.3.refs_2_
  16.4 1.6 %collective-permute-start.9 = (bf16[21,24,384]{2,1,0:T(8,128)(2,1)S(1)}, bf16[21,24,384]{2,1,0:T(8,128)(2,1)S(1)}, u32[]{:S(2)}, u32[]{:S(2)}) collective-permute-start(bf16[21,24,384]{2,1,0:T(8,128)(2,1)S(1)} %pack.3.rows_ref), channel_id=1, source_target_pairs={{0,2},{2,0},{1,3},{3,1},{4,6},{6,4},{5,7},{7,5},{8,10},{10,8},{9,1... | collective-permute-start | bytes 1161224 | tf_op jit(solution)/shard_map/ppermute | solution.py:410
  17.9 3.2 %collective-permute-start.6 = (bf16[28,24,128]{2,1,0:T(8,128)(2,1)S(1)}, bf16[28,24,128]{2,1,0:T(8,128)(2,1)S(1)}, u32[]{:S(2)}, u32[]{:S(2)}) collective-permute-start(bf16[28,24,128]{2,1,0:T(8,128)(2,1)S(1)} %get-tuple-element.29), channel_id=1, source_target_pairs={{0,4},{4,8},{8,12},{12,0},{1,5},{5,9},{9,13},{13,1},{2,6},{6,10},{... | collective-permute-start | bytes 516104 | tf_op jit(solution)/shard_map/ppermute | solution.py:409
  21.2 1.1 %collective-permute-start.4 = (bf16[28,24,128]{2,1,0:T(8,128)(2,1)S(1)}, bf16[28,24,128]{2,1,0:T(8,128)(2,1)S(1)}, u32[]{:S(2)}, u32[]{:S(2)}) collective-permute-start(bf16[28,24,128]{2,1,0:T(8,128)(2,1)S(1)} %get-tuple-element.27), channel_id=1, source_target_pairs={{0,12},{4,0},{8,4},{12,8},{1,13},{5,1},{9,5},{13,9},{2,14},{6,2},{... | collective-permute-start | bytes 516104 | tf_op jit(solution)/shard_map/ppermute | solution.py:409
  22.2 0.0 copy-done.2
  22.2 0.0 copy-done.3
  22.2 0.2 weigh.1.weights
  22.4 1.6 %collective-permute-start.10 = (bf16[21,24,384]{2,1,0:T(8,128)(2,1)S(1)}, bf16[21,24,384]{2,1,0:T(8,128)(2,1)S(1)}, u32[]{:S(2)}, u32[]{:S(2)}) collective-permute-start(bf16[21,24,384]{2,1,0:T(8,128)(2,1)S(1)} %pack.3.rows_ref), channel_id=1, source_target_pairs={{0,16},{16,0},{1,17},{17,1},{2,18},{18,2},{3,19},{19,3},{4,20},{20... | collective-permute-start | bytes 1161224 | tf_op jit(solution)/shard_map/ppermute | solution.py:411
  24.0 0.2 turn.4.refs_5_
  24.2 3.3 %collective-permute-done.6.near_ref = bf16[28,24,128]{2,1,0:T(8,128)(2,1)S(1)} collective-permute-done((bf16[28,24,128]{2,1,0:T(8,128)(2,1)S(1)}, bf16[28,24,128]{2,1,0:T(8,128)(2,1)S(1)}, u32[]{:S(2)}, u32[]{:S(2)}) %collective-permute-start.6) | collective-permute-done | bytes 172064 | tf_op jit(solution)/shard_map/ppermute | solution.py:409
  27.5 0.5 %collective-permute-start.7 = (bf16[28,24,128]{2,1,0:T(8,128)(2,1)S(1)}, bf16[28,24,128]{2,1,0:T(8,128)(2,1)S(1)}, u32[]{:S(2)}, u32[]{:S(2)}) collective-permute-start(bf16[28,24,128]{2,1,0:T(8,128)(2,1)S(1)} %collective-permute-done.6.near_ref), channel_id=1, source_target_pairs={{0,2},{2,0},{1,3},{3,1},{4,6},{6,4},{5,7},{7,5},{8,10},{10,8},{9,1... | collective-permute-start | bytes 516104 | tf_op jit(solution)/shard_map/ppermute | solution.py:410
  28.0 1.3 %collective-permute-done.4.near_ref = bf16[28,24,128]{2,1,0:T(8,128)(2,1)S(1)} collective-permute-done((bf16[28,24,128]{2,1,0:T(8,128)(2,1)S(1)}, bf16[28,24,128]{2,1,0:T(8,128)(2,1)S(1)}, u32[]{:S(2)}, u32[]{:S(2)}) %collective-permute-start.4) | collective-permute-done | bytes 172064 | tf_op jit(solution)/shard_map/ppermute | solution.py:409
  29.4 0.5 %collective-permute-start.5 = (bf16[28,24,128]{2,1,0:T(8,128)(2,1)S(1)}, bf16[28,24,128]{2,1,0:T(8,128)(2,1)S(1)}, u32[]{:S(2)}, u32[]{:S(2)}) collective-permute-start(bf16[28,24,128]{2,1,0:T(8,128)(2,1)S(1)} %collective-permute-done.4.near_ref), channel_id=1, source_target_pairs={{0,2},{2,0},{1,3},{3,1},{4,6},{6,4},{5,7},{7,5},{8,10},{10,8},{9,1... | collective-permute-start | bytes 516104 | tf_op jit(solution)/shard_map/ppermute | solution.py:410
  29.9 0.0 collective-permute-done.far_ref
  29.9 0.3 cross.1
  30.2 0.0 copy-start
  30.2 0.1 arrange.2.refs_0_
  30.3 0.6 %collective-permute-start.8 = (bf16[28,24,128]{2,1,0:T(8,128)(2,1)S(1)}, bf16[28,24,128]{2,1,0:T(8,128)(2,1)S(1)}, u32[]{:S(2)}, u32[]{:S(2)}) collective-permute-start(bf16[28,24,128]{2,1,0:T(8,128)(2,1)S(1)} %get-tuple-element.30), channel_id=1, source_target_pairs={{0,8},{4,12},{8,0},{12,4},{1,9},{5,13},{9,1},{13,5},{2,10},{6,14},... | collective-permute-start | bytes 516104 | tf_op jit(solution)/shard_map/ppermute | solution.py:409
  31.0 2.6 %collective-permute-done.9.rows_ref = bf16[21,24,384]{2,1,0:T(8,128)(2,1)S(1)} collective-permute-done((bf16[21,24,384]{2,1,0:T(8,128)(2,1)S(1)}, bf16[21,24,384]{2,1,0:T(8,128)(2,1)S(1)}, u32[]{:S(2)}, u32[]{:S(2)}) %collective-permute-start.9) | collective-permute-done | bytes 387104 | tf_op jit(solution)/shard_map/ppermute | solution.py:410
  33.6 1.5 %collective-permute-start.11 = (bf16[21,24,384]{2,1,0:T(8,128)(2,1)S(1)}, bf16[21,24,384]{2,1,0:T(8,128)(2,1)S(1)}, u32[]{:S(2)}, u32[]{:S(2)}) collective-permute-start(bf16[21,24,384]{2,1,0:T(8,128)(2,1)S(1)} %collective-permute-done.9.rows_ref), channel_id=1, source_target_pairs={{0,16},{16,0},{1,17},{17,1},{2,18},{18,2},{3,19},{19,3},{4,20},{20... | collective-permute-start | bytes 1161224 | tf_op jit(solution)/shard_map/ppermute | solution.py:411
  35.1 0.0 copy-done
  35.1 0.6 %own_table.1.refs_4_ = bf16[24,32,384]{2,1,0:T(8,128)(2,1)S(1)} custom-call(s32[8,128]{1,0:T(8,128)S(1)} %get-tuple-element.32.modes_ref, bf16[28,96,384]{2,1,0:T(8,128)(2,1)S(1)} %bitcast.4), custom_call_target="tpu_custom_call" | custom-call | flops 3000000000 | bytes 1000 | tf_op jit(solution)/shard_map/own_table/pallas_call | solution.py:207
  35.7 3.2 %collective-permute-done.5.far_ref = bf16[28,24,128]{2,1,0:T(8,128)(2,1)S(1)} collective-permute-done((bf16[28,24,128]{2,1,0:T(8,128)(2,1)S(1)}, bf16[28,24,128]{2,1,0:T(8,128)(2,1)S(1)}, u32[]{:S(2)}, u32[]{:S(2)}) %collective-permute-start.5) | collective-permute-done | bytes 172064 | tf_op jit(solution)/shard_map/ppermute | solution.py:410
  38.9 0.3 mix.2.refs_1_
  39.2 0.2 turn.5.refs_6_
  39.4 0.0 collective-permute-done.10.rows_ref
  39.4 0.2 turn.6.refs_7_
  39.7 0.0 collective-permute-done.7.far_ref
  39.7 0.9 %collective-permute-done.8.rows_ref = bf16[28,24,128]{2,1,0:T(8,128)(2,1)S(1)} collective-permute-done((bf16[28,24,128]{2,1,0:T(8,128)(2,1)S(1)}, bf16[28,24,128]{2,1,0:T(8,128)(2,1)S(1)}, u32[]{:S(2)}, u32[]{:S(2)}) %collective-permute-start.8) | collective-permute-done | bytes 172064 | tf_op jit(solution)/shard_map/ppermute | solution.py:409
  40.6 0.3 mix.3.refs_2_
  40.9 0.1 arrange.3.refs_3_
  41.0 0.3 collective-permute-done.11.rows_ref
  41.3 0.2 turn.7.refs_8_
  41.5 1.8 %contract.1 = bf16[2,24,64,384]{3,2,1,0:T(8,128)(2,1)} custom-call(bf16[24,32,128]{2,1,0:T(8,128)(2,1)S(1)} %arrange.2.refs_0_, bf16[24,32,128]{2,1,0:T(8,128)(2,1)S(1)} %mix.2.refs_1_, bf16[24,32,128]{2,1,0:T(8,128)(2,1)S(1)} %mix.3.refs_2_, bf16[24,32,128]{2,1,0:T(8,128)(2,1)S(1)} %arrange.3.refs_3_, bf16[24,32,384]{2,1,0:T(8,128)(2,1)S(1)} %own_table.1.refs_4_, ...), custom_call_target="tpu_custom_call" | custom-call | tf_op jit(solution)/shard_map/contract/pallas_call | solution.py:363
  (3 shorter events, 0.1 us)
Async XLA Ops:
  0.0 0.7 %copy-start.1 = (s32[192]{0:T(256)S(1)}, s32[192]{0:T(256)}, u32[]{:S(2)}) copy-start(s32[192]{0:T(256)} %ownership_ref.1) | copy-start | bytes 2308
  0.7 8.5 %copy-start.4 = (bf16[2,2,1440,96]{3,2,1,0:T(8,128)(2,1)S(1)}, bf16[2,2,1440,96]{3,2,1,0:T(8,128)(2,1)}, u32[]{:S(2)}) copy-start(bf16[2,2,1440,96]{3,2,1,0:T(8,128)(2,1)} %constant.12.clone) | copy-start | bytes 3317764
  2.2 13.6 %collective-permute-start.1 = (bf16[7,24,384]{2,1,0:T(8,128)(2,1)S(1)}, bf16[7,24,384]{2,1,0:T(8,128)(2,1)S(1)}, u32[]{:S(2)}, u32[]{:S(2)}) collective-permute-start(bf16[7,24,384]{2,1,0:T(8,128)(2,1)S(1)} %get-tuple-element.24), channel_id=1, source_target_pairs={{0,4},{4,8},{8,12},{12,0},{1,5},{5,9},{9,13},{13,1},{2,6},{6,10},{... | collective-permute-start | bytes 387080 | tf_op jit(solution)/shard_map/ppermute | solution.py:409
  5.2 11.1 %collective-permute-start.2 = (bf16[7,24,384]{2,1,0:T(8,128)(2,1)S(1)}, bf16[7,24,384]{2,1,0:T(8,128)(2,1)S(1)}, u32[]{:S(2)}, u32[]{:S(2)}) collective-permute-start(bf16[7,24,384]{2,1,0:T(8,128)(2,1)S(1)} %get-tuple-element.25), channel_id=1, source_target_pairs={{0,8},{4,12},{8,0},{12,4},{1,9},{5,13},{9,1},{13,5},{2,10},{6,14},... | collective-permute-start | bytes 387080 | tf_op jit(solution)/shard_map/ppermute | solution.py:409
  7.8 8.5 %collective-permute-start.3 = (bf16[7,24,384]{2,1,0:T(8,128)(2,1)S(1)}, bf16[7,24,384]{2,1,0:T(8,128)(2,1)S(1)}, u32[]{:S(2)}, u32[]{:S(2)}) collective-permute-start(bf16[7,24,384]{2,1,0:T(8,128)(2,1)S(1)} %get-tuple-element.26), channel_id=1, source_target_pairs={{0,12},{4,0},{8,4},{12,8},{1,13},{5,1},{9,5},{13,9},{2,14},{6,2},{... | collective-permute-start | bytes 387080 | tf_op jit(solution)/shard_map/ppermute | solution.py:409
  9.2 13.0 %copy-start.2 = (bf16[64,128]{1,0:T(8,128)(2,1)S(1)}, bf16[64,128]{1,0:T(8,128)(2,1)}, u32[]{:S(2)}) copy-start(bf16[64,128]{1,0:T(8,128)(2,1)} %w_real.1) | copy-start | bytes 49156
  9.2 13.0 %copy-start.3 = (bf16[64,128]{1,0:T(8,128)(2,1)S(1)}, bf16[64,128]{1,0:T(8,128)(2,1)}, u32[]{:S(2)}) copy-start(bf16[64,128]{1,0:T(8,128)(2,1)} %w_imag.1) | copy-start | bytes 49156
  14.2 15.7 %collective-permute-start = (bf16[56,24,128]{2,1,0:T(8,128)(2,1)S(1)}, bf16[56,24,128]{2,1,0:T(8,128)(2,1)S(1)}, u32[]{:S(2)}, u32[]{:S(2)}) collective-permute-start(bf16[56,24,128]{2,1,0:T(8,128)(2,1)S(1)} %pack.2.near_ref), channel_id=1, source_target_pairs={{0,2},{2,0},{1,3},{3,1},{4,6},{6,4},{5,7},{7,5},{8,10},{10,8},{9,1... | collective-permute-start | bytes 1032200 | tf_op jit(solution)/shard_map/ppermute | solution.py:410
  16.4 17.2 %collective-permute-start.9 = (bf16[21,24,384]{2,1,0:T(8,128)(2,1)S(1)}, bf16[21,24,384]{2,1,0:T(8,128)(2,1)S(1)}, u32[]{:S(2)}, u32[]{:S(2)}) collective-permute-start(bf16[21,24,384]{2,1,0:T(8,128)(2,1)S(1)} %pack.3.rows_ref), channel_id=1, source_target_pairs={{0,2},{2,0},{1,3},{3,1},{4,6},{6,4},{5,7},{7,5},{8,10},{10,8},{9,1... | collective-permute-start | bytes 1161224 | tf_op jit(solution)/shard_map/ppermute | solution.py:410
  17.9 9.6 %collective-permute-start.6 = (bf16[28,24,128]{2,1,0:T(8,128)(2,1)S(1)}, bf16[28,24,128]{2,1,0:T(8,128)(2,1)S(1)}, u32[]{:S(2)}, u32[]{:S(2)}) collective-permute-start(bf16[28,24,128]{2,1,0:T(8,128)(2,1)S(1)} %get-tuple-element.29), channel_id=1, source_target_pairs={{0,4},{4,8},{8,12},{12,0},{1,5},{5,9},{9,13},{13,1},{2,6},{6,10},{... | collective-permute-start | bytes 516104 | tf_op jit(solution)/shard_map/ppermute | solution.py:409
  21.2 8.2 %collective-permute-start.4 = (bf16[28,24,128]{2,1,0:T(8,128)(2,1)S(1)}, bf16[28,24,128]{2,1,0:T(8,128)(2,1)S(1)}, u32[]{:S(2)}, u32[]{:S(2)}) collective-permute-start(bf16[28,24,128]{2,1,0:T(8,128)(2,1)S(1)} %get-tuple-element.27), channel_id=1, source_target_pairs={{0,12},{4,0},{8,4},{12,8},{1,13},{5,1},{9,5},{13,9},{2,14},{6,2},{... | collective-permute-start | bytes 516104 | tf_op jit(solution)/shard_map/ppermute | solution.py:409
  22.4 17.0 %collective-permute-start.10 = (bf16[21,24,384]{2,1,0:T(8,128)(2,1)S(1)}, bf16[21,24,384]{2,1,0:T(8,128)(2,1)S(1)}, u32[]{:S(2)}, u32[]{:S(2)}) collective-permute-start(bf16[21,24,384]{2,1,0:T(8,128)(2,1)S(1)} %pack.3.rows_ref), channel_id=1, source_target_pairs={{0,16},{16,0},{1,17},{17,1},{2,18},{18,2},{3,19},{19,3},{4,20},{20... | collective-permute-start | bytes 1161224 | tf_op jit(solution)/shard_map/ppermute | solution.py:411
  27.5 12.2 %collective-permute-start.7 = (bf16[28,24,128]{2,1,0:T(8,128)(2,1)S(1)}, bf16[28,24,128]{2,1,0:T(8,128)(2,1)S(1)}, u32[]{:S(2)}, u32[]{:S(2)}) collective-permute-start(bf16[28,24,128]{2,1,0:T(8,128)(2,1)S(1)} %collective-permute-done.6.near_ref), channel_id=1, source_target_pairs={{0,2},{2,0},{1,3},{3,1},{4,6},{6,4},{5,7},{7,5},{8,10},{10,8},{9,1... | collective-permute-start | bytes 516104 | tf_op jit(solution)/shard_map/ppermute | solution.py:410
  29.4 9.5 %collective-permute-start.5 = (bf16[28,24,128]{2,1,0:T(8,128)(2,1)S(1)}, bf16[28,24,128]{2,1,0:T(8,128)(2,1)S(1)}, u32[]{:S(2)}, u32[]{:S(2)}) collective-permute-start(bf16[28,24,128]{2,1,0:T(8,128)(2,1)S(1)} %collective-permute-done.4.near_ref), channel_id=1, source_target_pairs={{0,2},{2,0},{1,3},{3,1},{4,6},{6,4},{5,7},{7,5},{8,10},{10,8},{9,1... | collective-permute-start | bytes 516104 | tf_op jit(solution)/shard_map/ppermute | solution.py:410
  30.2 4.8 %copy-start = (bf16[96,28,384]{2,0,1:T(8,128)(2,1)S(1)}, bf16[96,28,384]{2,0,1:T(8,128)(2,1)}, u32[]{:S(2)}) copy-start(bf16[96,28,384]{2,0,1:T(8,128)(2,1)} %param.7) | copy-start | bytes 6193156
  30.3 10.3 %collective-permute-start.8 = (bf16[28,24,128]{2,1,0:T(8,128)(2,1)S(1)}, bf16[28,24,128]{2,1,0:T(8,128)(2,1)S(1)}, u32[]{:S(2)}, u32[]{:S(2)}) collective-permute-start(bf16[28,24,128]{2,1,0:T(8,128)(2,1)S(1)} %get-tuple-element.30), channel_id=1, source_target_pairs={{0,8},{4,12},{8,0},{12,4},{1,9},{5,13},{9,1},{13,5},{2,10},{6,14},... | collective-permute-start | bytes 516104 | tf_op jit(solution)/shard_map/ppermute | solution.py:409
  33.6 7.7 %collective-permute-start.11 = (bf16[21,24,384]{2,1,0:T(8,128)(2,1)S(1)}, bf16[21,24,384]{2,1,0:T(8,128)(2,1)S(1)}, u32[]{:S(2)}, u32[]{:S(2)}) collective-permute-start(bf16[21,24,384]{2,1,0:T(8,128)(2,1)S(1)} %collective-permute-done.9.rows_ref), channel_id=1, source_target_pairs={{0,16},{16,0},{1,17},{17,1},{2,18},{18,2},{3,19},{19,3},{4,20},{20... | collective-permute-start | bytes 1161224 | tf_op jit(solution)/shard_map/ppermute | solution.py:411
